TPU v7x, 32 devices: a whole 2x2x4 slice. The times are simulated.
32 devices in a mesh: wide: 8 (over z, y), narrow: 4 (over x, core).
Axes of the slice: x: 2, y: 2, z: 4, core: 2. Of those that a mesh axis runs over, the one named last changes fastest.
Arguments:
- charges: float32 [2, 2097152], P(None, ('wide', 'narrow')), may hold values from -6 to 6
- source_order: int32 [2097152], P(('wide', 'narrow')), may hold values from 0 to 7, as said below
- velocity: bfloat16 [262144], P(('wide', 'narrow')), may hold values from 0.5 to 4
- leaf_weight: bfloat16 [16, 128], replicated, may hold values from -1.5 to 1.5
- mixing: bfloat16 [8, 2, 2, 128, 128], replicated, may hold values from -0.375 to 0.375
- eval_weight: bfloat16 [128, 16], replicated, may hold values from -0.5 to 0.5
- target_order: int32 [2097152], P(('wide', 'narrow')), may hold values from 0 to 7, as said below
Outputs:
- potentials: float32 [2, 2097152], P(None, ('wide', 'narrow'))
Inputs may be any that keep to these rules, and one draw needn't show every extreme that they name: `source_order`: each aligned block of 8 entries is a permutation of 0 .. 7. `target_order`: each aligned block of 8 entries is a permutation of 0 .. 7.
All inputs are finite; a program needn't handle non-finite values.
Results may differ from a plain program's by a relative error of at most 0.02.
Values may be sent and summed in bfloat16 or wider, within the bound.
No kernel may reach another device: no remote copies, remote signals or barrier semaphores. Data moves between devices by JAX's collectives and lax.ppermute only.
A program may use at most 128 MiB of HBM per device.

v0:
```python
import math

import jax
import jax.numpy as jnp
from jax import lax
from jax.sharding import PartitionSpec as P

LOCAL_LEVELS = 3


def from_partner(block, axis, distance):
    count = lax.axis_size(axis)
    route = []
    for low in range(count):
        high = low | 1 << distance
        if high != low and high < count:
            route += [(low, high), (high, low)]
    return lax.ppermute(block, axis, route)


def rotate(pre, speeds, section_no):
    rank = pre.shape[1] // 2
    nodes = jnp.cos(math.pi * (jnp.arange(rank, dtype=jnp.float32) + 0.5) / rank)
    theta = math.pi * (section_no + 1) * speeds.astype(jnp.float32)[:, None] * nodes[None, :]
    cosine = jnp.cos(theta)
    sine = jnp.sin(theta)
    real_part = pre[:, :rank]
    imag_part = pre[:, rank:]
    return jnp.concatenate(
        [real_part * cosine - imag_part * sine, real_part * sine + imag_part * cosine], axis=1
    ).astype(jnp.bfloat16)


def butterfly_section(state, speeds, mixing, section_no, stride):
    total, width = state.shape
    blocks = state.reshape(total // (2 * stride), 2, stride, width)
    first = blocks[:, 0].reshape(-1, width)
    second = blocks[:, 1].reshape(-1, width)
    results = []
    for target in range(2):
        pre = jnp.dot(first, mixing[section_no, target, 0], preferred_element_type=jnp.float32)
        pre = pre + jnp.dot(
            second, mixing[section_no, target, 1], preferred_element_type=jnp.float32
        )
        results.append(pre.reshape(total // (2 * stride), stride, width))
    pre = jnp.stack(results, axis=1).reshape(total, width)
    return rotate(pre, speeds, section_no)


def combine_pair(own_part, far_part, bit_value, speeds, mixing, section_no):
    section_maps = mixing[section_no]
    pre = jnp.dot(own_part, section_maps[bit_value, bit_value], preferred_element_type=jnp.float32)
    pre = pre + jnp.dot(
        far_part, section_maps[bit_value, 1 - bit_value], preferred_element_type=jnp.float32
    )
    return rotate(pre, speeds, section_no)


def pick_within_box(source_rows, order_rows):
    leaf_size = source_rows.shape[-1]
    picked = jnp.zeros(source_rows.shape, jnp.float32)
    for slot_no in range(leaf_size):
        picked = picked + jnp.where(
            order_rows[None] == slot_no, source_rows[..., slot_no : slot_no + 1], 0.0
        )
    return picked


def on_device(charges, source_order, velocity, leaf_weight, mixing, eval_weight, target_order):
    leaf_size = leaf_weight.shape[0] // 2
    box_count = charges.shape[1] // leaf_size
    charge_rows = charges.reshape(2, box_count, leaf_size)
    ordered = pick_within_box(charge_rows, source_order.reshape(box_count, leaf_size))
    leaf_in = ordered.transpose(1, 0, 2).reshape(box_count, 2 * leaf_size).astype(jnp.bfloat16)
    state = jnp.dot(leaf_in, leaf_weight, preferred_element_type=jnp.float32).astype(jnp.bfloat16)
    for section_no in range(LOCAL_LEVELS):
        state = butterfly_section(state, velocity, mixing, section_no, 2**section_no)
    section_base = LOCAL_LEVELS
    narrow_bits = lax.axis_size("narrow").bit_length() - 1
    wide_bits = lax.axis_size("wide").bit_length() - 1
    for bit_no in range(narrow_bits):
        far_part = from_partner(state, "narrow", bit_no)
        bit_value = lax.axis_index("narrow") >> bit_no & 1
        state = combine_pair(state, far_part, bit_value, velocity, mixing, section_base + bit_no)
    section_base = section_base + narrow_bits
    for bit_no in range(wide_bits):
        far_part = from_partner(state, "wide", bit_no)
        bit_value = lax.axis_index("wide") >> bit_no & 1
        state = combine_pair(state, far_part, bit_value, velocity, mixing, section_base + bit_no)
    values = jnp.dot(state, eval_weight, preferred_element_type=jnp.float32)
    field_rows = values.reshape(box_count, 2, leaf_size).transpose(1, 0, 2)
    picked = pick_within_box(field_rows, target_order.reshape(box_count, leaf_size))
    return picked.reshape(2, box_count * leaf_size)


def solution(mesh):
    return jax.shard_map(
        on_device,
        mesh=mesh,
        in_specs=(
            P(None, ("wide", "narrow")),
            P(("wide", "narrow")),
            P(("wide", "narrow")),
            P(),
            P(),
            P(),
            P(("wide", "narrow")),
        ),
        out_specs=P(None, ("wide", "narrow")),
        check_vma=False,
    )
```

profile of v0, /device:TPU:0, one launch (start us, length us, event | category | flops | bytes accessed | tf_op | source)
XLA Modules:
  0.0 617.8 jit_solution(17080955094555246256)
XLA Ops:
  0.0 9.3 %reshape.251 = f32[2,8192,8]{2,1,0:T(8,128)} reshape(f32[2,65536]{1,0:T(2,128)} %param.7) | data formatting | bytes 1048576 | tf_op jit(solution)/shard_map/reshape | solution.py:72
  9.3 45.3 %slice_reduce_fusion.7 = (f32[2,8192]{1,0:T(2,128)S(1)}, f32[2,8192]{1,0:T(2,128)S(1)}, f32[2,8192]{1,0:T(2,128)S(1)}, f32[2,8192]{1,0:T(2,128)S(1)}, f32[2,8192...) fusion(f32[2,8192,8]{2,1,0:T(8,128)} %reshape.251), kind=kLoop, calls=%fused_computation.14 | loop fusion | bytes 1048576 | tf_op jit(solution)/shard_map/slice | solution.py:64
  54.9 2.4 eq.154
  77.4 2.4 eq.166
  85.6 3.0 fusion.160
  93.7 15.6 %copy.28 = f32[4096,2,1,128]{3,1,0,2:T(2,128)S(1)} copy(f32[4096,2,1,128]{3,0,2,1:T(8,128)S(1)} %pad_maximum_fusion) | data formatting | bytes 8388608 | tf_op jit(solution)/shard_map/stack | solution.py:46
  109.3 4.6 fusion.159
  113.9 2.8 copy.53
  116.7 3.8 copy.54
  121.2 10.1 %fusion.65 = (bf16[8192,64]{0,1:T(8,128)(2,1)S(1)}, bf16[8192,64]{0,1:T(8,128)(2,1)}) fusion(f32[8192,64]{0,1:T(8,128)S(1)} %copy.53, f32[8192,64]{0,1:T(8,128)} %copy.54, f32[64]{0:T(128)S(1)} %multiply_cosine_fusion.8, f32[8192]{0:T(1024)S(1)} %get-tuple-element.77), kind=kLoop, calls=%fused_computation.105 | loop fusion | flops 4718592 | bytes 6324480 | tf_op jit(solution)/shard_map/convert.18
  135.5 6.8 %pad_maximum_fusion.9 = (bf16[2048,1,2,128]{3,2,1,0:T(2,128)(2,1)S(1)}, bf16[2048,1,2,128]{3,2,1,0:T(2,128)(2,1)S(1)}) fusion(bf16[2048,2,2,64]{3,2,1,0:T(2,128)(2,1)} %bitcast.161, bf16[2048,2,2,64]{3,2,1,0:T(2,128)(2,1)S(1)} %bitcast.159), kind=kLoop, calls=%fused_computation.121 | loop fusion | flops 4194304 | bytes 4194304 | tf_op jit(solution)/shard_map/concatenate | solution.py:29
  149.0 4.6 fusion.158
  153.6 2.8 copy.55
  156.4 3.8 copy.56
  160.2 10.1 %fusion.61 = (bf16[8192,64]{0,1:T(8,128)(2,1)S(1)}, bf16[8192,64]{0,1:T(8,128)(2,1)}) fusion(f32[8192,64]{0,1:T(8,128)S(1)} %copy.55, f32[8192,64]{0,1:T(8,128)} %copy.56, f32[8192]{0:T(1024)S(1)} %get-tuple-element.71, f32[64]{0:T(128)S(1)} %multiply_cosine_fusion.8), kind=kLoop, calls=%fused_computation.101 | loop fusion | flops 4718592 | bytes 6324480 | tf_op jit(solution)/shard_map/convert.14
  174.2 4.3 pad_maximum_fusion.8
  181.1 4.6 fusion.157
  185.7 3.8 copy.57
  189.5 3.8 copy.58
  193.3 9.5 %fusion.55 = (bf16[8192,64]{0,1:T(8,128)(2,1)S(1)}, bf16[8192,64]{0,1:T(8,128)(2,1)S(1)}) fusion(f32[8192,64]{0,1:T(8,128)} %copy.58, f32[8192,64]{0,1:T(8,128)} %copy.57, f32[8192]{0:T(1024)S(1)} %get-tuple-element.72, f32[64]{0:T(128)S(1)} %multiply_cosine_fusion.8), kind=kLoop, calls=%fused_computation.95 | loop fusion | flops 4718592 | bytes 6324480 | tf_op jit(solution)/shard_map/convert.10
  206.2 2.7 collective-permute-done
  211.3 8.4 %fusion.51 = (bf16[8192,64]{0,1:T(8,128)(2,1)S(1)}, bf16[8192,64]{0,1:T(8,128)(2,1)S(1)}) fusion(f32[8192,128]{0,1:T(8,128)S(1)} %convolution_add_fusion.4, f32[8192]{0:T(1024)S(1)} %copy-done.12, f32[64]{0:T(128)S(1)} %multiply_cosine_fusion.8), kind=kLoop, calls=%fused_computation.91 | loop fusion | flops 4718592 | bytes 6324480 | tf_op jit(solution)/shard_map/convert.8
  221.2 2.8 collective-permute-start.1
  224.8 45.5 %collective-permute-done.1 = bf16[8192,128]{0,1:T(8,128)(2,1)} collective-permute-done((bf16[8192,128]{0,1:T(8,128)(2,1)}, bf16[8192,128]{0,1:T(8,128)(2,1)}, u32[]{:S(2)}, u32[]{:S(2)}) %collective-permute-start.1) | collective-permute-done | bytes 2097184 | tf_op jit(solution)/shard_map/ppermute | solution.py:18
  272.7 8.6 %fusion.47 = (bf16[8192,64]{0,1:T(8,128)(2,1)S(1)}, bf16[8192,64]{0,1:T(8,128)(2,1)S(1)}) fusion(f32[8192,128]{0,1:T(8,128)S(1)} %convolution_add_fusion.3, f32[8192]{0:T(1024)S(1)} %copy-done.11, f32[64]{0:T(128)S(1)} %multiply_cosine_fusion.8), kind=kLoop, calls=%fused_computation.87 | loop fusion | flops 4718592 | bytes 6324480 | tf_op jit(solution)/shard_map/convert.6
  285.4 44.9 %collective-permute-done.2 = bf16[8192,128]{0,1:T(8,128)(2,1)} collective-permute-done((bf16[8192,128]{0,1:T(8,128)(2,1)}, bf16[8192,128]{0,1:T(8,128)(2,1)}, u32[]{:S(2)}, u32[]{:S(2)}) %collective-permute-start.2) | collective-permute-done | bytes 2097184 | tf_op jit(solution)/shard_map/ppermute | solution.py:18
  332.7 8.4 %fusion.43 = (bf16[8192,64]{0,1:T(8,128)(2,1)S(1)}, bf16[8192,64]{0,1:T(8,128)(2,1)S(1)}) fusion(f32[8192,128]{0,1:T(8,128)S(1)} %convolution_add_fusion.2, f32[8192]{0:T(1024)S(1)} %copy-done.10, f32[64]{0:T(128)S(1)} %multiply_cosine_fusion.8), kind=kLoop, calls=%fused_computation.83 | loop fusion | flops 4718592 | bytes 6324480 | tf_op jit(solution)/shard_map/convert.4
  345.0 44.2 %collective-permute-done.3 = bf16[8192,128]{0,1:T(8,128)(2,1)} collective-permute-done((bf16[8192,128]{0,1:T(8,128)(2,1)}, bf16[8192,128]{0,1:T(8,128)(2,1)}, u32[]{:S(2)}, u32[]{:S(2)}) %collective-permute-start.3) | collective-permute-done | bytes 2097184 | tf_op jit(solution)/shard_map/ppermute | solution.py:18
  391.7 8.4 %fusion.39 = (bf16[8192,64]{0,1:T(8,128)(2,1)S(1)}, bf16[8192,64]{0,1:T(8,128)(2,1)S(1)}) fusion(f32[8192,128]{0,1:T(8,128)S(1)} %convolution_add_fusion.1, f32[8192]{0:T(1024)S(1)} %copy-done.9, f32[64]{0:T(128)S(1)} %multiply_cosine_fusion.8), kind=kLoop, calls=%fused_computation.79 | loop fusion | flops 4718592 | bytes 6324480 | tf_op jit(solution)/shard_map/convert.2
  405.5 87.6 %collective-permute-done.4 = bf16[8192,128]{0,1:T(8,128)(2,1)} collective-permute-done((bf16[8192,128]{0,1:T(8,128)(2,1)}, bf16[8192,128]{0,1:T(8,128)(2,1)}, u32[]{:S(2)}, u32[]{:S(2)}) %collective-permute-start.4) | collective-permute-done | bytes 2097184 | tf_op jit(solution)/shard_map/ppermute | solution.py:18
  495.5 8.4 %fusion.35 = (bf16[8192,64]{0,1:T(8,128)(2,1)S(1)}, bf16[8192,64]{0,1:T(8,128)(2,1)S(1)}) fusion(f32[8192,128]{0,1:T(8,128)S(1)} %convolution_add_fusion, f32[8192]{0:T(1024)S(1)} %copy-done.8, f32[64]{0:T(128)S(1)} %multiply_cosine_fusion.8), kind=kLoop, calls=%fused_computation.75 | loop fusion | flops 4718592 | bytes 6324480 | tf_op jit(solution)/shard_map/convert
  505.5 5.6 broadcast_in_dim.302
  511.2 7.7 %broadcast_in_dim.303 = f32[2,65536]{1,0:T(2,128)S(1)} reshape(f32[2,8192,8]{2,1,0:T(8,128)} %broadcast_in_dim.302) | data formatting | bytes 1048576 | tf_op jit(solution)/shard_map/jit(_where)/broadcast_in_dim | solution.py:63
  518.9 5.3 broadcast_in_dim.307
  524.1 7.7 %broadcast_in_dim.308 = f32[2,65536]{1,0:T(2,128)S(1)} reshape(f32[2,8192,8]{2,1,0:T(8,128)} %broadcast_in_dim.307) | data formatting | bytes 1048576 | tf_op jit(solution)/shard_map/jit(_where)/broadcast_in_dim | solution.py:63
  532.0 5.4 broadcast_in_dim.311
  537.4 7.7 %broadcast_in_dim.312 = f32[2,65536]{1,0:T(2,128)S(1)} reshape(f32[2,8192,8]{2,1,0:T(8,128)} %broadcast_in_dim.311) | data formatting | bytes 1048576 | tf_op jit(solution)/shard_map/jit(_where)/broadcast_in_dim | solution.py:63
  545.1 5.3 broadcast_in_dim.315
  550.3 7.7 %broadcast_in_dim.316 = f32[2,65536]{1,0:T(2,128)S(1)} reshape(f32[2,8192,8]{2,1,0:T(8,128)} %broadcast_in_dim.315) | data formatting | bytes 1048576 | tf_op jit(solution)/shard_map/jit(_where)/broadcast_in_dim | solution.py:63
  558.1 5.4 broadcast_in_dim.319
  563.6 7.7 %broadcast_in_dim.320 = f32[2,65536]{1,0:T(2,128)S(1)} reshape(f32[2,8192,8]{2,1,0:T(8,128)} %broadcast_in_dim.319) | data formatting | bytes 1048576 | tf_op jit(solution)/shard_map/jit(_where)/broadcast_in_dim | solution.py:63
  571.3 5.3 broadcast_in_dim.323
  576.5 7.7 %broadcast_in_dim.324 = f32[2,65536]{1,0:T(2,128)S(1)} reshape(f32[2,8192,8]{2,1,0:T(8,128)} %broadcast_in_dim.323) | data formatting | bytes 1048576 | tf_op jit(solution)/shard_map/jit(_where)/broadcast_in_dim | solution.py:63
  585.2 5.5 broadcast_in_dim.327
  590.7 8.6 %broadcast_in_dim.328 = f32[2,65536]{1,0:T(2,128)} reshape(f32[2,8192,8]{2,1,0:T(8,128)} %broadcast_in_dim.327) | data formatting | bytes 1048576 | tf_op jit(solution)/shard_map/jit(_where)/broadcast_in_dim | solution.py:63
  599.3 5.2 broadcast_in_dim.331
  604.5 8.5 %broadcast_in_dim.332 = f32[2,65536]{1,0:T(2,128)} reshape(f32[2,8192,8]{2,1,0:T(8,128)} %broadcast_in_dim.331) | data formatting | bytes 1048576 | tf_op jit(solution)/shard_map/jit(_where)/broadcast_in_dim | solution.py:63
  613.0 4.5 select_add_fusion
  (94 shorter events, 82.7 us)
Async XLA Ops:
  0.0 84.8 %copy-start = (bf16[16,128]{1,0:T(8,128)(2,1)S(1)}, bf16[16,128]{1,0:T(8,128)(2,1)}, u32[]{:S(2)}) copy-start(bf16[16,128]{1,0:T(8,128)(2,1)} %param.10) | copy-start | bytes 12292
  9.3 45.3 %copy-start.6 = (s32[65536]{0:T(1024)S(1)}, s32[65536]{0:T(1024)}, u32[]{:S(2)}) copy-start(s32[65536]{0:T(1024)} %param.8) | copy-start | bytes 786436
  116.7 3.8 copy-start.13
  174.1 4.4 copy-start.2
  204.3 4.5 collective-permute-start
  206.2 5.1 copy-start.12
  219.7 4.3 copy-start.3
  221.2 49.1 %collective-permute-start.1 = (bf16[8192,128]{0,1:T(8,128)(2,1)}, bf16[8192,128]{0,1:T(8,128)(2,1)}, u32[]{:S(2)}, u32[]{:S(2)}) collective-permute-start(bf16[8192,128]{0,1:T(8,128)(2,1)} %pad_maximum_fusion.4), channel_id=1, source_target_pairs={{0,2},{2,0},{1,3},{3,1},{4,6},{6,4},{5,7},{7,5},{8,10},{10,8},{9,1... | collective-permute-start | bytes 6291464 | tf_op jit(solution)/shard_map/ppermute | solution.py:18
  224.8 47.9 %copy-start.11 = (f32[8192]{0:T(1024)S(1)}, f32[8192]{0:T(1024)}, u32[]{:S(2)}) copy-start(f32[8192]{0:T(1024)} %get-tuple-element.74) | copy-start | bytes 98308
  282.8 47.5 %collective-permute-start.2 = (bf16[8192,128]{0,1:T(8,128)(2,1)}, bf16[8192,128]{0,1:T(8,128)(2,1)}, u32[]{:S(2)}, u32[]{:S(2)}) collective-permute-start(bf16[8192,128]{0,1:T(8,128)(2,1)} %pad_maximum_fusion.5), channel_id=1, source_target_pairs={{0,4},{4,0},{8,12},{12,8},{16,20},{20,16},{24,28},{28,24},{1,5},{5... | collective-permute-start | bytes 6291464 | tf_op jit(solution)/shard_map/ppermute | solution.py:18
  285.4 47.3 %copy-start.10 = (f32[8192]{0:T(1024)S(1)}, f32[8192]{0:T(1024)}, u32[]{:S(2)}) copy-start(f32[8192]{0:T(1024)} %get-tuple-element.75) | copy-start | bytes 98308
  342.7 46.6 %collective-permute-start.3 = (bf16[8192,128]{0,1:T(8,128)(2,1)}, bf16[8192,128]{0,1:T(8,128)(2,1)}, u32[]{:S(2)}, u32[]{:S(2)}) collective-permute-start(bf16[8192,128]{0,1:T(8,128)(2,1)} %pad_maximum_fusion.6), channel_id=1, source_target_pairs={{0,8},{8,0},{4,12},{12,4},{16,24},{24,16},{20,28},{28,20},{1,9},{9... | collective-permute-start | bytes 6291464 | tf_op jit(solution)/shard_map/ppermute | solution.py:18
  345.0 46.7 %copy-start.9 = (f32[8192]{0:T(1024)S(1)}, f32[8192]{0:T(1024)}, u32[]{:S(2)}) copy-start(f32[8192]{0:T(1024)} %get-tuple-element.76) | copy-start | bytes 98308
  400.1 3.7 copy-start.7
  401.6 91.5 %collective-permute-start.4 = (bf16[8192,128]{0,1:T(8,128)(2,1)}, bf16[8192,128]{0,1:T(8,128)(2,1)}, u32[]{:S(2)}, u32[]{:S(2)}) collective-permute-start(bf16[8192,128]{0,1:T(8,128)(2,1)} %pad_maximum_fusion.7), channel_id=1, source_target_pairs={{0,16},{16,0},{4,20},{20,4},{8,24},{24,8},{12,28},{28,12},{1,17},{... | collective-permute-start | bytes 6291464 | tf_op jit(solution)/shard_map/ppermute | solution.py:18
  405.5 90.0 %copy-start.8 = (f32[8192]{0:T(1024)S(1)}, f32[8192]{0:T(1024)}, u32[]{:S(2)}) copy-start(f32[8192]{0:T(1024)} %get-tuple-element.70) | copy-start | bytes 98308
  495.5 8.4 %copy-start.14 = (bf16[128,16]{0,1:T(8,128)(2,1)S(1)}, bf16[128,16]{0,1:T(8,128)(2,1)}, u32[]{:S(2)}) copy-start(bf16[128,16]{0,1:T(8,128)(2,1)} %param.12) | copy-start | bytes 12292
  604.5 8.5 %copy-start.4 = (pred[65536]{0:T(1024)(128)(4,1)S(1)}, pred[65536]{0:T(1024)(128)(4,1)}, u32[]{:S(2)}) copy-start(pred[65536]{0:T(1024)(128)(4,1)} %get-tuple-element.58) | copy-start | bytes 196612
  604.5 8.5 %copy-start.5 = (pred[65536]{0:T(1024)(128)(4,1)S(1)}, pred[65536]{0:T(1024)(128)(4,1)}, u32[]{:S(2)}) copy-start(pred[65536]{0:T(1024)(128)(4,1)} %get-tuple-element.59) | copy-start | bytes 196612
  613.0 4.5 copy-start.1
where the time goes:
time: 623 us; the launch traced here: 618 us
  local copies, waits for them, and re-layouts  255 us (41%)
  waiting for transfers between devices  225 us (36%)
  other arithmetic  100 us (16%)
  matrix products  28.1 us (5%)
  starting transfers between devices  8.84 us (1%)
    ppermute x5, waiting for transfers between devices, from_partner(): return lax.ppermute(block, axis, route)  225 us
    broadcast_in_dim x16, local copies, waits for them, and re-layouts, pick_within_box(): jnp.where(order_rows[None] == slot_no, source_rows[..., slot_no:slot_no +...  106 us
    another operation x8, other arithmetic  72.1 us
    slice x2, local copies, waits for them, and re-layouts, pick_within_box(): source_rows[..., slot_no:slot_no + 1]  46.4 us
    eq x16, local copies, waits for them, and re-layouts, pick_within_box(): order_rows[None] == slot_no  29.8 us
    unnamed x40, local copies, waits for them, and re-layouts  22.3 us
    concatenate x7, other arithmetic, rotate(): jnp.concatenate([real_part * cosine - imag_part * sine, real_part * sine...  18.6 us
    another operation x1, local copies, waits for them, and re-layouts, butterfly_section(): pre = jnp.stack(results, axis=1).reshape(total, width)  15.6 us
  transfers between devices with their start and end apart: 5, of which 5 were waited for; matrix products, arithmetic and copies ran while one was open for 1% of the time, Pallas kernels for 0%

commit v1 on v0

v1 whole, which is shorter than its diff:
```python
import functools
import math

import jax
import jax.numpy as jnp
import numpy as np
from jax import lax
from jax.experimental import pallas as pl
from jax.experimental.pallas import tpu as pltpu
from jax.sharding import PartitionSpec as P

LANES = 128
AXES = ("wide", "narrow")


def lane_index(shape):
    return lax.broadcasted_iota(jnp.int32, shape, len(shape) - 1)


def row_index(shape):
    return lax.broadcasted_iota(jnp.int32, shape, len(shape) - 2)


def pick(rows, order, leaf):
    lanes = lane_index(order.shape)
    return jnp.take_along_axis(rows, order + lanes // leaf * leaf, axis=1)


def pack_kernel(leaf, charges_ref, order_ref, velocity_ref, out_ref):
    rows = order_ref.shape[0]
    step = min(rows, 64)

    @pl.loop(0, rows // step)
    def _(block):
        here = pl.ds(pl.multiple_of(block * step, step), step)
        order = order_ref[here, :]
        for part in range(2):
            values = charges_ref[pl.ds(block * (2 * step) + part, step, stride=2), :]
            out_ref[here, part * LANES : (part + 1) * LANES] = pick(values, order, leaf).astype(
                jnp.bfloat16
            )
        speeds = velocity_ref[pl.ds(block * (step // leaf), step // leaf), :]
        speeds = jnp.broadcast_to(speeds[:, None, :], (step // leaf, leaf, LANES))
        speeds = speeds.reshape(step, LANES)
        shape = (step, LANES)
        own = lane_index(shape) // (LANES // leaf) == row_index(shape) % leaf
        out_ref[here, 2 * LANES :] = jnp.where(own, speeds, 0.0).astype(jnp.bfloat16)


def unpack_kernel(leaf, values_ref, order_ref, out_ref):
    rows = order_ref.shape[0]
    step = min(rows, 64)

    @pl.loop(0, rows // step)
    def _(block):
        here = pl.ds(pl.multiple_of(block * step, step), step)
        order = order_ref[here, :]
        for part in range(2):
            values = values_ref[here, part * LANES : (part + 1) * LANES].astype(jnp.float32)
            out_ref[pl.ds(block * (2 * step) + part, step, stride=2), :] = pick(
                values, order, leaf
            )


def sine_cosine(turns):
    u = turns - jnp.round(turns)
    w = u * u
    sin_terms = [(-1) ** i * math.pi ** (2 * i + 1) / math.factorial(2 * i + 1) for i in range(8)]
    cos_terms = [(-1) ** i * math.pi ** (2 * i) / math.factorial(2 * i) for i in range(8)]
    half_sin = jnp.full_like(w, sin_terms[-1])
    for term in sin_terms[-2::-1]:
        half_sin = half_sin * w + term
    half_sin = half_sin * u
    half_cos = jnp.full_like(w, cos_terms[-1])
    for term in cos_terms[-2::-1]:
        half_cos = half_cos * w + term
    twice = half_sin + half_sin
    return twice * half_cos, 1.0 - twice * half_sin


def butterfly_kernel(
    levels, local_levels, rows_per, leaf,
    packed_ref, nodes_ref, leaf_ref, mixing_ref, eval_ref, out_ref,
    state, maps, leaf_maps, eval_maps, node_maps, twice_ref, cos_ref, sin_ref,
):
    rows = packed_ref.shape[0]
    half = LANES // 2
    pairs = state.shape[0]
    group = 2 * pairs
    f32, b16 = jnp.float32, jnp.bfloat16

    def swapped(x):
        return pltpu.roll(x, half, 1)

    low64 = lane_index((half, LANES)) < half

    @pl.loop(0, levels)
    def _(level):
        for target in range(2):
            for source in range(2):
                for part in range(2):
                    own = mixing_ref[
                        level, target, source, part * half : (part + 1) * half, :
                    ].astype(f32)
                    far = swapped(own)
                    top, bottom = 2 * part * half, (2 * part + 1) * half
                    place = maps.at[level, target, source]
                    place[top : top + half, :LANES] = jnp.where(low64, own, 0.0).astype(b16)
                    place[top : top + half, LANES:] = jnp.where(low64, far, 0.0).astype(b16)
                    place[bottom : bottom + half, :LANES] = jnp.where(low64, 0.0, far).astype(b16)
                    place[bottom : bottom + half, LANES:] = jnp.where(low64, 0.0, own).astype(b16)

    leaf_rows = leaf_ref[...].astype(f32)
    low = lane_index((LANES, LANES)) < half
    box_of_row = row_index((LANES, LANES)) // leaf
    box_of_lane = lane_index((half, LANES)) // leaf
    slot = lane_index((2 * leaf, 2 * LANES))
    spread = (slot // LANES * leaf + slot % leaf == row_index((2 * leaf, 2 * LANES))).astype(b16)
    eval_rows = jnp.dot(eval_ref[...], spread, preferred_element_type=f32)
    node_box = row_index((LANES, LANES)) % group
    for part in range(2):
        tiled = jnp.broadcast_to(
            leaf_rows[part * leaf : (part + 1) * leaf][None], (group, leaf, LANES)
        ).reshape(LANES, LANES)
        far = swapped(tiled)
        for pair in range(pairs):
            first, second = box_of_row == pair, box_of_row == pair + pairs
            here = slice(part * LANES, (part + 1) * LANES)
            leaf_maps[pair, here, :LANES] = jnp.where(
                low, jnp.where(first, tiled, 0.0), jnp.where(second, far, 0.0)
            ).astype(b16)
            leaf_maps[pair, here, LANES:] = jnp.where(
                low, jnp.where(first, far, 0.0), jnp.where(second, tiled, 0.0)
            ).astype(b16)
    for pair in range(pairs):
        for part in range(2):
            for number in range(2):
                top = (2 * part + number) * half
                for side in range(2):
                    block = eval_rows[
                        part * half : (part + 1) * half, side * LANES : (side + 1) * LANES
                    ]
                    eval_maps[pair, top : top + half, side * LANES : (side + 1) * LANES] = (
                        jnp.where(box_of_lane == pair + number * pairs, block, 0.0).astype(b16)
                    )
        for piece in range(3):
            nodes = nodes_ref[piece : piece + 1, :]
            mine = node_box == jnp.where(low, pair, pair + pairs)
            node_maps[pair, piece * LANES : (piece + 1) * LANES, :] = jnp.where(
                mine, nodes, 0.0
            ).astype(b16)

    step = min(rows, 128)

    @pl.loop(0, pairs * (rows // step))
    def _(item):
        pair, block = item // (rows // step), item % (rows // step)
        here = pl.ds(pl.multiple_of(block * step, step), step)
        charges = packed_ref[here, : 2 * LANES]
        state[pair, here, :] = jnp.dot(
            charges, leaf_maps[pair], preferred_element_type=f32
        ).astype(b16)
        speeds = packed_ref[here, 2 * LANES :]
        turns = jnp.dot(
            jnp.concatenate([speeds] * 3, axis=1), node_maps[pair], preferred_element_type=f32
        )
        sine, cosine = sine_cosine(turns)
        twice_ref[pair, here, :] = cosine + cosine
        cos_ref[0, pair, here, :] = cosine
        sin_ref[0, pair, here, :] = sine
        cos_ref[1, pair, here, :] = jnp.ones_like(cosine)
        sin_ref[1, pair, here, :] = jnp.zeros_like(sine)

    def turn(level, pre, index):
        now, other = level % 2, 1 - level % 2
        cosine, sine = cos_ref[(now, *index)], sin_ref[(now, *index)]
        real, imag = pre[:, :LANES], pre[:, LANES:]
        shape = cosine.shape
        cosine, sine = cosine.reshape(real.shape), sine.reshape(real.shape)
        turned = jnp.concatenate(
            [real * cosine - imag * sine, real * sine + imag * cosine], axis=1
        ).astype(b16)
        if level + 1 < levels:
            twice = twice_ref[index].reshape(real.shape)
            cos_ref[(other, *index)] = (
                twice * cosine - cos_ref[(other, *index)].reshape(real.shape)
            ).reshape(shape)
            sin_ref[(other, *index)] = (
                twice * sine - sin_ref[(other, *index)].reshape(real.shape)
            ).reshape(shape)
        return turned

    def mixed(level, target, first, second):
        return jnp.dot(first, maps[level, target, 0], preferred_element_type=f32) + jnp.dot(
            second, maps[level, target, 1], preferred_element_type=f32
        )

    for level in range(levels):
        if level < local_levels:
            blocks = rows // step
            stride = 1 << level

            @pl.loop(0, pairs // 2 * blocks)
            def _(item):
                which, block = item // blocks, item % blocks
                low_pair = which // stride * (2 * stride) + which % stride
                here = pl.ds(pl.multiple_of(block * step, step), step)
                first = state[low_pair, here, :]
                second = state[low_pair + stride, here, :]
                for target in range(2):
                    pair = low_pair + target * stride
                    pre = mixed(level, target, first, second)
                    state[pair, here, :] = turn(level, pre, (pair, here))

            continue
        stride = rows_per << (level - local_levels)
        if stride % 16 == 0:
            span = max(2 * step, 2 * stride)
            blocks = rows // span
            tops = span // (2 * stride)

            @pl.loop(0, pairs * blocks)
            def _(item):
                pair, block = item // blocks, item % blocks
                for start in range(0, stride, step):
                    count = min(step, stride)
                    for_targets = []
                    for source in range(2):
                        parts = []
                        for top in range(tops):
                            at = block * span + (2 * top + source) * stride + start
                            parts.append(state[pair, pl.ds(pl.multiple_of(at, 16), count), :])
                        for_targets.append(
                            parts[0] if tops == 1 else jnp.concatenate(parts, axis=0)
                        )
                    for target in range(2):
                        pre = mixed(level, target, *for_targets)
                        for top in range(tops):
                            at = block * span + (2 * top + target) * stride + start
                            here = pl.ds(pl.multiple_of(at, 16), count)
                            state[pair, here, :] = turn(
                                level, pre[top * count : (top + 1) * count], (pair, here)
                            )

        else:
            blocks = rows // step

            @pl.loop(0, pairs * blocks)
            def _(item):
                pair, block = item // blocks, item % blocks
                here = pl.ds(pl.multiple_of(block * step, step), step)
                own = state[pair, here, :].astype(f32)
                upper = row_index(own.shape) // stride % 2 == 1
                first = jnp.where(upper, pltpu.roll(own, stride, 0), own).astype(b16)
                second = jnp.where(upper, own, pltpu.roll(own, step - stride, 0)).astype(b16)
                pre = jnp.where(
                    upper, mixed(level, 1, first, second), mixed(level, 0, first, second)
                )
                state[pair, here, :] = turn(level, pre, (pair, here))

    @pl.loop(0, rows // step)
    def _(block):
        here = pl.ds(pl.multiple_of(block * step, step), step)
        total = jnp.dot(state[0, here, :], eval_maps[0], preferred_element_type=f32)
        for pair in range(1, pairs):
            total = total + jnp.dot(
                state[pair, here, :], eval_maps[pair], preferred_element_type=f32
            )
        out_ref[here, :] = total.astype(b16)


def split_nodes(rank):
    nodes = np.cos(np.pi * (np.arange(rank) + 0.5) / rank) / 2
    pieces = []
    rest = np.tile(nodes, LANES // rank)
    for _ in range(3):
        piece = rest.astype(jnp.bfloat16)
        pieces.append(piece.astype(np.float32))
        rest = rest - piece.astype(np.float64)
    return np.stack(pieces)


def on_device(charges, source_order, velocity, leaf_weight, mixing, eval_weight, target_order):
    leaf = leaf_weight.shape[0] // 2
    width = leaf_weight.shape[1]
    boxes = charges.shape[1] // leaf
    group = LANES // leaf
    rows = boxes // group
    devices = lax.axis_size("wide") * lax.axis_size("narrow")
    rows_per = rows // devices
    levels = mixing.shape[0]
    local_levels = levels - (devices.bit_length() - 1)
    pairs = group // 2
    vmem = pltpu.CompilerParams(vmem_limit_bytes=48 * 2**20)

    charge_rows = charges.reshape(2, rows, LANES).transpose(1, 0, 2).reshape(2 * rows, LANES)
    speed_rows = velocity.astype(jnp.float32).reshape(boxes // LANES, LANES)
    packed = pl.pallas_call(
        functools.partial(pack_kernel, leaf),
        out_shape=jax.ShapeDtypeStruct((rows, 3 * LANES), jnp.bfloat16),
        compiler_params=vmem,
        name="pack",
    )(charge_rows, source_order.reshape(rows, LANES), speed_rows)

    packed = lax.all_to_all(
        packed.reshape(devices, rows_per, 3 * LANES), AXES, 0, 0, tiled=True
    ).reshape(rows, 3 * LANES)

    nodes = jnp.asarray(split_nodes(width // 2))
    table = pltpu.VMEM((pairs, rows, LANES), jnp.float32)
    values = pl.pallas_call(
        functools.partial(butterfly_kernel, levels, local_levels, rows_per, leaf),
        out_shape=jax.ShapeDtypeStruct((rows, 2 * LANES), jnp.bfloat16),
        scratch_shapes=[
            pltpu.VMEM((pairs, rows, 2 * LANES), jnp.bfloat16),
            pltpu.VMEM((levels, 2, 2, 2 * LANES, 2 * LANES), jnp.bfloat16),
            pltpu.VMEM((pairs, 2 * LANES, 2 * LANES), jnp.bfloat16),
            pltpu.VMEM((pairs, 2 * LANES, 2 * LANES), jnp.bfloat16),
            pltpu.VMEM((pairs, 3 * LANES, LANES), jnp.bfloat16),
            table,
            pltpu.VMEM((2, pairs, rows, LANES), jnp.float32),
            pltpu.VMEM((2, pairs, rows, LANES), jnp.float32),
        ],
        compiler_params=vmem,
        name="butterfly",
    )(packed, nodes, leaf_weight, mixing, eval_weight)

    values = lax.all_to_all(
        values.reshape(devices, rows_per, 2 * LANES), AXES, 0, 0, tiled=True
    ).reshape(rows, 2 * LANES)

    out = pl.pallas_call(
        functools.partial(unpack_kernel, leaf),
        out_shape=jax.ShapeDtypeStruct((2 * rows, LANES), jnp.float32),
        compiler_params=vmem,
        name="unpack",
    )(values, target_order.reshape(rows, LANES))
    return out.reshape(rows, 2, LANES).transpose(1, 0, 2).reshape(2, rows * LANES)


def solution(mesh):
    return jax.shard_map(
        on_device,
        mesh=mesh,
        in_specs=(
            P(None, AXES),
            P(AXES),
            P(AXES),
            P(),
            P(),
            P(),
            P(AXES),
        ),
        out_specs=P(None, AXES),
        check_vma=False,
    )
```

time: 623 us -> 80.6 us (0.13)
  local copies, waits for them, and re-layouts: 255 us -> 2.14 us
  waiting for transfers between devices: 225 us -> 13 us
  other arithmetic: 100 us -> 0.81 us
  Pallas kernels: 0 us -> 43.9 us
  matrix products: 28.1 us -> 0 us
  blocking collectives: 0 us -> 13 us
    ppermute x5 -> x0, waiting for transfers between devices: 225 us -> none  [from_partner(): return lax.ppermute(block, axis, route)]
    broadcast_in_dim x16 -> x0, local copies, waits for them, and re-layouts: 106 us -> none  [pick_within_box(): jnp.where(order_rows[None] == slot_no, source_rows[..., slot_no:slot_no +...]
    another operation x11 -> x0, other arithmetic: 75.2 us -> none
    slice x7 -> x0, local copies, waits for them, and re-layouts: 63.7 us -> none  [the longest x2 46.4 us: pick_within_box(): source_rows[..., slot_no:slot_no + 1]]
    pallas_call x0 -> x3, Pallas kernels: none -> 43.9 us  [the longest x1 40.8 us: on_device(): pl.pallas_call(functools.partial(butterfly_kernel, levels, local_levels,...]
    eq x16 -> x0, local copies, waits for them, and re-layouts: 29.8 us -> none  [pick_within_box(): order_rows[None] == slot_no]
    dot_general x24 -> x0, matrix products: 28.1 us -> none  [the longest x5 12 us: combine_pair(): jnp.dot(far_part, section_maps[bit_value, 1 - bit_value], preferred_eleme...]
    another operation x5 -> x0, local copies, waits for them, and re-layouts: 23.6 us -> none  [the longest x1 15.6 us: butterfly_section(): pre = jnp.stack(results, axis=1).reshape(total, width)]
  transfers between devices with their start and end apart: 5 -> 1, of which waited for: 5 -> 1; matrix products, arithmetic and copies ran while one was open for 1% -> 0% of each run, Pallas kernels for 0% -> 0%
where the time goes in v1:
time: 80.6 us; the launch traced here: 80.3 us
  Pallas kernels  43.9 us (54%)
  waiting for transfers between devices  13 us (16%)
  blocking collectives  13 us (16%)
  starting transfers between devices  7.3 us (9%)
  local copies, waits for them, and re-layouts  2.14 us (3%)
  other arithmetic  0.81 us (1%)
    pallas_call x1, Pallas kernels, on_device(): pl.pallas_call(functools.partial(butterfly_kernel, levels, local_levels,...  40.8 us
    all_to_all x1, blocking collectives, on_device(): lax.all_to_all(values.reshape(devices, rows_per, 2 * LANES), AXES, 0, 0,...  13 us
    all_to_all x1, waiting for transfers between devices, on_device(): lax.all_to_all(packed.reshape(devices, rows_per, 3 * LANES), AXES, 0, 0,...  13 us
    all_to_all x1, starting transfers between devices, on_device(): lax.all_to_all(packed.reshape(devices, rows_per, 3 * LANES), AXES, 0, 0,...  7.3 us
    unnamed x15, local copies, waits for them, and re-layouts  2.14 us
  transfers between devices with their start and end apart: 1, of which 1 were waited for; matrix products, arithmetic and copies ran while one was open for 0% of the time, Pallas kernels for 0%

profile of v1, /device:TPU:0, one launch (start us, length us, event | category | flops | bytes accessed | tf_op | source)
XLA Modules:
  0.0 80.3 jit_solution(2426854652787066985)
XLA Ops:
  0.0 0.0 copy-start
  0.0 0.8 %bitcast_convert_fusion.velocity_ref = f32[64,128]{1,0:T(8,128)S(1)} fusion(bf16[8192]{0:T(1024)(128)(2,1)} %param.10), kind=kLoop, calls=%fused_computation | loop fusion | flops 8192 | bytes 49152 | tf_op jit(solution)/shard_map/reshape | solution.py:297
  0.8 0.0 copy-start.1
  0.8 1.0 %copy-done.1 = f32[2,65536]{1,0:T(2,128)S(1)} copy-done((f32[2,65536]{1,0:T(2,128)S(1)}, f32[2,65536]{1,0:T(2,128)}, u32[]{:S(2)}) %copy-start.1) | copy-done | bytes 524312
  1.9 0.0 copy-start.2
  1.9 0.9 %copy-done.2 = s32[65536]{0:T(1024)S(1)} copy-done((s32[65536]{0:T(1024)S(1)}, s32[65536]{0:T(1024)}, u32[]{:S(2)}) %copy-start.2) | copy-done | bytes 262168
  2.8 1.5 %pack.1 = bf16[512,384]{1,0:T(8,128)(2,1)} custom-call(f32[1024,128]{1,0:T(8,128)S(1)} %bitcast.22, s32[512,128]{1,0:T(8,128)S(1)} %bitcast.23, f32[64,128]{1,0:T(8,128)S(1)} %bitcast_convert_fusion.velocity_ref), custom_call_target="tpu_custom_call" | custom-call | tf_op jit(solution)/shard_map/pack/pallas_call | solution.py:298
  4.4 0.0 copy-start.6
  4.4 7.3 %all-to-all-start = ((bf16[32,16,384]{2,1,0:T(8,128)(2,1)}), bf16[32,16,384]{2,1,0:T(8,128)(2,1)S(1)}, u32[]{:S(2)}, u32[]{:S(2)}) async-start(bf16[32,16,384]{2,1,0:T(8,128)(2,1)} %bitcast.5), calls=%async_computation | async-start | bytes 786432 | tf_op jit(solution)/shard_map/all_to_all | solution.py:305
  11.7 0.0 copy-done.6
  11.7 0.0 copy-start.4
  11.7 0.0 copy-start.5
  11.7 0.1 copy.10.eval_ref
  11.8 13.0 %all-to-all-done = bf16[32,16,384]{2,1,0:T(8,128)(2,1)S(1)} async-done(((bf16[32,16,384]{2,1,0:T(8,128)(2,1)}), bf16[32,16,384]{2,1,0:T(8,128)(2,1)S(1)}, u32[]{:S(2)}, u32[]{:S(2)}) %all-to-all-start) | async-done | bytes 393248 | tf_op jit(solution)/shard_map/all_to_all | solution.py:305
  24.8 0.0 copy-done
  24.8 0.0 copy-done.4
  24.8 0.0 copy-done.5
  24.8 40.8 %butterfly.1 = bf16[512,256]{1,0:T(8,128)(2,1)S(1)} custom-call(bf16[512,384]{1,0:T(8,128)(2,1)S(1)} %bitcast.19, f32[3,128]{1,0:T(4,128)S(1)} %copy-done.5, bf16[16,128]{1,0:T(8,128)(2,1)S(1)} %copy-done.4, bf16[8,2,2,128,128]{4,3,2,1,0:T(8,128)(2,1)S(1)} %copy-done, bf16[128,16]{1,0:T(8,128)(2,1)S(1)} %copy.10.eval_ref), custom_call_target="tpu_custom_call" | custom-call | tf_op jit(solution)/shard_map/butterfly/pallas_call | solution.py:311
  65.7 0.0 copy-start.3
  65.7 13.0 %all_to_all.10 = bf16[32,16,256]{2,1,0:T(8,128)(2,1)S(1)} all-to-all(bf16[32,16,256]{2,1,0:T(8,128)(2,1)S(1)} %bitcast.20), channel_id=1, replica_groups=mesh['wide'=8,'narrow'=4] {'wide','narrow'}, dimensions={0} | all-to-all | bytes 524288 | tf_op jit(solution)/shard_map/all_to_all | solution.py:328
  78.7 0.0 copy-done.3
  78.7 1.6 %unpack.1 = f32[1024,128]{1,0:T(8,128)} custom-call(bf16[512,256]{1,0:T(8,128)(2,1)S(1)} %bitcast.21, s32[512,128]{1,0:T(8,128)S(1)} %bitcast.24), custom_call_target="tpu_custom_call" | custom-call | tf_op jit(solution)/shard_map/unpack/pallas_call | solution.py:332
Async XLA Ops:
  0.0 24.8 %copy-start = (bf16[8,2,2,128,128]{4,3,2,1,0:T(8,128)(2,1)S(1)}, bf16[8,2,2,128,128]{4,3,2,1,0:T(8,128)(2,1)}, u32[]{:S(2)}) copy-start(bf16[8,2,2,128,128]{4,3,2,1,0:T(8,128)(2,1)} %mixing_ref.1) | copy-start | bytes 3145732
  0.8 1.0 %copy-start.1 = (f32[2,65536]{1,0:T(2,128)S(1)}, f32[2,65536]{1,0:T(2,128)}, u32[]{:S(2)}) copy-start(f32[2,65536]{1,0:T(2,128)} %param.8) | copy-start | bytes 1572868
  1.9 0.9 %copy-start.2 = (s32[65536]{0:T(1024)S(1)}, s32[65536]{0:T(1024)}, u32[]{:S(2)}) copy-start(s32[65536]{0:T(1024)} %param.9) | copy-start | bytes 786436
  4.4 7.3 %copy-start.6 = (bf16[128,16]{0,1:T(8,128)(2,1)S(1)}, bf16[128,16]{0,1:T(8,128)(2,1)}, u32[]{:S(2)}) copy-start(bf16[128,16]{0,1:T(8,128)(2,1)} %param.13) | copy-start | bytes 12292
  4.4 20.5 %all-to-all-start = ((bf16[32,16,384]{2,1,0:T(8,128)(2,1)}), bf16[32,16,384]{2,1,0:T(8,128)(2,1)S(1)}, u32[]{:S(2)}, u32[]{:S(2)}) async-start(bf16[32,16,384]{2,1,0:T(8,128)(2,1)} %bitcast.5), calls=%async_computation | async-start | bytes 786432 | tf_op jit(solution)/shard_map/all_to_all | solution.py:305
  11.7 13.2 %copy-start.4 = (bf16[16,128]{1,0:T(8,128)(2,1)S(1)}, bf16[16,128]{1,0:T(8,128)(2,1)}, u32[]{:S(2)}) copy-start(bf16[16,128]{1,0:T(8,128)(2,1)} %leaf_ref.1) | copy-start | bytes 12292
  11.7 13.2 %copy-start.5 = (f32[3,128]{1,0:T(4,128)S(1)}, f32[3,128]{1,0:T(4,128)}, u32[]{:S(2)}) copy-start(f32[3,128]{1,0:T(4,128)} %constant.2.clone.nodes_ref) | copy-start | bytes 4612
  65.7 13.1 %copy-start.3 = (s32[65536]{0:T(1024)S(1)}, s32[65536]{0:T(1024)}, u32[]{:S(2)}) copy-start(s32[65536]{0:T(1024)} %param.14) | copy-start | bytes 786436

commit v2 on v0

v2 whole, which is shorter than its diff:
```python
import functools
import math

import jax
import jax.numpy as jnp
import numpy as np
from jax import lax
from jax.experimental import pallas as pl
from jax.experimental.pallas import tpu as pltpu
from jax.sharding import PartitionSpec as P

LANES = 128
HALF = LANES // 2
TILE = 16
AXES = ("wide", "narrow")
F32, B16 = jnp.float32, jnp.bfloat16
UNITS = 32
VMEM = pltpu.CompilerParams(vmem_limit_bytes=56 * 2**20)


def lane_index(shape):
    return lax.broadcasted_iota(jnp.int32, shape, len(shape) - 1)


def row_index(shape):
    return lax.broadcasted_iota(jnp.int32, shape, len(shape) - 2)


def swapped(x):
    return pltpu.roll(x, HALF, 1)


def odd_bits(number):
    for shift in (16, 8, 4, 2, 1):
        number = number ^ lax.shift_right_logical(number, shift)
    return number & 1


def device_number():
    return lax.axis_index("wide") * lax.axis_size("narrow") + lax.axis_index("narrow")


def pack_kernel(leaf, charges_ref, order_ref, velocity_ref, out_ref):
    rows = order_ref.shape[0]
    odd = odd_bits(device_number()) == 1
    step = min(rows, 64)
    lanes = lane_index((step, LANES))
    group = LANES // leaf

    @pl.loop(0, rows // step)
    def _(block):
        here = pl.ds(pl.multiple_of(block * step, step), step)
        index = order_ref[here, :] + lanes // leaf * leaf
        for part in range(2):
            values = charges_ref[pl.ds(block * (2 * step) + part, step, stride=2), :]
            values = jnp.take_along_axis(values, index, axis=1)
            values = jnp.where(odd, swapped(values), values)
            out_ref[here, part * LANES : (part + 1) * LANES] = values.astype(B16)

    speeds = velocity_ref[...].astype(F32)
    lanes = lane_index(speeds.shape)
    speeds = jnp.take_along_axis(speeds, lanes ^ jnp.where(odd, group // 2, 0), axis=1)
    count = speeds.shape[0]
    speeds = jnp.broadcast_to(speeds[:, None, :], (count, leaf, LANES)).reshape(rows, LANES)
    own = lane_index(speeds.shape) // group == row_index(speeds.shape) % leaf
    speeds = jnp.where(own, speeds, 0.0)
    shift = group
    while shift < LANES:
        speeds = speeds + pltpu.roll(speeds, shift, 1)
        shift *= 2
    out_ref[:, 2 * LANES :] = speeds.astype(B16)


def unpack_kernel(leaf, values_ref, order_ref, out_ref):
    rows = order_ref.shape[0]
    odd = odd_bits(device_number()) == 1
    step = min(rows, 64)
    base = lane_index((step, LANES)) // leaf * leaf ^ jnp.where(odd, HALF, 0)

    @pl.loop(0, rows // step)
    def _(block):
        here = pl.ds(pl.multiple_of(block * step, step), step)
        index = order_ref[here, :] + base
        for part in range(2):
            values = values_ref[here, part * LANES : (part + 1) * LANES].astype(F32)
            out_ref[pl.ds(block * (2 * step) + part, step, stride=2), :] = jnp.take_along_axis(
                values, index, axis=1
            )


def odd_pair(pair):
    return bin(pair).count("1") % 2 == 1


def maps_kernel(leaf, leaf_ref, mixing_ref, eval_ref, nodes_ref, maps, leaf_maps, eval_maps, node_maps):
    levels = mixing_ref.shape[0]
    pairs = leaf_maps.shape[0]
    group = 2 * pairs
    low = lane_index((HALF, LANES)) < HALF

    @pl.loop(0, levels)
    def _(level):
        for source in range(2):
            for part in range(2):
                rows = slice(part * HALF, (part + 1) * HALF)
                to_first = mixing_ref[level, 0, source, rows, :].astype(F32)
                to_second = mixing_ref[level, 1, source, rows, :].astype(F32)
                first_far, second_far = swapped(to_first), swapped(to_second)
                for order in range(2):
                    top = part * LANES + (source ^ order) * HALF
                    place = maps.at[level, order, top : top + HALF]
                    if order == 0:
                        real = jnp.where(low, to_first, second_far)
                        imag = jnp.where(low, first_far, to_second)
                    else:
                        real = jnp.where(low, to_second, first_far)
                        imag = jnp.where(low, second_far, to_first)
                    place[:, :LANES] = real.astype(B16)
                    place[:, LANES:] = imag.astype(B16)

    leaf_rows = leaf_ref[...].astype(F32)
    low = lane_index((LANES, LANES)) < HALF
    box_of_row = row_index((LANES, LANES)) // leaf
    box_of_lane = lane_index((HALF, LANES)) // leaf
    slot = lane_index((2 * leaf, 2 * LANES))
    spread = (slot // LANES * leaf + slot % leaf == row_index((2 * leaf, 2 * LANES))).astype(B16)
    eval_rows = jnp.dot(eval_ref[...], spread, preferred_element_type=F32)
    node_row = row_index((LANES, LANES))
    nodes = jnp.zeros((LANES, LANES), F32)
    for piece in range(3):
        nodes = jnp.where(node_row // group == piece, nodes_ref[piece : piece + 1, :], nodes)
    node_maps[...] = jnp.zeros(node_maps.shape, B16)
    for pair in range(pairs):
        left, right = (pair + pairs, pair) if odd_pair(pair) else (pair, pair + pairs)
        for part in range(2):
            tiled = jnp.broadcast_to(
                leaf_rows[part * leaf : (part + 1) * leaf][None], (group, leaf, LANES)
            ).reshape(LANES, LANES)
            far = swapped(tiled)
            first, second = box_of_row == left, box_of_row == right
            here = slice(part * LANES, (part + 1) * LANES)
            leaf_maps[pair, here, :LANES] = jnp.where(
                low, jnp.where(first, tiled, 0.0), jnp.where(second, far, 0.0)
            ).astype(B16)
            leaf_maps[pair, here, LANES:] = jnp.where(
                low, jnp.where(first, far, 0.0), jnp.where(second, tiled, 0.0)
            ).astype(B16)
            for number, box in enumerate((left, right)):
                top = (2 * part + number) * HALF
                for side in range(2):
                    lanes = slice(side * LANES, (side + 1) * LANES)
                    block = eval_rows[part * HALF : (part + 1) * HALF, lanes]
                    eval_maps[pair, top : top + HALF, lanes] = jnp.where(
                        box_of_lane == box, block, 0.0
                    ).astype(B16)
        lanes = slice(pair % 2 * LANES, (pair % 2 + 1) * LANES)
        mine = node_row % group == jnp.where(low, left, right)
        node_maps[pair // 2, :LANES, lanes] = jnp.where(mine, nodes, 0.0).astype(B16)


def sine_cosine(turns):
    u = turns - jnp.round(turns)
    w = u * u
    sin_terms = [(-1) ** i * math.pi ** (2 * i + 1) / math.factorial(2 * i + 1) for i in range(7)]
    cos_terms = [(-1) ** i * math.pi ** (2 * i) / math.factorial(2 * i) for i in range(7)]
    half_sin = jnp.full_like(w, sin_terms[-1])
    for term in sin_terms[-2::-1]:
        half_sin = half_sin * w + term
    half_sin = half_sin * u
    half_cos = jnp.full_like(w, cos_terms[-1])
    for term in cos_terms[-2::-1]:
        half_cos = half_cos * w + term
    twice = half_sin + half_sin
    return twice * half_cos, 1.0 - twice * half_sin


def butterfly_kernel(
    plan, packed_ref, maps, leaf_maps, eval_maps, node_maps, out_ref,
    state_a, state_b, twice_ref, *tables,
):
    rows = packed_ref.shape[0]
    pairs = leaf_maps.shape[0]
    levels = len(plan)
    states = (state_a, state_b)
    cosines, sines = tables[:3], tables[3:]
    low = lane_index((TILE, LANES)) < HALF
    low16 = lax.broadcasted_iota(jnp.int16, (TILE, LANES), 1) < jnp.int16(HALF)

    def merged(mask, first, second):
        return jnp.concatenate(
            [
                jnp.where(mask, first[:, :LANES], second[:, :LANES]),
                jnp.where(mask, first[:, LANES:], second[:, LANES:]),
            ],
            axis=1,
        )

    def turned(level, tile, real, imag):
        now, last, coming = level % 3, (level - 1) % 3, (level + 1) % 3
        cosine, sine = cosines[now][tile], sines[now][tile]
        target = states[1 - level % 2]
        target[tile, :, :LANES] = (real * cosine - imag * sine).astype(B16)
        target[tile, :, LANES:] = (real * sine + imag * cosine).astype(B16)
        if level + 1 < levels:
            twice = twice_ref[tile]
            last_cosine = cosines[last][tile] if level else 1.0
            cosines[coming][tile] = twice * cosine - last_cosine
            sines[coming][tile] = twice * sine - sines[last][tile] if level else twice * sine

    half_tiles = state_a.shape[0] // 2
    units = min(UNITS, half_tiles)
    blocks = half_tiles // units

    def tiles_of(level, block, unit):
        bit = plan[level][1]
        stride = 1 << bit
        if stride >= units:
            start = block * units
            base = lax.shift_left(lax.shift_right_logical(start, bit), bit + 1) | (
                start & (stride - 1)
            )
            tile = base + unit
        else:
            tile = block * (2 * units) + (unit >> bit << (bit + 1) | unit & (stride - 1))
        return tile, tile + stride

    def run(*accumulators):
        def load_maps(level):
            for order in range(2):
                pltpu.matmul_push_rhs(maps[level, order], 0, order)

        def send(level, block, unit, fresh):
            source = states[level % 2]
            first, second = (source[tile] for tile in tiles_of(level, block, unit))
            for order in range(2):
                pltpu.matmul_acc_lhs(
                    accumulators[2 * unit + order],
                    merged(low16, *((second, first) if order else (first, second))),
                    load_staged_rhs=0 if fresh and unit == 0 else None,
                )

        def finish(level, block, unit):
            one, other = (pltpu.matmul_pop(accumulators[2 * unit + order]) for order in range(2))
            for target, tile in enumerate(tiles_of(level, block, unit)):
                left, right = (other, one) if target else (one, other)
                turned(
                    level, tile,
                    jnp.where(low, left[:, :LANES], right[:, :LANES]),
                    jnp.where(low, left[:, LANES:], right[:, LANES:]),
                )

        def within_tiles(level):
            stride = plan[level][1]
            upper = row_index((TILE, 2 * LANES)) // stride % 2 == 1
            mask = (lane_index((TILE, 2 * LANES)) % LANES < HALF) != upper

            def one_tile(tile, fresh):
                own = states[level % 2][tile].astype(F32)
                far = jnp.where(
                    upper, pltpu.roll(own, stride, 0), pltpu.roll(own, TILE - stride, 0)
                )
                pre = []
                for order in range(2):
                    lhs = jnp.where(mask, far, own) if order else jnp.where(mask, own, far)
                    pltpu.matmul_acc_lhs(
                        accumulators[order], lhs.astype(B16), load_staged_rhs=0 if fresh else None
                    )
                    pre.append(pltpu.matmul_pop(accumulators[order]))
                mixed = jnp.where(mask, *pre)
                turned(level, tile, mixed[:, :LANES], mixed[:, LANES:])

            one_tile(0, True)

            @pl.loop(1, 2 * half_tiles)
            def _(tile):
                one_tile(tile, False)

        row_tiles = rows // TILE
        few = min(TILE, row_tiles)

        @pl.loop(0, pairs // 2 * (row_tiles // few))
        def _(item):
            duo, start = item // (row_tiles // few), item % (row_tiles // few) * few
            for order in range(2):
                pltpu.matmul_push_rhs(node_maps[duo], 0, order)
                pltpu.matmul_push_rhs(leaf_maps[2 * duo + order], 1, order)
            strips = [pl.ds(pl.multiple_of((start + i) * TILE, TILE), TILE) for i in range(few)]
            for i, strip in enumerate(strips):
                speeds = packed_ref[strip, 2 * LANES :]
                pltpu.matmul_acc_lhs(
                    accumulators[2 * few + i],
                    jnp.concatenate([speeds, speeds], axis=1),
                    load_staged_rhs=0 if i < 2 else None,
                )
            for i, strip in enumerate(strips):
                for order in range(2):
                    pltpu.matmul_acc_lhs(
                        accumulators[2 * i + order],
                        packed_ref[strip, : 2 * LANES],
                        load_staged_rhs=1 if i == 0 else None,
                    )
            for i in range(few):
                turns = pltpu.matmul_pop(accumulators[2 * few + i])
                for order in range(2):
                    tile = (start + i) * pairs + 2 * duo + order
                    sine, cosine = sine_cosine(turns[:, order * LANES : (order + 1) * LANES])
                    twice_ref[tile] = cosine + cosine
                    cosines[0][tile] = cosine
                    sines[0][tile] = sine
                    state_a[tile] = pltpu.matmul_pop(accumulators[2 * i + order]).astype(B16)

        flowing = False
        for level in range(levels):
            if not flowing:
                load_maps(level)
            if plan[level][0] == "rows":
                within_tiles(level)
                continue
            if not flowing:
                for unit in range(units):
                    send(level, 0, unit, True)

            @pl.loop(0, blocks - 1)
            def _(block):
                for unit in range(units):
                    finish(level, block, unit)
                    send(level, block + 1, unit, False)

            flowing = blocks > 2 and level + 1 < levels and plan[level + 1][0] == "tiles"
            if flowing:
                load_maps(level + 1)
            for unit in range(units):
                finish(level, blocks - 1, unit)
                if flowing:
                    send(level + 1, 0, unit, True)

        final = states[levels % 2]
        share = row_tiles // 2
        for pair in range(pairs):
            for order in range(2):
                pltpu.matmul_push_rhs(eval_maps[pair], pair % 2, order)
            for i in range(share):
                for order in range(2):
                    pltpu.matmul_acc_lhs(
                        accumulators[2 * i + order],
                        final[(order * share + i) * pairs + pair],
                        load_staged_rhs=pair % 2 if i == 0 else None,
                    )
        for i in range(share):
            for order in range(2):
                top = (order * share + i) * TILE
                out_ref[top : top + TILE, :] = pltpu.matmul_pop(
                    accumulators[2 * i + order]
                ).astype(B16)

    pl.run_scoped(
        run, *[pltpu.ACC(order)((TILE, 2 * LANES), F32) for _ in range(units) for order in range(2)]
    )


def split_nodes(rank):
    nodes = np.cos(np.pi * (np.arange(rank) + 0.5) / rank) / 2
    pieces = []
    rest = np.tile(nodes, LANES // rank)
    for _ in range(3):
        piece = rest.astype(B16)
        pieces.append(piece.astype(np.float32))
        rest = rest - piece.astype(np.float64)
    return np.stack(pieces)


def level_plan(levels, local_levels, rows_per):
    plan = [("tiles", level) for level in range(local_levels)]
    stride = rows_per
    for _ in range(levels - local_levels):
        if stride < TILE:
            plan.append(("rows", stride))
        else:
            plan.append(("tiles", local_levels + (stride // TILE).bit_length() - 1))
        stride *= 2
    return tuple(plan)


def on_device(charges, source_order, velocity, leaf_weight, mixing, eval_weight, target_order):
    leaf = leaf_weight.shape[0] // 2
    width = leaf_weight.shape[1]
    boxes = charges.shape[1] // leaf
    group = LANES // leaf
    pairs = group // 2
    rows = boxes // group
    devices = lax.axis_size("wide") * lax.axis_size("narrow")
    rows_per = rows // devices
    levels = mixing.shape[0]
    local_levels = levels - (devices.bit_length() - 1)
    assert width == LANES and 1 << local_levels == pairs

    charge_rows = charges.reshape(2, rows, LANES).transpose(1, 0, 2).reshape(2 * rows, LANES)
    packed = pl.pallas_call(
        functools.partial(pack_kernel, leaf),
        out_shape=jax.ShapeDtypeStruct((rows, 3 * LANES), B16),
        compiler_params=VMEM,
        name="pack",
    )(charge_rows, source_order.reshape(rows, LANES), velocity.reshape(boxes // LANES, LANES))

    packed = lax.all_to_all(
        packed.reshape(devices, rows_per, 3 * LANES), AXES, 0, 0, tiled=True
    ).reshape(rows, 3 * LANES)

    square = (2 * LANES, 2 * LANES)
    weights = pl.pallas_call(
        functools.partial(maps_kernel, leaf),
        out_shape=[
            jax.ShapeDtypeStruct((levels, 2, *square), B16),
            jax.ShapeDtypeStruct((pairs, *square), B16),
            jax.ShapeDtypeStruct((pairs, *square), B16),
            jax.ShapeDtypeStruct((pairs // 2, *square), B16),
        ],
        compiler_params=VMEM,
        cost_estimate=pl.CostEstimate(flops=10**9, bytes_accessed=10**7, transcendentals=0),
        name="maps",
    )(leaf_weight, mixing, eval_weight, jnp.asarray(split_nodes(width // 2)))

    tiles = rows // TILE * pairs
    state = pltpu.VMEM((tiles, TILE, 2 * LANES), B16)
    table = pltpu.VMEM((tiles, TILE, LANES), F32)
    values = pl.pallas_call(
        functools.partial(butterfly_kernel, level_plan(levels, local_levels, rows_per)),
        out_shape=jax.ShapeDtypeStruct((rows, 2 * LANES), B16),
        scratch_shapes=[state, state] + [table] * 7,
        compiler_params=VMEM,
        name="butterfly",
    )(packed, *weights)

    values = lax.all_to_all(
        values.reshape(devices, rows_per, 2 * LANES), AXES, 0, 0, tiled=True
    ).reshape(rows, 2 * LANES)

    out = pl.pallas_call(
        functools.partial(unpack_kernel, leaf),
        out_shape=jax.ShapeDtypeStruct((2 * rows, LANES), F32),
        compiler_params=VMEM,
        name="unpack",
    )(values, target_order.reshape(rows, LANES))
    return out.reshape(rows, 2, LANES).transpose(1, 0, 2).reshape(2, rows * LANES)


def solution(mesh):
    mapped = jax.shard_map(
        on_device,
        mesh=mesh,
        in_specs=(
            P(None, AXES),
            P(AXES),
            P(AXES),
            P(),
            P(),
            P(),
            P(AXES),
        ),
        out_specs=P(None, AXES),
        check_vma=False,
    )

    def program(*arrays):
        with jax.sharding.use_abstract_mesh(mesh.abstract_mesh):
            return mapped(*arrays)

    return program
```

time: 623 us -> 59.2 us (0.10)
  local copies, waits for them, and re-layouts: 255 us -> 2.14 us
  waiting for transfers between devices: 225 us -> 7.44 us
  other arithmetic: 100 us -> 0 us
  matrix products: 28.1 us -> 0 us
  Pallas kernels: 0 us -> 28.1 us
  blocking collectives: 0 us -> 13.9 us
    ppermute x5 -> x0, waiting for transfers between devices: 225 us -> none  [from_partner(): return lax.ppermute(block, axis, route)]
    broadcast_in_dim x16 -> x0, local copies, waits for them, and re-layouts: 106 us -> none  [pick_within_box(): jnp.where(order_rows[None] == slot_no, source_rows[..., slot_no:slot_no +...]
    another operation x11 -> x0, other arithmetic: 75.2 us -> none
    slice x7 -> x0, local copies, waits for them, and re-layouts: 63.7 us -> none  [the longest x2 46.4 us: pick_within_box(): source_rows[..., slot_no:slot_no + 1]]
    eq x16 -> x0, local copies, waits for them, and re-layouts: 29.8 us -> none  [pick_within_box(): order_rows[None] == slot_no]
    pallas_call x0 -> x4, Pallas kernels: none -> 28.1 us  [the longest x1 17.6 us: on_device(): pl.pallas_call(functools.partial(butterfly_kernel, level_plan(levels, loc...]
    dot_general x24 -> x0, matrix products: 28.1 us -> none  [the longest x5 12 us: combine_pair(): jnp.dot(far_part, section_maps[bit_value, 1 - bit_value], preferred_eleme...]
    another operation x5 -> x0, local copies, waits for them, and re-layouts: 23.6 us -> none  [the longest x1 15.6 us: butterfly_section(): pre = jnp.stack(results, axis=1).reshape(total, width)]
  transfers between devices with their start and end apart: 5 -> 1, of which waited for: 5 -> 1; matrix products, arithmetic and copies ran while one was open for 1% -> 2% of each run, Pallas kernels for 0% -> 7%
where the time goes in v2:
time: 59.2 us; the launch traced here: 58.9 us
  Pallas kernels  28.1 us (47%)
  blocking collectives  13.9 us (23%)
  waiting for transfers between devices  7.44 us (13%)
  starting transfers between devices  7.3 us (12%)
  local copies, waits for them, and re-layouts  2.14 us (4%)
    pallas_call x1, Pallas kernels, on_device(): pl.pallas_call(functools.partial(butterfly_kernel, level_plan(levels, loc...  17.6 us
    all_to_all x1, blocking collectives, on_device(): lax.all_to_all(values.reshape(devices, rows_per, 2 * LANES), AXES, 0, 0,...  13.9 us
    all_to_all x1, waiting for transfers between devices, on_device(): lax.all_to_all(packed.reshape(devices, rows_per, 3 * LANES), AXES, 0, 0,...  7.44 us
    all_to_all x1, starting transfers between devices, on_device(): lax.all_to_all(packed.reshape(devices, rows_per, 3 * LANES), AXES, 0, 0,...  7.3 us
    pallas_call x1, Pallas kernels, on_device(): pl.pallas_call(functools.partial(maps_kernel, leaf), out_shape=[jax.Shape...  4.35 us
    pallas_call x1, Pallas kernels, on_device(): pl.pallas_call(functools.partial(pack_kernel, leaf), out_shape=jax.ShapeD...  3.59 us
    pallas_call x1, Pallas kernels, on_device(): pl.pallas_call(functools.partial(unpack_kernel, leaf), out_shape=jax.Shap...  2.56 us
    unnamed x3, local copies, waits for them, and re-layouts  2.14 us
  transfers between devices with their start and end apart: 1, of which 1 were waited for; matrix products, arithmetic and copies ran while one was open for 2% of the time, Pallas kernels for 7%

profile of v2, /device:TPU:0, one launch (start us, length us, event | category | flops | bytes accessed | tf_op | source)
XLA Modules:
  0.0 58.9 jit_solution(4128365944434669182)
XLA Ops:
  0.0 3.6 %pack.1 = bf16[512,384]{1,0:T(8,128)(2,1)} custom-call(f32[1024,128]{1,0:T(8,128)} %bitcast.21, s32[512,128]{1,0:T(8,128)} %bitcast.22, bf16[64,128]{1,0:T(8,128)(2,1)} %bitcast.24), custom_call_target="tpu_custom_call" | custom-call | tf_op jit(solution)/shard_map/pack/pallas_call | solution.py:398
  3.6 7.3 %all-to-all-start = ((bf16[32,16,384]{2,1,0:T(8,128)(2,1)}), bf16[32,16,384]{2,1,0:T(8,128)(2,1)S(1)}, u32[]{:S(2)}, u32[]{:S(2)}) async-start(bf16[32,16,384]{2,1,0:T(8,128)(2,1)} %bitcast.17), calls=%async_computation | async-start | bytes 786432 | tf_op jit(solution)/shard_map/all_to_all | solution.py:405
  10.9 1.4 %copy.10.eval_ref = bf16[128,16]{1,0:T(8,128)(2,1)} copy(bf16[128,16]{0,1:T(8,128)(2,1)} %param.13) | data formatting | bytes 8192 | tf_op args[5]
  12.3 4.4 %maps.1 = (bf16[8,2,256,256]{3,2,1,0:T(8,128)(2,1)}, bf16[8,256,256]{2,1,0:T(8,128)(2,1)}, bf16[8,256,256]{2,1,0:T(8,128)(2,1)}, bf16[4,256,256]{2,1,0:T(8,128)(2,1)}) custom-call(bf16[16,128]{1,0:T(8,128)(2,1)} %leaf_ref.1, bf16[8,2,2,128,128]{4,3,2,1,0:T(8,128)(2,1)} %mixing_ref.1, bf16[128,16]{1,0:T(8,128)(2,1)} %copy.10.eval_ref, ...), custom_call_target="tpu_custom_call" | custom-call | flops 1000000000 | bytes 10000000 | tf_op jit(solution)/shard_map/maps/pallas_call | solution.py:410
  16.6 7.4 %all-to-all-done = bf16[32,16,384]{2,1,0:T(8,128)(2,1)S(1)} async-done(((bf16[32,16,384]{2,1,0:T(8,128)(2,1)}), bf16[32,16,384]{2,1,0:T(8,128)(2,1)S(1)}, u32[]{:S(2)}, u32[]{:S(2)}) %all-to-all-start) | async-done | bytes 393248 | tf_op jit(solution)/shard_map/all_to_all | solution.py:405
  24.1 0.0 copy-start
  24.1 0.7 %copy-done = bf16[32,16,384]{2,1,0:T(8,128)(2,1)} copy-done((bf16[32,16,384]{2,1,0:T(8,128)(2,1)}, bf16[32,16,384]{2,1,0:T(8,128)(2,1)S(1)}, u32[]{:S(2)}) %copy-start) | copy-done | bytes 393240
  24.8 17.6 %butterfly.1 = bf16[512,256]{1,0:T(8,128)(2,1)} custom-call(bf16[512,384]{1,0:T(8,128)(2,1)} %bitcast.18, bf16[8,2,256,256]{3,2,1,0:T(8,128)(2,1)} %get-tuple-element.9.maps, bf16[8,256,256]{2,1,0:T(8,128)(2,1)} %get-tuple-element.10.leaf_maps, bf16[8,256,256]{2,1,0:T(8,128)(2,1)} %get-tuple-element.11.eval_maps, ...), custom_call_target="tpu_custom_call" | custom-call | tf_op jit(solution)/shard_map/butterfly/pallas_call | solution.py:426
  42.4 13.9 %all_to_all.10 = bf16[32,16,256]{2,1,0:T(8,128)(2,1)} all-to-all(bf16[32,16,256]{2,1,0:T(8,128)(2,1)} %bitcast.20), channel_id=1, replica_groups=mesh['wide'=8,'narrow'=4] {'wide','narrow'}, dimensions={0} | all-to-all | bytes 524288 | tf_op jit(solution)/shard_map/all_to_all | solution.py:434
  56.3 2.6 %unpack.1 = f32[1024,128]{1,0:T(8,128)} custom-call(bf16[512,256]{1,0:T(8,128)(2,1)} %bitcast.19, s32[512,128]{1,0:T(8,128)} %bitcast.23), custom_call_target="tpu_custom_call" | custom-call | tf_op jit(solution)/shard_map/unpack/pallas_call | solution.py:438
Async XLA Ops:
  3.6 20.5 %all-to-all-start = ((bf16[32,16,384]{2,1,0:T(8,128)(2,1)}), bf16[32,16,384]{2,1,0:T(8,128)(2,1)S(1)}, u32[]{:S(2)}, u32[]{:S(2)}) async-start(bf16[32,16,384]{2,1,0:T(8,128)(2,1)} %bitcast.17), calls=%async_computation | async-start | bytes 786432 | tf_op jit(solution)/shard_map/all_to_all | solution.py:405
  24.1 0.7 %copy-start = (bf16[32,16,384]{2,1,0:T(8,128)(2,1)}, bf16[32,16,384]{2,1,0:T(8,128)(2,1)S(1)}, u32[]{:S(2)}) copy-start(bf16[32,16,384]{2,1,0:T(8,128)(2,1)S(1)} %all-to-all-done) | copy-start | bytes 1179652

commit v3 on v2

--- a/solution.py
+++ b/solution.py
@@ -15,7 +15,8 @@
 AXES = ("wide", "narrow")
 F32, B16 = jnp.float32, jnp.bfloat16
 UNITS = 32
-VMEM = pltpu.CompilerParams(vmem_limit_bytes=56 * 2**20)
+def vmem(mebibytes):
+    return pltpu.CompilerParams(vmem_limit_bytes=mebibytes * 2**20)
 
 
 def lane_index(shape):
@@ -398,7 +399,7 @@
     packed = pl.pallas_call(
         functools.partial(pack_kernel, leaf),
         out_shape=jax.ShapeDtypeStruct((rows, 3 * LANES), B16),
-        compiler_params=VMEM,
+        compiler_params=vmem(8),
         name="pack",
     )(charge_rows, source_order.reshape(rows, LANES), velocity.reshape(boxes // LANES, LANES))
 
@@ -415,7 +416,7 @@
             jax.ShapeDtypeStruct((pairs, *square), B16),
             jax.ShapeDtypeStruct((pairs // 2, *square), B16),
         ],
-        compiler_params=VMEM,
+        compiler_params=vmem(20),
         cost_estimate=pl.CostEstimate(flops=10**9, bytes_accessed=10**7, transcendentals=0),
         name="maps",
     )(leaf_weight, mixing, eval_weight, jnp.asarray(split_nodes(width // 2)))
@@ -427,7 +428,7 @@
         functools.partial(butterfly_kernel, level_plan(levels, local_levels, rows_per)),
         out_shape=jax.ShapeDtypeStruct((rows, 2 * LANES), B16),
         scratch_shapes=[state, state] + [table] * 7,
-        compiler_params=VMEM,
+        compiler_params=vmem(32),
         name="butterfly",
     )(packed, *weights)
 
@@ -438,7 +439,7 @@
     out = pl.pallas_call(
         functools.partial(unpack_kernel, leaf),
         out_shape=jax.ShapeDtypeStruct((2 * rows, LANES), F32),
-        compiler_params=VMEM,
+        compiler_params=vmem(8),
         name="unpack",
     )(values, target_order.reshape(rows, LANES))
     return out.reshape(rows, 2, LANES).transpose(1, 0, 2).reshape(2, rows * LANES)

time: 59.2 us -> 57.6 us (0.973)
  local copies, waits for them, and re-layouts: 2.14 us -> 11.5 us
  Pallas kernels: 28.1 us -> 20 us
  waiting for transfers between devices: 7.44 us -> 5.13 us
  blocking collectives: 13.9 us -> 13 us
    unnamed x3 -> x25, local copies, waits for them, and re-layouts: 2.14 us -> 11.5 us
    pallas_call x1, Pallas kernels: 17.6 us -> 14.5 us  [on_device(): pl.pallas_call(functools.partial(butterfly_kernel, level_plan(levels, loc...]
    pallas_call x1, Pallas kernels: 4.35 us -> 1.51 us  [on_device(): pl.pallas_call(functools.partial(maps_kernel, leaf), out_shape=[jax.Shape...]
    all_to_all x1, waiting for transfers between devices: 7.44 us -> 5.13 us  [on_device(): lax.all_to_all(packed.reshape(devices, rows_per, 3 * LANES), AXES, 0, 0,...]
    pallas_call x1, Pallas kernels: 3.59 us -> 2.47 us  [on_device(): pl.pallas_call(functools.partial(pack_kernel, leaf), out_shape=jax.ShapeD...]
    pallas_call x1, Pallas kernels: 2.56 us -> 1.53 us  [on_device(): pl.pallas_call(functools.partial(unpack_kernel, leaf), out_shape=jax.Shap...]
    all_to_all x1, blocking collectives: 13.9 us -> 13 us  [on_device(): lax.all_to_all(values.reshape(devices, rows_per, 2 * LANES), AXES, 0, 0,...]
  transfers between devices with their start and end apart: 1 -> 1, of which waited for: 1 -> 1; matrix products, arithmetic and copies ran while one was open for 2% -> 2% of each run, Pallas kernels for 7% -> 3%
where the time goes in v3:
time: 57.6 us; the launch traced here: 57 us
  Pallas kernels  20 us (35%)
  blocking collectives  13 us (23%)
  local copies, waits for them, and re-layouts  11.5 us (20%)
  starting transfers between devices  7.3 us (13%)
  waiting for transfers between devices  5.13 us (9%)
    pallas_call x1, Pallas kernels, on_device(): pl.pallas_call(functools.partial(butterfly_kernel, level_plan(levels, loc...  14.5 us
    all_to_all x1, blocking collectives, on_device(): lax.all_to_all(values.reshape(devices, rows_per, 2 * LANES), AXES, 0, 0,...  13 us
    unnamed x25, local copies, waits for them, and re-layouts  11.5 us
    all_to_all x1, starting transfers between devices, on_device(): lax.all_to_all(packed.reshape(devices, rows_per, 3 * LANES), AXES, 0, 0,...  7.3 us
    all_to_all x1, waiting for transfers between devices, on_device(): lax.all_to_all(packed.reshape(devices, rows_per, 3 * LANES), AXES, 0, 0,...  5.13 us
    pallas_call x1, Pallas kernels, on_device(): pl.pallas_call(functools.partial(pack_kernel, leaf), out_shape=jax.ShapeD...  2.47 us
    pallas_call x1, Pallas kernels, on_device(): pl.pallas_call(functools.partial(unpack_kernel, leaf), out_shape=jax.Shap...  1.53 us
    pallas_call x1, Pallas kernels, on_device(): pl.pallas_call(functools.partial(maps_kernel, leaf), out_shape=[jax.Shape...  1.51 us
  transfers between devices with their start and end apart: 1, of which 1 were waited for; matrix products, arithmetic and copies ran while one was open for 2% of the time, Pallas kernels for 3%

profile of v3, /device:TPU:0, one launch (start us, length us, event | category | flops | bytes accessed | tf_op | source)
XLA Modules:
  0.0 57.0 jit_solution(1483689607965483026)
XLA Ops:
  0.0 0.0 copy-start.2
  0.0 1.0 %copy-done.2 = f32[2,65536]{1,0:T(2,128)S(1)} copy-done((f32[2,65536]{1,0:T(2,128)S(1)}, f32[2,65536]{1,0:T(2,128)}, u32[]{:S(2)}) %copy-start.2) | copy-done | bytes 524312
  1.0 0.0 copy-start.5
  1.0 0.9 %copy-done.5 = s32[65536]{0:T(1024)S(1)} copy-done((s32[65536]{0:T(1024)S(1)}, s32[65536]{0:T(1024)}, u32[]{:S(2)}) %copy-start.5) | copy-done | bytes 262168
  2.0 0.0 copy-start.8
  2.0 0.7 %copy-done.8 = bf16[8192]{0:T(1024)(128)(2,1)S(1)} copy-done((bf16[8192]{0:T(1024)(128)(2,1)S(1)}, bf16[8192]{0:T(1024)(128)(2,1)}, u32[]{:S(2)}) %copy-start.8) | copy-done | bytes 16408
  2.7 2.5 %pack.1 = bf16[512,384]{1,0:T(8,128)(2,1)} custom-call(f32[1024,128]{1,0:T(8,128)S(1)} %bitcast.20, s32[512,128]{1,0:T(8,128)S(1)} %bitcast.21, bf16[64,128]{1,0:T(8,128)(2,1)S(1)} %bitcast.23), custom_call_target="tpu_custom_call" | custom-call | tf_op jit(solution)/shard_map/pack/pallas_call | solution.py:399
  5.2 7.3 %all-to-all-start = ((bf16[32,16,384]{2,1,0:T(8,128)(2,1)}), bf16[32,16,384]{2,1,0:T(8,128)(2,1)S(1)}, u32[]{:S(2)}, u32[]{:S(2)}) async-start(bf16[32,16,384]{2,1,0:T(8,128)(2,1)} %bitcast.5), calls=%async_computation | async-start | bytes 786432 | tf_op jit(solution)/shard_map/all_to_all | solution.py:406
  12.5 1.4 %copy.10.eval_ref = bf16[128,16]{1,0:T(8,128)(2,1)} copy(bf16[128,16]{0,1:T(8,128)(2,1)} %param.13) | data formatting | bytes 8192 | tf_op args[5]
  13.9 0.0 copy-start.7
  13.9 0.8 %copy-done.7 = bf16[128,16]{1,0:T(8,128)(2,1)S(1)} copy-done((bf16[128,16]{1,0:T(8,128)(2,1)S(1)}, bf16[128,16]{1,0:T(8,128)(2,1)}, u32[]{:S(2)}) %copy-start.7) | copy-done | bytes 4120
  14.7 0.0 copy-start.9
  14.7 1.2 %copy-done.9 = bf16[8,2,2,128,128]{4,3,2,1,0:T(8,128)(2,1)S(1)} copy-done((bf16[8,2,2,128,128]{4,3,2,1,0:T(8,128)(2,1)S(1)}, bf16[8,2,2,128,128]{4,3,2,1,0:T(8,128)(2,1)}, u32[]{:S(2)}) %copy-start.9) | copy-done | bytes 1048600
  15.9 0.0 copy-start.10
  15.9 0.7 %copy-done.10 = bf16[16,128]{1,0:T(8,128)(2,1)S(1)} copy-done((bf16[16,128]{1,0:T(8,128)(2,1)S(1)}, bf16[16,128]{1,0:T(8,128)(2,1)}, u32[]{:S(2)}) %copy-start.10) | copy-done | bytes 4120
  16.6 0.0 copy-start.11
  16.6 0.7 %copy-done.11 = f32[3,128]{1,0:T(4,128)S(1)} copy-done((f32[3,128]{1,0:T(4,128)S(1)}, f32[3,128]{1,0:T(4,128)}, u32[]{:S(2)}) %copy-start.11) | copy-done | bytes 1560
  17.2 1.5 %maps.1 = (bf16[8,2,256,256]{3,2,1,0:T(8,128)(2,1)S(1)}, bf16[8,256,256]{2,1,0:T(8,128)(2,1)S(1)}, bf16[8,256,256]{2,1,0:T(8,128)(2,1)S(1)}, bf16[4,256,256]{2,1,0:T(8,128)(2,1)S(1)}) custom-call(bf16[16,128]{1,0:T(8,128)(2,1)S(1)} %copy-done.10, bf16[8,2,2,128,128]{4,3,2,1,0:T(8,128)(2,1)S(1)} %copy-done.9, bf16[128,16]{1,0:T(8,128)(2,1)S(1)} %copy-done.7, ...), custom_call_target="tpu_custom_call" | custom-call | flops 1000000000 | bytes 10000000 | tf_op jit(solution)/shard_map/maps/pallas_call | solution.py:411
  18.8 0.0 copy-start
  18.8 1.0 %copy-done = bf16[8,256,256]{2,1,0:T(8,128)(2,1)} copy-done((bf16[8,256,256]{2,1,0:T(8,128)(2,1)}, bf16[8,256,256]{2,1,0:T(8,128)(2,1)S(1)}, u32[]{:S(2)}) %copy-start) | copy-done | bytes 1048600
  19.7 0.0 copy-start.3
  19.7 0.8 %copy-done.3 = bf16[4,256,256]{2,1,0:T(8,128)(2,1)} copy-done((bf16[4,256,256]{2,1,0:T(8,128)(2,1)}, bf16[4,256,256]{2,1,0:T(8,128)(2,1)S(1)}, u32[]{:S(2)}) %copy-start.3) | copy-done | bytes 524312
  20.5 5.1 %all-to-all-done = bf16[32,16,384]{2,1,0:T(8,128)(2,1)S(1)} async-done(((bf16[32,16,384]{2,1,0:T(8,128)(2,1)}), bf16[32,16,384]{2,1,0:T(8,128)(2,1)S(1)}, u32[]{:S(2)}, u32[]{:S(2)}) %all-to-all-start) | async-done | bytes 393248 | tf_op jit(solution)/shard_map/all_to_all | solution.py:406
  25.7 0.0 copy-start.1
  25.7 1.2 %copy-done.1 = bf16[8,256,256]{2,1,0:T(8,128)(2,1)S(1)} copy-done((bf16[8,256,256]{2,1,0:T(8,128)(2,1)S(1)}, bf16[8,256,256]{2,1,0:T(8,128)(2,1)}, u32[]{:S(2)}) %copy-start.1) | copy-done | bytes 1048600
  26.9 0.0 copy-start.4
  26.9 1.0 %copy-done.4 = bf16[4,256,256]{2,1,0:T(8,128)(2,1)S(1)} copy-done((bf16[4,256,256]{2,1,0:T(8,128)(2,1)S(1)}, bf16[4,256,256]{2,1,0:T(8,128)(2,1)}, u32[]{:S(2)}) %copy-start.4) | copy-done | bytes 524312
  27.9 0.0 copy-start.6
  27.9 14.5 %butterfly.1 = bf16[512,256]{1,0:T(8,128)(2,1)S(1)} custom-call(bf16[512,384]{1,0:T(8,128)(2,1)S(1)} %bitcast.17, bf16[8,2,256,256]{3,2,1,0:T(8,128)(2,1)S(1)} %get-tuple-element.9.maps, bf16[8,256,256]{2,1,0:T(8,128)(2,1)S(1)} %get-tuple-element.10.leaf_maps, bf16[8,256,256]{2,1,0:T(8,128)(2,1)S(1)} %copy-done.1, bf16[4,256,256]{2,1,0:T(8,128)(2,1)S(1)} %copy-done.4), custom_call_target="tpu_custom_call" | custom-call | tf_op jit(solution)/shard_map/butterfly/pallas_call | solution.py:427
  42.4 13.0 %all_to_all.10 = bf16[32,16,256]{2,1,0:T(8,128)(2,1)S(1)} all-to-all(bf16[32,16,256]{2,1,0:T(8,128)(2,1)S(1)} %bitcast.19), channel_id=1, replica_groups=mesh['wide'=8,'narrow'=4] {'wide','narrow'}, dimensions={0} | all-to-all | bytes 524288 | tf_op jit(solution)/shard_map/all_to_all | solution.py:435
  55.4 0.0 copy-done.6
  55.4 1.5 %unpack.1 = f32[1024,128]{1,0:T(8,128)} custom-call(bf16[512,256]{1,0:T(8,128)(2,1)S(1)} %bitcast.18, s32[512,128]{1,0:T(8,128)S(1)} %bitcast.22), custom_call_target="tpu_custom_call" | custom-call | tf_op jit(solution)/shard_map/unpack/pallas_call | solution.py:439
Async XLA Ops:
  0.0 1.0 %copy-start.2 = (f32[2,65536]{1,0:T(2,128)S(1)}, f32[2,65536]{1,0:T(2,128)}, u32[]{:S(2)}) copy-start(f32[2,65536]{1,0:T(2,128)} %param.8) | copy-start | bytes 1572868
  1.0 0.9 %copy-start.5 = (s32[65536]{0:T(1024)S(1)}, s32[65536]{0:T(1024)}, u32[]{:S(2)}) copy-start(s32[65536]{0:T(1024)} %param.9) | copy-start | bytes 786436
  2.0 0.7 %copy-start.8 = (bf16[8192]{0:T(1024)(128)(2,1)S(1)}, bf16[8192]{0:T(1024)(128)(2,1)}, u32[]{:S(2)}) copy-start(bf16[8192]{0:T(1024)(128)(2,1)} %param.10) | copy-start | bytes 49156
  5.2 20.5 %all-to-all-start = ((bf16[32,16,384]{2,1,0:T(8,128)(2,1)}), bf16[32,16,384]{2,1,0:T(8,128)(2,1)S(1)}, u32[]{:S(2)}, u32[]{:S(2)}) async-start(bf16[32,16,384]{2,1,0:T(8,128)(2,1)} %bitcast.5), calls=%async_computation | async-start | bytes 786432 | tf_op jit(solution)/shard_map/all_to_all | solution.py:406
  13.9 0.8 %copy-start.7 = (bf16[128,16]{1,0:T(8,128)(2,1)S(1)}, bf16[128,16]{1,0:T(8,128)(2,1)}, u32[]{:S(2)}) copy-start(bf16[128,16]{1,0:T(8,128)(2,1)} %copy.10.eval_ref) | copy-start | bytes 12292
  14.7 1.2 %copy-start.9 = (bf16[8,2,2,128,128]{4,3,2,1,0:T(8,128)(2,1)S(1)}, bf16[8,2,2,128,128]{4,3,2,1,0:T(8,128)(2,1)}, u32[]{:S(2)}) copy-start(bf16[8,2,2,128,128]{4,3,2,1,0:T(8,128)(2,1)} %mixing_ref.1) | copy-start | bytes 3145732
  15.9 0.7 %copy-start.10 = (bf16[16,128]{1,0:T(8,128)(2,1)S(1)}, bf16[16,128]{1,0:T(8,128)(2,1)}, u32[]{:S(2)}) copy-start(bf16[16,128]{1,0:T(8,128)(2,1)} %leaf_ref.1) | copy-start | bytes 12292
  16.6 0.7 %copy-start.11 = (f32[3,128]{1,0:T(4,128)S(1)}, f32[3,128]{1,0:T(4,128)}, u32[]{:S(2)}) copy-start(f32[3,128]{1,0:T(4,128)} %constant.2.clone.nodes_ref) | copy-start | bytes 4612
  18.8 1.0 %copy-start = (bf16[8,256,256]{2,1,0:T(8,128)(2,1)}, bf16[8,256,256]{2,1,0:T(8,128)(2,1)S(1)}, u32[]{:S(2)}) copy-start(bf16[8,256,256]{2,1,0:T(8,128)(2,1)S(1)} %get-tuple-element.11.eval_maps) | copy-start | bytes 3145732
  19.7 0.8 %copy-start.3 = (bf16[4,256,256]{2,1,0:T(8,128)(2,1)}, bf16[4,256,256]{2,1,0:T(8,128)(2,1)S(1)}, u32[]{:S(2)}) copy-start(bf16[4,256,256]{2,1,0:T(8,128)(2,1)S(1)} %get-tuple-element.12.node_maps) | copy-start | bytes 1572868
  25.7 1.2 %copy-start.1 = (bf16[8,256,256]{2,1,0:T(8,128)(2,1)S(1)}, bf16[8,256,256]{2,1,0:T(8,128)(2,1)}, u32[]{:S(2)}) copy-start(bf16[8,256,256]{2,1,0:T(8,128)(2,1)} %copy-done) | copy-start | bytes 3145732
  26.9 1.0 %copy-start.4 = (bf16[4,256,256]{2,1,0:T(8,128)(2,1)S(1)}, bf16[4,256,256]{2,1,0:T(8,128)(2,1)}, u32[]{:S(2)}) copy-start(bf16[4,256,256]{2,1,0:T(8,128)(2,1)} %copy-done.3) | copy-start | bytes 1572868
  27.9 27.5 %copy-start.6 = (s32[65536]{0:T(1024)S(1)}, s32[65536]{0:T(1024)}, u32[]{:S(2)}) copy-start(s32[65536]{0:T(1024)} %param.14) | copy-start | bytes 786436

commit v4 on v3

--- a/solution.py
+++ b/solution.py
@@ -15,6 +15,7 @@
 AXES = ("wide", "narrow")
 F32, B16 = jnp.float32, jnp.bfloat16
 UNITS = 32
+ROOM = 200
 def vmem(mebibytes):
     return pltpu.CompilerParams(vmem_limit_bytes=mebibytes * 2**20)
 
@@ -93,10 +94,13 @@
     return bin(pair).count("1") % 2 == 1
 
 
-def maps_kernel(leaf, leaf_ref, mixing_ref, eval_ref, nodes_ref, maps, leaf_maps, eval_maps, node_maps):
+def boxes_of_pair(pair, pairs):
+    return (pair + pairs, pair) if odd_pair(pair) else (pair, pair + pairs)
+
+
+def maps_kernel(leaf, mixing_ref, eval_ref, weights):
     levels = mixing_ref.shape[0]
-    pairs = leaf_maps.shape[0]
-    group = 2 * pairs
+    pairs = LANES // leaf // 2
     low = lane_index((HALF, LANES)) < HALF
 
     @pl.loop(0, levels)
@@ -109,7 +113,7 @@
                 first_far, second_far = swapped(to_first), swapped(to_second)
                 for order in range(2):
                     top = part * LANES + (source ^ order) * HALF
-                    place = maps.at[level, order, top : top + HALF]
+                    place = weights.at[2 * level + order, top : top + HALF]
                     if order == 0:
                         real = jnp.where(low, to_first, second_far)
                         imag = jnp.where(low, first_far, to_second)
@@ -119,44 +123,52 @@
                     place[:, :LANES] = real.astype(B16)
                     place[:, LANES:] = imag.astype(B16)
 
-    leaf_rows = leaf_ref[...].astype(F32)
-    low = lane_index((LANES, LANES)) < HALF
-    box_of_row = row_index((LANES, LANES)) // leaf
     box_of_lane = lane_index((HALF, LANES)) // leaf
     slot = lane_index((2 * leaf, 2 * LANES))
     spread = (slot // LANES * leaf + slot % leaf == row_index((2 * leaf, 2 * LANES))).astype(B16)
     eval_rows = jnp.dot(eval_ref[...], spread, preferred_element_type=F32)
-    node_row = row_index((LANES, LANES))
-    nodes = jnp.zeros((LANES, LANES), F32)
+    for pair in range(pairs):
+        for number, box in enumerate(boxes_of_pair(pair, pairs)):
+            for part in range(2):
+                top = (2 * part + number) * HALF
+                for side in range(2):
+                    lanes = slice(side * LANES, (side + 1) * LANES)
+                    block = eval_rows[part * HALF : (part + 1) * HALF, lanes]
+                    weights[2 * levels + pair, top : top + HALF, lanes] = jnp.where(
+                        box_of_lane == box, block, 0.0
+                    ).astype(B16)
+
+
+def first_maps(leaf, pairs, leaf_ref, nodes_ref, leaf_maps, node_maps):
+    group = 2 * pairs
+    leaf_rows = leaf_ref[...].astype(F32)
+    shape = (LANES, LANES)
+    low = lane_index(shape) < HALF
+    box_of_row = row_index(shape) // leaf
+    node_row = row_index(shape)
+    nodes = jnp.zeros(shape, F32)
     for piece in range(3):
         nodes = jnp.where(node_row // group == piece, nodes_ref[piece : piece + 1, :], nodes)
-    node_maps[...] = jnp.zeros(node_maps.shape, B16)
-    for pair in range(pairs):
-        left, right = (pair + pairs, pair) if odd_pair(pair) else (pair, pair + pairs)
-        for part in range(2):
-            tiled = jnp.broadcast_to(
-                leaf_rows[part * leaf : (part + 1) * leaf][None], (group, leaf, LANES)
-            ).reshape(LANES, LANES)
-            far = swapped(tiled)
+    for part in range(2):
+        tiled = jnp.broadcast_to(
+            leaf_rows[part * leaf : (part + 1) * leaf][None], (group, leaf, LANES)
+        ).reshape(shape)
+        far = swapped(tiled)
+        here = slice(part * LANES, (part + 1) * LANES)
+        for pair in range(pairs):
+            left, right = boxes_of_pair(pair, pairs)
             first, second = box_of_row == left, box_of_row == right
-            here = slice(part * LANES, (part + 1) * LANES)
             leaf_maps[pair, here, :LANES] = jnp.where(
                 low, jnp.where(first, tiled, 0.0), jnp.where(second, far, 0.0)
             ).astype(B16)
             leaf_maps[pair, here, LANES:] = jnp.where(
                 low, jnp.where(first, far, 0.0), jnp.where(second, tiled, 0.0)
             ).astype(B16)
-            for number, box in enumerate((left, right)):
-                top = (2 * part + number) * HALF
-                for side in range(2):
-                    lanes = slice(side * LANES, (side + 1) * LANES)
-                    block = eval_rows[part * HALF : (part + 1) * HALF, lanes]
-                    eval_maps[pair, top : top + HALF, lanes] = jnp.where(
-                        box_of_lane == box, block, 0.0
-                    ).astype(B16)
-        lanes = slice(pair % 2 * LANES, (pair % 2 + 1) * LANES)
-        mine = node_row % group == jnp.where(low, left, right)
-        node_maps[pair // 2, :LANES, lanes] = jnp.where(mine, nodes, 0.0).astype(B16)
+            lanes = slice(pair % 2 * LANES, (pair % 2 + 1) * LANES)
+            mine = node_row % group == jnp.where(low, left, right)
+            node_maps[pair // 2, here, lanes] = jnp.where(
+                mine, nodes if part == 0 else 0.0, 0.0
+            ).astype(B16)
 
 
 def sine_cosine(turns):
@@ -176,11 +188,11 @@
 
 
 def butterfly_kernel(
-    plan, packed_ref, maps, leaf_maps, eval_maps, node_maps, out_ref,
+    plan, leaf, pairs, packed_ref, leaf_ref, nodes_ref, weights_ref, out_ref,
+    leaf_maps, node_maps, weights, arrived,
     state_a, state_b, twice_ref, *tables,
 ):
     rows = packed_ref.shape[0]
-    pairs = leaf_maps.shape[0]
     levels = len(plan)
     states = (state_a, state_b)
     cosines, sines = tables[:3], tables[3:]
@@ -225,10 +237,21 @@
             tile = block * (2 * units) + (unit >> bit << (bit + 1) | unit & (stride - 1))
         return tile, tile + stride
 
+    bounds = (0, 2 * levels, 2 * levels + pairs)
+    fetches = [
+        pltpu.make_async_copy(
+            weights_ref.at[start:stop], weights.at[start:stop], arrived.at[number]
+        )
+        for number, (start, stop) in enumerate(zip(bounds, bounds[1:]))
+    ]
+    for fetch in fetches:
+        fetch.start()
+    first_maps(leaf, pairs, leaf_ref, nodes_ref, leaf_maps, node_maps)
+
     def run(*accumulators):
         def load_maps(level):
             for order in range(2):
-                pltpu.matmul_push_rhs(maps[level, order], 0, order)
+                pltpu.matmul_push_rhs(weights[2 * level + order], 0, order)
 
         def send(level, block, unit, fresh):
             source = states[level % 2]
@@ -310,6 +333,7 @@
                     sines[0][tile] = sine
                     state_a[tile] = pltpu.matmul_pop(accumulators[2 * i + order]).astype(B16)
 
+        fetches[0].wait()
         flowing = False
         for level in range(levels):
             if not flowing:
@@ -335,11 +359,12 @@
                 if flowing:
                     send(level + 1, 0, unit, True)
 
+        fetches[1].wait()
         final = states[levels % 2]
         share = row_tiles // 2
         for pair in range(pairs):
             for order in range(2):
-                pltpu.matmul_push_rhs(eval_maps[pair], pair % 2, order)
+                pltpu.matmul_push_rhs(weights[2 * levels + pair], pair % 2, order)
             for i in range(share):
                 for order in range(2):
                     pltpu.matmul_acc_lhs(
@@ -399,7 +424,7 @@
     packed = pl.pallas_call(
         functools.partial(pack_kernel, leaf),
         out_shape=jax.ShapeDtypeStruct((rows, 3 * LANES), B16),
-        compiler_params=vmem(8),
+        compiler_params=vmem(56),
         name="pack",
     )(charge_rows, source_order.reshape(rows, LANES), velocity.reshape(boxes // LANES, LANES))
 
@@ -408,29 +433,37 @@
     ).reshape(rows, 3 * LANES)
 
     square = (2 * LANES, 2 * LANES)
+    count = 2 * levels + pairs
     weights = pl.pallas_call(
         functools.partial(maps_kernel, leaf),
-        out_shape=[
-            jax.ShapeDtypeStruct((levels, 2, *square), B16),
-            jax.ShapeDtypeStruct((pairs, *square), B16),
-            jax.ShapeDtypeStruct((pairs, *square), B16),
-            jax.ShapeDtypeStruct((pairs // 2, *square), B16),
-        ],
-        compiler_params=vmem(20),
+        grid=(1,),
+        out_specs=pl.BlockSpec((count, *square), lambda step: (0, 0, 0)),
+        out_shape=jax.ShapeDtypeStruct((max(count, ROOM), *square), B16),
+        compiler_params=vmem(56),
         cost_estimate=pl.CostEstimate(flops=10**9, bytes_accessed=10**7, transcendentals=0),
         name="maps",
-    )(leaf_weight, mixing, eval_weight, jnp.asarray(split_nodes(width // 2)))
+    )(mixing, eval_weight)
 
     tiles = rows // TILE * pairs
     state = pltpu.VMEM((tiles, TILE, 2 * LANES), B16)
     table = pltpu.VMEM((tiles, TILE, LANES), F32)
     values = pl.pallas_call(
-        functools.partial(butterfly_kernel, level_plan(levels, local_levels, rows_per)),
+        functools.partial(butterfly_kernel, level_plan(levels, local_levels, rows_per), leaf, pairs),
         out_shape=jax.ShapeDtypeStruct((rows, 2 * LANES), B16),
-        scratch_shapes=[state, state] + [table] * 7,
-        compiler_params=vmem(32),
+        in_specs=[pl.BlockSpec(memory_space=pltpu.VMEM)] * 3
+        + [pl.BlockSpec(memory_space=pltpu.HBM)],
+        scratch_shapes=[
+            pltpu.VMEM((pairs, *square), B16),
+            pltpu.VMEM((pairs // 2, *square), B16),
+            pltpu.VMEM((count, *square), B16),
+            pltpu.SemaphoreType.DMA((2,)),
+            state,
+            state,
+        ]
+        + [table] * 7,
+        compiler_params=vmem(40),
         name="butterfly",
-    )(packed, *weights)
+    )(packed, leaf_weight, jnp.asarray(split_nodes(width // 2)), weights)
 
     values = lax.all_to_all(
         values.reshape(devices, rows_per, 2 * LANES), AXES, 0, 0, tiled=True

time: 57.6 us -> 54 us (0.938)
  local copies, waits for them, and re-layouts: 11.5 us -> 1.41 us
  Pallas kernels: 20 us -> 24.4 us
  waiting for transfers between devices: 5.13 us -> 7.58 us
    unnamed x25 -> x7, local copies, waits for them, and re-layouts: 11.5 us -> 1.41 us
    pallas_call x1, Pallas kernels: 1.51 us -> 4.2 us  [on_device(): pl.pallas_call(functools.partial(maps_kernel, leaf), grid=(1,), out_specs...]
    all_to_all x1, waiting for transfers between devices: 5.13 us -> 7.58 us  [on_device(): lax.all_to_all(packed.reshape(devices, rows_per, 3 * LANES), AXES, 0, 0,...]
    pallas_call x1, Pallas kernels: 2.47 us -> 3.61 us  [on_device(): pl.pallas_call(functools.partial(pack_kernel, leaf), out_shape=jax.ShapeD...]
    pallas_call x1, Pallas kernels: 14.5 us -> 15 us  [on_device(): pl.pallas_call(functools.partial(butterfly_kernel, level_plan(levels, loc...]
  transfers between devices with their start and end apart: 1 -> 1, of which waited for: 1 -> 1; matrix products, arithmetic and copies ran while one was open for 2% -> 3% of each run, Pallas kernels for 3% -> 8%
where the time goes in v4:
time: 54 us; the launch traced here: 53.7 us
  Pallas kernels  24.4 us (45%)
  blocking collectives  13 us (24%)
  waiting for transfers between devices  7.58 us (14%)
  starting transfers between devices  7.3 us (14%)
  local copies, waits for them, and re-layouts  1.41 us (3%)
    pallas_call x1, Pallas kernels, on_device(): pl.pallas_call(functools.partial(butterfly_kernel, level_plan(levels, loc...  15 us
    all_to_all x1, blocking collectives, on_device(): lax.all_to_all(values.reshape(devices, rows_per, 2 * LANES), AXES, 0, 0,...  13 us
    all_to_all x1, waiting for transfers between devices, on_device(): lax.all_to_all(packed.reshape(devices, rows_per, 3 * LANES), AXES, 0, 0,...  7.58 us
    all_to_all x1, starting transfers between devices, on_device(): lax.all_to_all(packed.reshape(devices, rows_per, 3 * LANES), AXES, 0, 0,...  7.3 us
    pallas_call x1, Pallas kernels, on_device(): pl.pallas_call(functools.partial(maps_kernel, leaf), grid=(1,), out_specs...  4.2 us
    pallas_call x1, Pallas kernels, on_device(): pl.pallas_call(functools.partial(pack_kernel, leaf), out_shape=jax.ShapeD...  3.61 us
    pallas_call x1, Pallas kernels, on_device(): pl.pallas_call(functools.partial(unpack_kernel, leaf), out_shape=jax.Shap...  1.53 us
    unnamed x7, local copies, waits for them, and re-layouts  1.41 us
  transfers between devices with their start and end apart: 1, of which 1 were waited for; matrix products, arithmetic and copies ran while one was open for 3% of the time, Pallas kernels for 8%

profile of v4, /device:TPU:0, one launch (start us, length us, event | category | flops | bytes accessed | tf_op | source)
XLA Modules:
  0.0 53.7 jit_solution(12103330742751645493)
XLA Ops:
  0.0 0.0 copy-start.2
  0.0 0.0 copy-start.1
  0.0 3.6 %pack.1 = bf16[512,384]{1,0:T(8,128)(2,1)} custom-call(f32[1024,128]{1,0:T(8,128)} %bitcast.22, s32[512,128]{1,0:T(8,128)} %bitcast.23, bf16[64,128]{1,0:T(8,128)(2,1)} %bitcast.24), custom_call_target="tpu_custom_call" | custom-call | tf_op jit(solution)/shard_map/pack/pallas_call | solution.py:424
  3.6 7.3 %all-to-all-start = ((bf16[32,16,384]{2,1,0:T(8,128)(2,1)}), bf16[32,16,384]{2,1,0:T(8,128)(2,1)S(1)}, u32[]{:S(2)}, u32[]{:S(2)}) async-start(bf16[32,16,384]{2,1,0:T(8,128)(2,1)} %bitcast.21), calls=%async_computation | async-start | bytes 786432 | tf_op jit(solution)/shard_map/all_to_all | solution.py:431
  10.9 1.4 %copy.10.eval_ref = bf16[128,16]{1,0:T(8,128)(2,1)} copy(bf16[128,16]{0,1:T(8,128)(2,1)} %param.13) | data formatting | bytes 8192 | tf_op args[5]
  12.3 0.0 copy-start
  12.3 4.2 %maps.1.weights_ref = bf16[200,256,256]{2,1,0:T(8,128)(2,1)} custom-call(bf16[8,2,2,128,128]{4,3,2,1,0:T(8,128)(2,1)} %mixing_ref.1, bf16[128,16]{1,0:T(8,128)(2,1)} %copy.10.eval_ref), custom_call_target="tpu_custom_call" | custom-call | flops 1000000000 | bytes 10000000 | tf_op jit(solution)/shard_map/maps/pallas_call | solution.py:437
  16.5 7.6 %all-to-all-done = bf16[32,16,384]{2,1,0:T(8,128)(2,1)S(1)} async-done(((bf16[32,16,384]{2,1,0:T(8,128)(2,1)}), bf16[32,16,384]{2,1,0:T(8,128)(2,1)S(1)}, u32[]{:S(2)}, u32[]{:S(2)}) %all-to-all-start) | async-done | bytes 393248 | tf_op jit(solution)/shard_map/all_to_all | solution.py:431
  24.1 0.0 copy-done.2
  24.1 0.0 copy-done.1
  24.1 15.0 %butterfly.1 = bf16[512,256]{1,0:T(8,128)(2,1)S(1)} custom-call(bf16[512,384]{1,0:T(8,128)(2,1)S(1)} %bitcast.17, bf16[16,128]{1,0:T(8,128)(2,1)S(1)} %copy-done.1, f32[3,128]{1,0:T(4,128)S(1)} %copy-done.2, bf16[200,256,256]{2,1,0:T(8,128)(2,1)} %maps.1.weights_ref), custom_call_target="tpu_custom_call" | custom-call | tf_op jit(solution)/shard_map/butterfly/pallas_call | solution.py:450
  39.2 13.0 %all_to_all.10 = bf16[32,16,256]{2,1,0:T(8,128)(2,1)S(1)} all-to-all(bf16[32,16,256]{2,1,0:T(8,128)(2,1)S(1)} %bitcast.18), channel_id=1, replica_groups=mesh['wide'=8,'narrow'=4] {'wide','narrow'}, dimensions={0} | all-to-all | bytes 524288 | tf_op jit(solution)/shard_map/all_to_all | solution.py:468
  52.2 0.0 copy-done
  52.2 1.5 %unpack.1 = f32[1024,128]{1,0:T(8,128)} custom-call(bf16[512,256]{1,0:T(8,128)(2,1)S(1)} %bitcast.19, s32[512,128]{1,0:T(8,128)S(1)} %bitcast.20), custom_call_target="tpu_custom_call" | custom-call | tf_op jit(solution)/shard_map/unpack/pallas_call | solution.py:472
Async XLA Ops:
  0.0 24.1 %copy-start.2 = (f32[3,128]{1,0:T(4,128)S(1)}, f32[3,128]{1,0:T(4,128)}, u32[]{:S(2)}) copy-start(f32[3,128]{1,0:T(4,128)} %constant.2.clone.nodes_ref) | copy-start | bytes 4612
  0.0 24.1 %copy-start.1 = (bf16[16,128]{1,0:T(8,128)(2,1)S(1)}, bf16[16,128]{1,0:T(8,128)(2,1)}, u32[]{:S(2)}) copy-start(bf16[16,128]{1,0:T(8,128)(2,1)} %leaf_ref.1) | copy-start | bytes 12292
  3.6 20.5 %all-to-all-start = ((bf16[32,16,384]{2,1,0:T(8,128)(2,1)}), bf16[32,16,384]{2,1,0:T(8,128)(2,1)S(1)}, u32[]{:S(2)}, u32[]{:S(2)}) async-start(bf16[32,16,384]{2,1,0:T(8,128)(2,1)} %bitcast.21), calls=%async_computation | async-start | bytes 786432 | tf_op jit(solution)/shard_map/all_to_all | solution.py:431
  12.3 39.9 %copy-start = (s32[65536]{0:T(1024)S(1)}, s32[65536]{0:T(1024)}, u32[]{:S(2)}) copy-start(s32[65536]{0:T(1024)} %param.14) | copy-start | bytes 786436

commit v5 on v4

--- a/solution.py
+++ b/solution.py
@@ -11,6 +11,7 @@
 
 LANES = 128
 HALF = LANES // 2
+QUARTER = LANES // 4
 TILE = 16
 AXES = ("wide", "narrow")
 F32, B16 = jnp.float32, jnp.bfloat16
@@ -94,6 +95,15 @@
     return bin(pair).count("1") % 2 == 1
 
 
+def mirrored(index):
+    place = index % HALF
+    return index - place + jnp.where(place < QUARTER, place, HALF + QUARTER - 1 - place)
+
+
+def sign_of(index):
+    return jnp.where((index >= HALF) & (index % HALF >= QUARTER), -1.0, 1.0)
+
+
 def boxes_of_pair(pair, pairs):
     return (pair + pairs, pair) if odd_pair(pair) else (pair, pair + pairs)
 
@@ -102,14 +112,26 @@
     levels = mixing_ref.shape[0]
     pairs = LANES // leaf // 2
     low = lane_index((HALF, LANES)) < HALF
+    shape = (LANES, LANES)
+    mirror = jnp.where(
+        row_index(shape) == mirrored(lane_index(shape)), sign_of(lane_index(shape)), 0.0
+    ).astype(B16)
+    mirror_back = jnp.where(
+        lane_index(shape) == mirrored(row_index(shape)), sign_of(row_index(shape)), 0.0
+    ).astype(B16)
+
+    def mirrored_map(matrix):
+        matrix = jnp.dot(matrix, mirror, preferred_element_type=F32).astype(B16)
+        return jnp.dot(mirror_back, matrix, preferred_element_type=F32)
 
     @pl.loop(0, levels)
     def _(level):
         for source in range(2):
+            both = [mirrored_map(mixing_ref[level, target, source]) for target in range(2)]
             for part in range(2):
-                rows = slice(part * HALF, (part + 1) * HALF)
-                to_first = mixing_ref[level, 0, source, rows, :].astype(F32)
-                to_second = mixing_ref[level, 1, source, rows, :].astype(F32)
+                to_first, to_second = (
+                    matrix[part * HALF : (part + 1) * HALF] for matrix in both
+                )
                 first_far, second_far = swapped(to_first), swapped(to_second)
                 for order in range(2):
                     top = part * LANES + (source ^ order) * HALF
@@ -126,7 +148,8 @@
     box_of_lane = lane_index((HALF, LANES)) // leaf
     slot = lane_index((2 * leaf, 2 * LANES))
     spread = (slot // LANES * leaf + slot % leaf == row_index((2 * leaf, 2 * LANES))).astype(B16)
-    eval_rows = jnp.dot(eval_ref[...], spread, preferred_element_type=F32)
+    eval_rows = jnp.dot(mirror_back, eval_ref[...], preferred_element_type=F32).astype(B16)
+    eval_rows = jnp.dot(eval_rows, spread, preferred_element_type=F32)
     for pair in range(pairs):
         for number, box in enumerate(boxes_of_pair(pair, pairs)):
             for part in range(2):
@@ -142,7 +165,10 @@
 def first_maps(leaf, pairs, leaf_ref, nodes_ref, leaf_maps, node_maps):
     group = 2 * pairs
     leaf_rows = leaf_ref[...].astype(F32)
+    lanes = lane_index(leaf_rows.shape)
+    leaf_rows = jnp.take_along_axis(leaf_rows, mirrored(lanes), axis=1) * sign_of(lanes)
     shape = (LANES, LANES)
+    in_left = lane_index(shape) % HALF < QUARTER
     low = lane_index(shape) < HALF
     box_of_row = row_index(shape) // leaf
     node_row = row_index(shape)
@@ -165,10 +191,10 @@
                 low, jnp.where(first, far, 0.0), jnp.where(second, tiled, 0.0)
             ).astype(B16)
             lanes = slice(pair % 2 * LANES, (pair % 2 + 1) * LANES)
-            mine = node_row % group == jnp.where(low, left, right)
-            node_maps[pair // 2, here, lanes] = jnp.where(
-                mine, nodes if part == 0 else 0.0, 0.0
-            ).astype(B16)
+            mine = (node_row % group == jnp.where(in_left, left, right)) & (
+                lane_index(shape) // HALF == part
+            )
+            node_maps[pair // 2, here, lanes] = jnp.where(mine, nodes, 0.0).astype(B16)
 
 
 def sine_cosine(turns):
@@ -187,56 +213,24 @@
     return twice * half_cos, 1.0 - twice * half_sin
 
 
+def reversed_bits(number, bits):
+    return sum((number >> bit & 1) << (bits - 1 - bit) for bit in range(bits))
+
+
 def butterfly_kernel(
     plan, leaf, pairs, packed_ref, leaf_ref, nodes_ref, weights_ref, out_ref,
-    leaf_maps, node_maps, weights, arrived,
-    state_a, state_b, twice_ref, *tables,
+    leaf_maps, node_maps, weights, arrived, state_a, state_b, tables,
 ):
     rows = packed_ref.shape[0]
     levels = len(plan)
     states = (state_a, state_b)
-    cosines, sines = tables[:3], tables[3:]
-    low = lane_index((TILE, LANES)) < HALF
-    low16 = lax.broadcasted_iota(jnp.int16, (TILE, LANES), 1) < jnp.int16(HALF)
-
-    def merged(mask, first, second):
-        return jnp.concatenate(
-            [
-                jnp.where(mask, first[:, :LANES], second[:, :LANES]),
-                jnp.where(mask, first[:, LANES:], second[:, LANES:]),
-            ],
-            axis=1,
-        )
-
-    def turned(level, tile, real, imag):
-        now, last, coming = level % 3, (level - 1) % 3, (level + 1) % 3
-        cosine, sine = cosines[now][tile], sines[now][tile]
-        target = states[1 - level % 2]
-        target[tile, :, :LANES] = (real * cosine - imag * sine).astype(B16)
-        target[tile, :, LANES:] = (real * sine + imag * cosine).astype(B16)
-        if level + 1 < levels:
-            twice = twice_ref[tile]
-            last_cosine = cosines[last][tile] if level else 1.0
-            cosines[coming][tile] = twice * cosine - last_cosine
-            sines[coming][tile] = twice * sine - sines[last][tile] if level else twice * sine
-
+    rotations = [sum(kind == "tiles" for kind, _ in plan[:level]) for level in range(levels)]
+    row_tiles = rows // TILE
+    row_bits, pair_bits = row_tiles.bit_length() - 1, pairs.bit_length() - 1
     half_tiles = state_a.shape[0] // 2
     units = min(UNITS, half_tiles)
     blocks = half_tiles // units
-
-    def tiles_of(level, block, unit):
-        bit = plan[level][1]
-        stride = 1 << bit
-        if stride >= units:
-            start = block * units
-            base = lax.shift_left(lax.shift_right_logical(start, bit), bit + 1) | (
-                start & (stride - 1)
-            )
-            tile = base + unit
-        else:
-            tile = block * (2 * units) + (unit >> bit << (bit + 1) | unit & (stride - 1))
-        return tile, tile + stride
-
+    index_bits = row_bits + pair_bits
     bounds = (0, 2 * levels, 2 * levels + pairs)
     fetches = [
         pltpu.make_async_copy(
@@ -248,73 +242,64 @@
         fetch.start()
     first_maps(leaf, pairs, leaf_ref, nodes_ref, leaf_maps, node_maps)
 
+    low = lax.broadcasted_iota(jnp.int16, (TILE, LANES), 1) < jnp.int16(HALF)
+    lanes = lane_index((TILE // 2, LANES))
+    upper_rows = lanes // HALF * QUARTER + lanes % QUARTER
+    lower_rows = upper_rows + HALF
+
+    def place_of(row_tile, pair):
+        return reversed_bits(pair, pair_bits) << row_bits | reversed_bits(row_tile, row_bits)
+
+    def merged(first, second):
+        return jnp.concatenate(
+            [
+                jnp.where(low, first[:, :LANES], second[:, :LANES]),
+                jnp.where(low, first[:, LANES:], second[:, LANES:]),
+            ],
+            axis=1,
+        )
+
+    def spread(table):
+        return jnp.concatenate(
+            [
+                jnp.take_along_axis(table, upper_rows, axis=1),
+                jnp.take_along_axis(table, lower_rows, axis=1),
+            ],
+            axis=0,
+        )
+
+    def moved(place, count):
+        count = count % index_bits
+        return (place << count | place >> (index_bits - count)) & (2 * half_tiles - 1)
+
+    def turned(mixed, level, state, source, place):
+        real, imag = mixed[:, :LANES], mixed[:, LANES:]
+        cosine, sine = tables[level, source, :, :LANES], tables[level, source, :, LANES:]
+        state[place, :, :LANES] = real * cosine - imag * sine
+        state[place, :, LANES:] = real * sine + imag * cosine
+
     def run(*accumulators):
-        def load_maps(level):
-            for order in range(2):
-                pltpu.matmul_push_rhs(weights[2 * level + order], 0, order)
-
-        def send(level, block, unit, fresh):
-            source = states[level % 2]
-            first, second = (source[tile] for tile in tiles_of(level, block, unit))
-            for order in range(2):
-                pltpu.matmul_acc_lhs(
-                    accumulators[2 * unit + order],
-                    merged(low16, *((second, first) if order else (first, second))),
-                    load_staged_rhs=0 if fresh and unit == 0 else None,
-                )
-
-        def finish(level, block, unit):
-            one, other = (pltpu.matmul_pop(accumulators[2 * unit + order]) for order in range(2))
-            for target, tile in enumerate(tiles_of(level, block, unit)):
-                left, right = (other, one) if target else (one, other)
-                turned(
-                    level, tile,
-                    jnp.where(low, left[:, :LANES], right[:, :LANES]),
-                    jnp.where(low, left[:, LANES:], right[:, LANES:]),
-                )
-
-        def within_tiles(level):
-            stride = plan[level][1]
-            upper = row_index((TILE, 2 * LANES)) // stride % 2 == 1
-            mask = (lane_index((TILE, 2 * LANES)) % LANES < HALF) != upper
-
-            def one_tile(tile, fresh):
-                own = states[level % 2][tile].astype(F32)
-                far = jnp.where(
-                    upper, pltpu.roll(own, stride, 0), pltpu.roll(own, TILE - stride, 0)
-                )
-                pre = []
-                for order in range(2):
-                    lhs = jnp.where(mask, far, own) if order else jnp.where(mask, own, far)
-                    pltpu.matmul_acc_lhs(
-                        accumulators[order], lhs.astype(B16), load_staged_rhs=0 if fresh else None
-                    )
-                    pre.append(pltpu.matmul_pop(accumulators[order]))
-                mixed = jnp.where(mask, *pre)
-                turned(level, tile, mixed[:, :LANES], mixed[:, LANES:])
-
-            one_tile(0, True)
-
-            @pl.loop(1, 2 * half_tiles)
-            def _(tile):
-                one_tile(tile, False)
-
-        row_tiles = rows // TILE
         few = min(TILE, row_tiles)
 
         @pl.loop(0, pairs // 2 * (row_tiles // few))
         def _(item):
             duo, start = item // (row_tiles // few), item % (row_tiles // few) * few
+            base = place_of(start, 2 * duo)
             for order in range(2):
                 pltpu.matmul_push_rhs(node_maps[duo], 0, order)
                 pltpu.matmul_push_rhs(leaf_maps[2 * duo + order], 1, order)
             strips = [pl.ds(pl.multiple_of((start + i) * TILE, TILE), TILE) for i in range(few)]
-            for i, strip in enumerate(strips):
-                speeds = packed_ref[strip, 2 * LANES :]
+            for i in range(0, few, 2):
+                speeds = [packed_ref[strips[i + side], 2 * LANES :].astype(F32) for side in range(2)]
+                speeds = jnp.concatenate(
+                    [
+                        jnp.concatenate([part[: TILE // 2] for part in speeds], axis=0),
+                        jnp.concatenate([part[TILE // 2 :] for part in speeds], axis=0),
+                    ],
+                    axis=1,
+                ).astype(B16)
                 pltpu.matmul_acc_lhs(
-                    accumulators[2 * few + i],
-                    jnp.concatenate([speeds, speeds], axis=1),
-                    load_staged_rhs=0 if i < 2 else None,
+                    accumulators[2 * few + i // 2], speeds, load_staged_rhs=0 if i < 4 else None
                 )
             for i, strip in enumerate(strips):
                 for order in range(2):
@@ -323,41 +308,114 @@
                         packed_ref[strip, : 2 * LANES],
                         load_staged_rhs=1 if i == 0 else None,
                     )
-            for i in range(few):
-                turns = pltpu.matmul_pop(accumulators[2 * few + i])
+            for i in range(0, few, 2):
+                turns = pltpu.matmul_pop(accumulators[2 * few + i // 2])
                 for order in range(2):
-                    tile = (start + i) * pairs + 2 * duo + order
                     sine, cosine = sine_cosine(turns[:, order * LANES : (order + 1) * LANES])
-                    twice_ref[tile] = cosine + cosine
-                    cosines[0][tile] = cosine
-                    sines[0][tile] = sine
-                    state_a[tile] = pltpu.matmul_pop(accumulators[2 * i + order]).astype(B16)
-
-        fetches[0].wait()
-        flowing = False
-        for level in range(levels):
-            if not flowing:
-                load_maps(level)
-            if plan[level][0] == "rows":
-                within_tiles(level)
-                continue
-            if not flowing:
-                for unit in range(units):
-                    send(level, 0, unit, True)
-
+                    for side in range(2):
+                        place = base + place_of(i + side, order)
+                        state_a[place] = pltpu.matmul_pop(
+                            accumulators[2 * (i + side) + order]
+                        ).astype(B16)
+                        here = slice(side * TILE // 2, (side + 1) * TILE // 2)
+                        cosines, sines = spread(cosine[here]), spread(sine[here])
+                        twice = cosines + cosines
+                        last_cosines, last_sines = 1.0, 0.0
+                        for level in range(levels):
+                            spot = moved(base, rotations[level]) + moved(
+                                place_of(i + side, order), rotations[level]
+                            )
+                            tables[level, spot, :, :LANES] = cosines.astype(B16)
+                            tables[level, spot, :, LANES:] = sines.astype(B16)
+                            cosines, last_cosines = twice * cosines - last_cosines, cosines
+                            sines, last_sines = twice * sines - last_sines, sines
+
+        def load_maps(level):
+            for order in range(2):
+                pltpu.matmul_push_rhs(weights[2 * level + order], 0, order)
+
+        def send(state, block, unit, fresh):
+            number = block * units + unit
+            first, second = state[number], state[number + half_tiles]
+            for order in range(2):
+                pltpu.matmul_acc_lhs(
+                    accumulators[2 * unit + order],
+                    merged(second, first) if order else merged(first, second),
+                    load_staged_rhs=0 if fresh and unit == 0 else None,
+                )
+
+        def received(unit):
+            return [
+                pltpu.matmul_pop(accumulators[2 * unit + order]).astype(B16) for order in range(2)
+            ]
+
+        def finish(level, target, block, unit):
+            one, other = received(unit)
+            number = block * units + unit
+            turned(merged(one, other), level, target, number, 2 * number)
+            turned(merged(other, one), level, target, number + half_tiles, 2 * number + 1)
+
+        def across_tiles(level, source, target, next_level):
             @pl.loop(0, blocks - 1)
             def _(block):
                 for unit in range(units):
-                    finish(level, block, unit)
-                    send(level, block + 1, unit, False)
-
-            flowing = blocks > 2 and level + 1 < levels and plan[level + 1][0] == "tiles"
-            if flowing:
-                load_maps(level + 1)
+                    finish(level, target, block, unit)
+                    send(source, block + 1, unit, False)
+
+            if next_level is not None:
+                load_maps(next_level)
             for unit in range(units):
-                finish(level, blocks - 1, unit)
-                if flowing:
-                    send(level + 1, 0, unit, True)
+                finish(level, target, blocks - 1, unit)
+                if next_level is not None:
+                    send(target, 0, unit, True)
+
+        def within_tiles(level, source, target, stride):
+            upper = row_index((TILE, 2 * LANES)) // stride % 2 == 1
+            mask = (lane_index((TILE, 2 * LANES)) % LANES < HALF) != upper
+
+            def one_tile(place, fresh):
+                own = source[place].astype(F32)
+                other = jnp.where(
+                    upper, pltpu.roll(own, stride, 0), pltpu.roll(own, TILE - stride, 0)
+                )
+                pre = []
+                for order in range(2):
+                    lhs = jnp.where(mask, other, own) if order else jnp.where(mask, own, other)
+                    pltpu.matmul_acc_lhs(
+                        accumulators[order], lhs.astype(B16), load_staged_rhs=0 if fresh else None
+                    )
+                    pre.append(pltpu.matmul_pop(accumulators[order]))
+                turned(jnp.where(mask, *pre).astype(B16), level, target, place, place)
+
+            one_tile(0, True)
+
+            @pl.loop(1, 2 * half_tiles)
+            def _(place):
+                one_tile(place, False)
+
+        fetches[0].wait()
+        if levels % 2 == 0 and blocks > 3 and all(kind == "tiles" for kind, _ in plan):
+            load_maps(0)
+            for unit in range(units):
+                send(state_a, 0, unit, True)
+
+            @pl.loop(0, levels // 2)
+            def _(two):
+                across_tiles(2 * two, state_a, state_b, 2 * two + 1)
+                across_tiles(2 * two + 1, state_b, state_a, jnp.minimum(2 * two + 2, levels - 1))
+
+            for unit in range(units):
+                received(unit)
+        else:
+            for level, (kind, stride) in enumerate(plan):
+                source, target = states[level % 2], states[1 - level % 2]
+                load_maps(level)
+                if kind == "rows":
+                    within_tiles(level, source, target, stride)
+                    continue
+                for unit in range(units):
+                    send(source, 0, unit, True)
+                across_tiles(level, source, target, None)
 
         fetches[1].wait()
         final = states[levels % 2]
@@ -369,7 +427,7 @@
                 for order in range(2):
                     pltpu.matmul_acc_lhs(
                         accumulators[2 * i + order],
-                        final[(order * share + i) * pairs + pair],
+                        final[place_of(order * share + i, pair)],
                         load_staged_rhs=pair % 2 if i == 0 else None,
                     )
         for i in range(share):
@@ -385,9 +443,9 @@
 
 
 def split_nodes(rank):
-    nodes = np.cos(np.pi * (np.arange(rank) + 0.5) / rank) / 2
+    nodes = np.cos(np.pi * (np.arange(QUARTER) + 0.5) / rank) / 2
     pieces = []
-    rest = np.tile(nodes, LANES // rank)
+    rest = np.tile(nodes, LANES // QUARTER)
     for _ in range(3):
         piece = rest.astype(B16)
         pieces.append(piece.astype(np.float32))
@@ -446,7 +504,6 @@
 
     tiles = rows // TILE * pairs
     state = pltpu.VMEM((tiles, TILE, 2 * LANES), B16)
-    table = pltpu.VMEM((tiles, TILE, LANES), F32)
     values = pl.pallas_call(
         functools.partial(butterfly_kernel, level_plan(levels, local_levels, rows_per), leaf, pairs),
         out_shape=jax.ShapeDtypeStruct((rows, 2 * LANES), B16),
@@ -459,8 +516,8 @@
             pltpu.SemaphoreType.DMA((2,)),
             state,
             state,
-        ]
-        + [table] * 7,
+            pltpu.VMEM((levels, tiles, TILE, 2 * LANES), B16),
+        ],
         compiler_params=vmem(40),
         name="butterfly",
     )(packed, leaf_weight, jnp.asarray(split_nodes(width // 2)), weights)

time: 54 us -> 51.7 us (0.957)
  waiting for transfers between devices: 7.58 us -> 5.13 us
    pallas_call x1, Pallas kernels: 4.2 us -> 6.65 us  [on_device(): pl.pallas_call(functools.partial(maps_kernel, leaf), grid=(1,), out_specs...]
    all_to_all x1, waiting for transfers between devices: 7.58 us -> 5.13 us  [on_device(): lax.all_to_all(packed.reshape(devices, rows_per, 3 * LANES), AXES, 0, 0,...]
    pallas_call x1, Pallas kernels: 15 us -> 12.8 us  [on_device(): pl.pallas_call(functools.partial(butterfly_kernel, level_plan(levels, loc...]
  transfers between devices with their start and end apart: 1 -> 1, of which waited for: 1 -> 1; matrix products, arithmetic and copies ran while one was open for 3% -> 3% of each run, Pallas kernels for 8% -> 13%
where the time goes in v5:
time: 51.7 us; the launch traced here: 51.4 us
  Pallas kernels  24.6 us (48%)
  blocking collectives  13 us (25%)
  starting transfers between devices  7.3 us (14%)
  waiting for transfers between devices  5.13 us (10%)
  local copies, waits for them, and re-layouts  1.41 us (3%)
    all_to_all x1, blocking collectives, on_device(): lax.all_to_all(values.reshape(devices, rows_per, 2 * LANES), AXES, 0, 0,...  13 us
    pallas_call x1, Pallas kernels, on_device(): pl.pallas_call(functools.partial(butterfly_kernel, level_plan(levels, loc...  12.8 us
    all_to_all x1, starting transfers between devices, on_device(): lax.all_to_all(packed.reshape(devices, rows_per, 3 * LANES), AXES, 0, 0,...  7.3 us
    pallas_call x1, Pallas kernels, on_device(): pl.pallas_call(functools.partial(maps_kernel, leaf), grid=(1,), out_specs...  6.65 us
    all_to_all x1, waiting for transfers between devices, on_device(): lax.all_to_all(packed.reshape(devices, rows_per, 3 * LANES), AXES, 0, 0,...  5.13 us
    pallas_call x1, Pallas kernels, on_device(): pl.pallas_call(functools.partial(pack_kernel, leaf), out_shape=jax.ShapeD...  3.61 us
    pallas_call x1, Pallas kernels, on_device(): pl.pallas_call(functools.partial(unpack_kernel, leaf), out_shape=jax.Shap...  1.53 us
    unnamed x7, local copies, waits for them, and re-layouts  1.41 us
  transfers between devices with their start and end apart: 1, of which 1 were waited for; matrix products, arithmetic and copies ran while one was open for 3% of the time, Pallas kernels for 13%

profile of v5, /device:TPU:0, one launch (start us, length us, event | category | flops | bytes accessed | tf_op | source)
XLA Modules:
  0.0 51.4 jit_solution(14536581813773938153)
XLA Ops:
  0.0 0.0 copy-start.2
  0.0 0.0 copy-start.1
  0.0 3.6 %pack.1 = bf16[512,384]{1,0:T(8,128)(2,1)} custom-call(f32[1024,128]{1,0:T(8,128)} %bitcast.22, s32[512,128]{1,0:T(8,128)} %bitcast.23, bf16[64,128]{1,0:T(8,128)(2,1)} %bitcast.24), custom_call_target="tpu_custom_call" | custom-call | tf_op jit(solution)/shard_map/pack/pallas_call | solution.py:482
  3.6 7.3 %all-to-all-start = ((bf16[32,16,384]{2,1,0:T(8,128)(2,1)}), bf16[32,16,384]{2,1,0:T(8,128)(2,1)S(1)}, u32[]{:S(2)}, u32[]{:S(2)}) async-start(bf16[32,16,384]{2,1,0:T(8,128)(2,1)} %bitcast.21), calls=%async_computation | async-start | bytes 786432 | tf_op jit(solution)/shard_map/all_to_all | solution.py:489
  10.9 1.4 %copy.10.eval_ref = bf16[128,16]{1,0:T(8,128)(2,1)} copy(bf16[128,16]{0,1:T(8,128)(2,1)} %param.13) | data formatting | bytes 8192 | tf_op args[5]
  12.3 0.0 copy-start
  12.3 6.6 %maps.1.weights_ref = bf16[200,256,256]{2,1,0:T(8,128)(2,1)} custom-call(bf16[8,2,2,128,128]{4,3,2,1,0:T(8,128)(2,1)} %mixing_ref.1, bf16[128,16]{1,0:T(8,128)(2,1)} %copy.10.eval_ref), custom_call_target="tpu_custom_call" | custom-call | flops 1000000000 | bytes 10000000 | tf_op jit(solution)/shard_map/maps/pallas_call | solution.py:495
  19.0 5.1 %all-to-all-done = bf16[32,16,384]{2,1,0:T(8,128)(2,1)S(1)} async-done(((bf16[32,16,384]{2,1,0:T(8,128)(2,1)}), bf16[32,16,384]{2,1,0:T(8,128)(2,1)S(1)}, u32[]{:S(2)}, u32[]{:S(2)}) %all-to-all-start) | async-done | bytes 393248 | tf_op jit(solution)/shard_map/all_to_all | solution.py:489
  24.1 0.0 copy-done.2
  24.1 0.0 copy-done.1
  24.1 12.8 %butterfly.1 = bf16[512,256]{1,0:T(8,128)(2,1)S(1)} custom-call(bf16[512,384]{1,0:T(8,128)(2,1)S(1)} %bitcast.17, bf16[16,128]{1,0:T(8,128)(2,1)S(1)} %copy-done.1, f32[3,128]{1,0:T(4,128)S(1)} %copy-done.2, bf16[200,256,256]{2,1,0:T(8,128)(2,1)} %maps.1.weights_ref), custom_call_target="tpu_custom_call" | custom-call | tf_op jit(solution)/shard_map/butterfly/pallas_call | solution.py:507
  36.9 13.0 %all_to_all.10 = bf16[32,16,256]{2,1,0:T(8,128)(2,1)S(1)} all-to-all(bf16[32,16,256]{2,1,0:T(8,128)(2,1)S(1)} %bitcast.18), channel_id=1, replica_groups=mesh['wide'=8,'narrow'=4] {'wide','narrow'}, dimensions={0} | all-to-all | bytes 524288 | tf_op jit(solution)/shard_map/all_to_all | solution.py:525
  49.9 0.0 copy-done
  49.9 1.5 %unpack.1 = f32[1024,128]{1,0:T(8,128)} custom-call(bf16[512,256]{1,0:T(8,128)(2,1)S(1)} %bitcast.19, s32[512,128]{1,0:T(8,128)S(1)} %bitcast.20), custom_call_target="tpu_custom_call" | custom-call | tf_op jit(solution)/shard_map/unpack/pallas_call | solution.py:529
Async XLA Ops:
  0.0 24.1 %copy-start.2 = (f32[3,128]{1,0:T(4,128)S(1)}, f32[3,128]{1,0:T(4,128)}, u32[]{:S(2)}) copy-start(f32[3,128]{1,0:T(4,128)} %constant.2.clone.nodes_ref) | copy-start | bytes 4612
  0.0 24.1 %copy-start.1 = (bf16[16,128]{1,0:T(8,128)(2,1)S(1)}, bf16[16,128]{1,0:T(8,128)(2,1)}, u32[]{:S(2)}) copy-start(bf16[16,128]{1,0:T(8,128)(2,1)} %leaf_ref.1) | copy-start | bytes 12292
  3.6 20.5 %all-to-all-start = ((bf16[32,16,384]{2,1,0:T(8,128)(2,1)}), bf16[32,16,384]{2,1,0:T(8,128)(2,1)S(1)}, u32[]{:S(2)}, u32[]{:S(2)}) async-start(bf16[32,16,384]{2,1,0:T(8,128)(2,1)} %bitcast.21), calls=%async_computation | async-start | bytes 786432 | tf_op jit(solution)/shard_map/all_to_all | solution.py:489
  12.3 37.6 %copy-start = (s32[65536]{0:T(1024)S(1)}, s32[65536]{0:T(1024)}, u32[]{:S(2)}) copy-start(s32[65536]{0:T(1024)} %param.14) | copy-start | bytes 786436

commit v6 on v5

--- a/solution.py
+++ b/solution.py
@@ -21,6 +21,9 @@
     return pltpu.CompilerParams(vmem_limit_bytes=mebibytes * 2**20)
 
 
+STRIPS = 4
+
+
 def lane_index(shape):
     return lax.broadcasted_iota(jnp.int32, shape, len(shape) - 1)
 
@@ -43,52 +46,80 @@
     return lax.axis_index("wide") * lax.axis_size("narrow") + lax.axis_index("narrow")
 
 
-def pack_kernel(leaf, charges_ref, order_ref, velocity_ref, out_ref):
+def pack_kernel(
+    leaf, charges_hbm, order_hbm, velocity_hbm, out_hbm,
+    charges_ref, order_ref, velocity_ref, out_ref, arrived, gone,
+):
     rows = order_ref.shape[0]
+    strip = rows // STRIPS
+    group = LANES // leaf
+    pairs = ((charges_hbm, charges_ref), (order_hbm, order_ref), (velocity_hbm, velocity_ref))
+
+    def part(ref, number):
+        height = ref.shape[0] // STRIPS
+        return ref.at[number * height : (number + 1) * height]
+
+    fetches = [
+        [
+            pltpu.make_async_copy(part(far, number), part(near, number), arrived.at[number, kind])
+            for kind, (far, near) in enumerate(pairs)
+        ]
+        for number in range(STRIPS)
+    ]
+    stores = [
+        pltpu.make_async_copy(part(out_ref, number), part(out_hbm, number), gone.at[number])
+        for number in range(STRIPS)
+    ]
+    for fetch in sum(fetches, []):
+        fetch.start()
     odd = odd_bits(device_number()) == 1
-    step = min(rows, 64)
-    lanes = lane_index((step, LANES))
-    group = LANES // leaf
-
-    @pl.loop(0, rows // step)
-    def _(block):
-        here = pl.ds(pl.multiple_of(block * step, step), step)
+    lanes = lane_index((strip, LANES))
+    own = lanes // group == row_index((strip, LANES)) % leaf
+    speed_lanes = lane_index((strip // leaf, LANES)) ^ jnp.where(odd, group // 2, 0)
+    for number in range(STRIPS):
+        for fetch in fetches[number]:
+            fetch.wait()
+        here = slice(number * strip, (number + 1) * strip)
         index = order_ref[here, :] + lanes // leaf * leaf
-        for part in range(2):
-            values = charges_ref[pl.ds(block * (2 * step) + part, step, stride=2), :]
+        for half in range(2):
+            values = charges_ref[pl.ds(2 * number * strip + half, strip, stride=2), :]
             values = jnp.take_along_axis(values, index, axis=1)
             values = jnp.where(odd, swapped(values), values)
-            out_ref[here, part * LANES : (part + 1) * LANES] = values.astype(B16)
-
-    speeds = velocity_ref[...].astype(F32)
-    lanes = lane_index(speeds.shape)
-    speeds = jnp.take_along_axis(speeds, lanes ^ jnp.where(odd, group // 2, 0), axis=1)
-    count = speeds.shape[0]
-    speeds = jnp.broadcast_to(speeds[:, None, :], (count, leaf, LANES)).reshape(rows, LANES)
-    own = lane_index(speeds.shape) // group == row_index(speeds.shape) % leaf
-    speeds = jnp.where(own, speeds, 0.0)
-    shift = group
-    while shift < LANES:
-        speeds = speeds + pltpu.roll(speeds, shift, 1)
-        shift *= 2
-    out_ref[:, 2 * LANES :] = speeds.astype(B16)
-
-
-def unpack_kernel(leaf, values_ref, order_ref, out_ref):
+            out_ref[here, half * LANES : (half + 1) * LANES] = values.astype(B16)
+        top = number * strip // leaf
+        speeds = velocity_ref[top : top + strip // leaf, :].astype(F32)
+        speeds = jnp.take_along_axis(speeds, speed_lanes, axis=1)
+        speeds = jnp.broadcast_to(speeds[:, None, :], (strip // leaf, leaf, LANES))
+        speeds = jnp.where(own, speeds.reshape(strip, LANES), 0.0)
+        shift = group
+        while shift < LANES:
+            speeds = speeds + pltpu.roll(speeds, shift, 1)
+            shift *= 2
+        out_ref[here, 2 * LANES :] = speeds.astype(B16)
+        stores[number].start()
+    for store in stores:
+        store.wait()
+
+
+def unpack_kernel(leaf, values_ref, order_ref, out_hbm, out_ref, gone):
     rows = order_ref.shape[0]
+    strip = rows // STRIPS
     odd = odd_bits(device_number()) == 1
-    step = min(rows, 64)
-    base = lane_index((step, LANES)) // leaf * leaf ^ jnp.where(odd, HALF, 0)
-
-    @pl.loop(0, rows // step)
-    def _(block):
-        here = pl.ds(pl.multiple_of(block * step, step), step)
+    base = lane_index((strip, LANES)) // leaf * leaf ^ jnp.where(odd, HALF, 0)
+    stores = []
+    for number in range(STRIPS):
+        here = slice(number * strip, (number + 1) * strip)
         index = order_ref[here, :] + base
-        for part in range(2):
-            values = values_ref[here, part * LANES : (part + 1) * LANES].astype(F32)
-            out_ref[pl.ds(block * (2 * step) + part, step, stride=2), :] = jnp.take_along_axis(
+        for half in range(2):
+            values = values_ref[here, half * LANES : (half + 1) * LANES].astype(F32)
+            out_ref[pl.ds(2 * number * strip + half, strip, stride=2), :] = jnp.take_along_axis(
                 values, index, axis=1
             )
+        wide = slice(2 * number * strip, 2 * (number + 1) * strip)
+        stores.append(pltpu.make_async_copy(out_ref.at[wide], out_hbm.at[wide], gone.at[number]))
+        stores[-1].start()
+    for store in stores:
+        store.wait()
 
 
 def odd_pair(pair):
@@ -281,26 +312,42 @@
     def run(*accumulators):
         few = min(TILE, row_tiles)
 
-        @pl.loop(0, pairs // 2 * (row_tiles // few))
+        rounds = row_tiles // few
+
+        def strip_of(item, i):
+            return pl.ds(pl.multiple_of((item % rounds * few + i) * TILE, TILE), TILE)
+
+        def push_nodes(item):
+            for order in range(2):
+                pltpu.matmul_push_rhs(node_maps[item // rounds], 0, order)
+
+        def send_speeds(item, i):
+            speeds = [packed_ref[strip_of(item, i + side), 2 * LANES :] for side in range(2)]
+            speeds = [part.astype(F32) for part in speeds]
+            speeds = jnp.concatenate(
+                [
+                    jnp.concatenate([part[: TILE // 2] for part in speeds], axis=0),
+                    jnp.concatenate([part[TILE // 2 :] for part in speeds], axis=0),
+                ],
+                axis=1,
+            ).astype(B16)
+            pltpu.matmul_acc_lhs(
+                accumulators[2 * few + i // 2], speeds, load_staged_rhs=0 if i < 4 else None
+            )
+
+        items = pairs // 2 * rounds
+        push_nodes(0)
+        for i in range(0, few, 2):
+            send_speeds(0, i)
+
+        @pl.loop(0, items)
         def _(item):
-            duo, start = item // (row_tiles // few), item % (row_tiles // few) * few
+            duo, start = item // rounds, item % rounds * few
             base = place_of(start, 2 * duo)
+            coming = jnp.minimum(item + 1, items - 1)
             for order in range(2):
-                pltpu.matmul_push_rhs(node_maps[duo], 0, order)
                 pltpu.matmul_push_rhs(leaf_maps[2 * duo + order], 1, order)
-            strips = [pl.ds(pl.multiple_of((start + i) * TILE, TILE), TILE) for i in range(few)]
-            for i in range(0, few, 2):
-                speeds = [packed_ref[strips[i + side], 2 * LANES :].astype(F32) for side in range(2)]
-                speeds = jnp.concatenate(
-                    [
-                        jnp.concatenate([part[: TILE // 2] for part in speeds], axis=0),
-                        jnp.concatenate([part[TILE // 2 :] for part in speeds], axis=0),
-                    ],
-                    axis=1,
-                ).astype(B16)
-                pltpu.matmul_acc_lhs(
-                    accumulators[2 * few + i // 2], speeds, load_staged_rhs=0 if i < 4 else None
-                )
+            strips = [strip_of(item, i) for i in range(few)]
             for i, strip in enumerate(strips):
                 for order in range(2):
                     pltpu.matmul_acc_lhs(
@@ -308,8 +355,10 @@
                         packed_ref[strip, : 2 * LANES],
                         load_staged_rhs=1 if i == 0 else None,
                     )
+            push_nodes(coming)
             for i in range(0, few, 2):
                 turns = pltpu.matmul_pop(accumulators[2 * few + i // 2])
+                send_speeds(coming, i)
                 for order in range(2):
                     sine, cosine = sine_cosine(turns[:, order * LANES : (order + 1) * LANES])
                     for side in range(2):
@@ -330,6 +379,9 @@
                             cosines, last_cosines = twice * cosines - last_cosines, cosines
                             sines, last_sines = twice * sines - last_sines, sines
 
+        for i in range(0, few, 2):
+            pltpu.matmul_pop(accumulators[2 * few + i // 2])
+
         def load_maps(level):
             for order in range(2):
                 pltpu.matmul_push_rhs(weights[2 * level + order], 0, order)
@@ -479,9 +531,20 @@
     assert width == LANES and 1 << local_levels == pairs
 
     charge_rows = charges.reshape(2, rows, LANES).transpose(1, 0, 2).reshape(2 * rows, LANES)
+    in_hbm = pl.BlockSpec(memory_space=pltpu.HBM)
     packed = pl.pallas_call(
         functools.partial(pack_kernel, leaf),
+        in_specs=[in_hbm] * 3,
+        out_specs=in_hbm,
         out_shape=jax.ShapeDtypeStruct((rows, 3 * LANES), B16),
+        scratch_shapes=[
+            pltpu.VMEM((2 * rows, LANES), F32),
+            pltpu.VMEM((rows, LANES), jnp.int32),
+            pltpu.VMEM((boxes // LANES, LANES), B16),
+            pltpu.VMEM((rows, 3 * LANES), B16),
+            pltpu.SemaphoreType.DMA((STRIPS, 3)),
+            pltpu.SemaphoreType.DMA((STRIPS,)),
+        ],
         compiler_params=vmem(56),
         name="pack",
     )(charge_rows, source_order.reshape(rows, LANES), velocity.reshape(boxes // LANES, LANES))
@@ -508,7 +571,7 @@
         functools.partial(butterfly_kernel, level_plan(levels, local_levels, rows_per), leaf, pairs),
         out_shape=jax.ShapeDtypeStruct((rows, 2 * LANES), B16),
         in_specs=[pl.BlockSpec(memory_space=pltpu.VMEM)] * 3
-        + [pl.BlockSpec(memory_space=pltpu.HBM)],
+        + [in_hbm],
         scratch_shapes=[
             pltpu.VMEM((pairs, *square), B16),
             pltpu.VMEM((pairs // 2, *square), B16),
@@ -528,7 +591,9 @@
 
     out = pl.pallas_call(
         functools.partial(unpack_kernel, leaf),
+        out_specs=in_hbm,
         out_shape=jax.ShapeDtypeStruct((2 * rows, LANES), F32),
+        scratch_shapes=[pltpu.VMEM((2 * rows, LANES), F32), pltpu.SemaphoreType.DMA((STRIPS,))],
         compiler_params=vmem(8),
         name="unpack",
     )(values, target_order.reshape(rows, LANES))

time: 51.7 us -> 50.8 us (0.983)
  Pallas kernels: 24.6 us -> 23.7 us
    pallas_call x2, Pallas kernels: 5.14 us -> 3.98 us  [the longest x1 3.03 us: on_device(): pl.pallas_call(functools.partial(pack_kernel, leaf), in_specs=[in_hbm] *...]
where the time goes in v6:
time: 50.8 us; the launch traced here: 50.6 us
  Pallas kernels  23.7 us (47%)
  blocking collectives  13 us (26%)
  starting transfers between devices  7.3 us (14%)
  waiting for transfers between devices  5.13 us (10%)
  local copies, waits for them, and re-layouts  1.41 us (3%)
    all_to_all x1, blocking collectives, on_device(): lax.all_to_all(values.reshape(devices, rows_per, 2 * LANES), AXES, 0, 0,...  13 us
    pallas_call x1, Pallas kernels, on_device(): pl.pallas_call(functools.partial(butterfly_kernel, level_plan(levels, loc...  13 us
    all_to_all x1, starting transfers between devices, on_device(): lax.all_to_all(packed.reshape(devices, rows_per, 3 * LANES), AXES, 0, 0,...  7.3 us
    pallas_call x1, Pallas kernels, on_device(): pl.pallas_call(functools.partial(maps_kernel, leaf), grid=(1,), out_specs...  6.65 us
    all_to_all x1, waiting for transfers between devices, on_device(): lax.all_to_all(packed.reshape(devices, rows_per, 3 * LANES), AXES, 0, 0,...  5.13 us
    pallas_call x1, Pallas kernels, on_device(): pl.pallas_call(functools.partial(pack_kernel, leaf), in_specs=[in_hbm] *...  3.03 us
    unnamed x7, local copies, waits for them, and re-layouts  1.41 us
  transfers between devices with their start and end apart: 1, of which 1 were waited for; matrix products, arithmetic and copies ran while one was open for 3% of the time, Pallas kernels for 13%

profile of v6, /device:TPU:0, one launch (start us, length us, event | category | flops | bytes accessed | tf_op | source)
XLA Modules:
  0.0 50.6 jit_solution(15353785470743192797)
XLA Ops:
  0.0 0.0 copy-start.2
  0.0 0.0 copy-start.1
  0.0 3.0 %pack.1 = bf16[512,384]{1,0:T(8,128)(2,1)} custom-call(f32[1024,128]{1,0:T(8,128)} %bitcast.22, s32[512,128]{1,0:T(8,128)} %bitcast.23, bf16[64,128]{1,0:T(8,128)(2,1)} %bitcast.24), custom_call_target="tpu_custom_call" | custom-call | tf_op jit(solution)/shard_map/pack/pallas_call | solution.py:535
  3.0 7.3 %all-to-all-start = ((bf16[32,16,384]{2,1,0:T(8,128)(2,1)}), bf16[32,16,384]{2,1,0:T(8,128)(2,1)S(1)}, u32[]{:S(2)}, u32[]{:S(2)}) async-start(bf16[32,16,384]{2,1,0:T(8,128)(2,1)} %bitcast.21), calls=%async_computation | async-start | bytes 786432 | tf_op jit(solution)/shard_map/all_to_all | solution.py:552
  10.3 1.4 %copy.10.eval_ref = bf16[128,16]{1,0:T(8,128)(2,1)} copy(bf16[128,16]{0,1:T(8,128)(2,1)} %param.13) | data formatting | bytes 8192 | tf_op args[5]
  11.7 0.0 copy-start
  11.8 6.6 %maps.1.weights_ref = bf16[200,256,256]{2,1,0:T(8,128)(2,1)} custom-call(bf16[8,2,2,128,128]{4,3,2,1,0:T(8,128)(2,1)} %mixing_ref.1, bf16[128,16]{1,0:T(8,128)(2,1)} %copy.10.eval_ref), custom_call_target="tpu_custom_call" | custom-call | flops 1000000000 | bytes 10000000 | tf_op jit(solution)/shard_map/maps/pallas_call | solution.py:558
  18.4 5.1 %all-to-all-done = bf16[32,16,384]{2,1,0:T(8,128)(2,1)S(1)} async-done(((bf16[32,16,384]{2,1,0:T(8,128)(2,1)}), bf16[32,16,384]{2,1,0:T(8,128)(2,1)S(1)}, u32[]{:S(2)}, u32[]{:S(2)}) %all-to-all-start) | async-done | bytes 393248 | tf_op jit(solution)/shard_map/all_to_all | solution.py:552
  23.5 0.0 copy-done.2
  23.5 0.0 copy-done.1
  23.5 13.0 %butterfly.1 = bf16[512,256]{1,0:T(8,128)(2,1)S(1)} custom-call(bf16[512,384]{1,0:T(8,128)(2,1)S(1)} %bitcast.17, bf16[16,128]{1,0:T(8,128)(2,1)S(1)} %copy-done.1, f32[3,128]{1,0:T(4,128)S(1)} %copy-done.2, bf16[200,256,256]{2,1,0:T(8,128)(2,1)} %maps.1.weights_ref), custom_call_target="tpu_custom_call" | custom-call | tf_op jit(solution)/shard_map/butterfly/pallas_call | solution.py:570
  36.6 13.0 %all_to_all.10 = bf16[32,16,256]{2,1,0:T(8,128)(2,1)S(1)} all-to-all(bf16[32,16,256]{2,1,0:T(8,128)(2,1)S(1)} %bitcast.18), channel_id=1, replica_groups=mesh['wide'=8,'narrow'=4] {'wide','narrow'}, dimensions={0} | all-to-all | bytes 524288 | tf_op jit(solution)/shard_map/all_to_all | solution.py:588
  49.6 0.0 copy-done
  49.6 1.0 %unpack.1 = f32[1024,128]{1,0:T(8,128)} custom-call(bf16[512,256]{1,0:T(8,128)(2,1)S(1)} %bitcast.19, s32[512,128]{1,0:T(8,128)S(1)} %bitcast.20), custom_call_target="tpu_custom_call" | custom-call | tf_op jit(solution)/shard_map/unpack/pallas_call | solution.py:592
Async XLA Ops:
  0.0 23.5 %copy-start.2 = (f32[3,128]{1,0:T(4,128)S(1)}, f32[3,128]{1,0:T(4,128)}, u32[]{:S(2)}) copy-start(f32[3,128]{1,0:T(4,128)} %constant.2.clone.nodes_ref) | copy-start | bytes 4612
  0.0 23.5 %copy-start.1 = (bf16[16,128]{1,0:T(8,128)(2,1)S(1)}, bf16[16,128]{1,0:T(8,128)(2,1)}, u32[]{:S(2)}) copy-start(bf16[16,128]{1,0:T(8,128)(2,1)} %leaf_ref.1) | copy-start | bytes 12292
  3.0 20.5 %all-to-all-start = ((bf16[32,16,384]{2,1,0:T(8,128)(2,1)}), bf16[32,16,384]{2,1,0:T(8,128)(2,1)S(1)}, u32[]{:S(2)}, u32[]{:S(2)}) async-start(bf16[32,16,384]{2,1,0:T(8,128)(2,1)} %bitcast.21), calls=%async_computation | async-start | bytes 786432 | tf_op jit(solution)/shard_map/all_to_all | solution.py:552
  11.7 37.9 %copy-start = (s32[65536]{0:T(1024)S(1)}, s32[65536]{0:T(1024)}, u32[]{:S(2)}) copy-start(s32[65536]{0:T(1024)} %param.14) | copy-start | bytes 786436

commit v7 on v6

--- a/solution.py
+++ b/solution.py
@@ -36,6 +36,13 @@
     return pltpu.roll(x, HALF, 1)
 
 
+def repeated(x, group):
+    while group < LANES:
+        x = x + pltpu.roll(x, group, 1)
+        group *= 2
+    return x
+
+
 def odd_bits(number):
     for shift in (16, 8, 4, 2, 1):
         number = number ^ lax.shift_right_logical(number, shift)
@@ -50,6 +57,7 @@
     leaf, charges_hbm, order_hbm, velocity_hbm, out_hbm,
     charges_ref, order_ref, velocity_ref, out_ref, arrived, gone,
 ):
+    slabs = len(out_ref.shape) == 3
     rows = order_ref.shape[0]
     strip = rows // STRIPS
     group = LANES // leaf
@@ -84,18 +92,30 @@
         for half in range(2):
             values = charges_ref[pl.ds(2 * number * strip + half, strip, stride=2), :]
             values = jnp.take_along_axis(values, index, axis=1)
-            values = jnp.where(odd, swapped(values), values)
-            out_ref[here, half * LANES : (half + 1) * LANES] = values.astype(B16)
+            values = jnp.where(odd, swapped(values), values).astype(B16)
+            if slabs:
+                for slab in range(strip // TILE):
+                    out_ref[number * (strip // TILE) + slab, half * TILE : (half + 1) * TILE, :] = (
+                        values[slab * TILE : (slab + 1) * TILE]
+                    )
+            else:
+                out_ref[here, half * LANES : (half + 1) * LANES] = values
         top = number * strip // leaf
         speeds = velocity_ref[top : top + strip // leaf, :].astype(F32)
         speeds = jnp.take_along_axis(speeds, speed_lanes, axis=1)
-        speeds = jnp.broadcast_to(speeds[:, None, :], (strip // leaf, leaf, LANES))
-        speeds = jnp.where(own, speeds.reshape(strip, LANES), 0.0)
-        shift = group
-        while shift < LANES:
-            speeds = speeds + pltpu.roll(speeds, shift, 1)
-            shift *= 2
-        out_ref[here, 2 * LANES :] = speeds.astype(B16)
+        if slabs:
+            for slab in range(strip // TILE):
+                first = slab * TILE // leaf
+                own_rows = speeds[first // 8 * 8 : first // 8 * 8 + 8]
+                if first % 8:
+                    own_rows = pltpu.roll(own_rows, 8 - first % 8, 0)
+                out_ref[number * (strip // TILE) + slab, 2 * TILE :, :] = jnp.where(
+                    row_index((8, LANES)) < TILE // leaf, own_rows, 0.0
+                ).astype(B16)
+        else:
+            speeds = jnp.broadcast_to(speeds[:, None, :], (strip // leaf, leaf, LANES))
+            speeds = jnp.where(own, speeds.reshape(strip, LANES), 0.0)
+            out_ref[here, 2 * LANES :] = repeated(speeds, group).astype(B16)
         stores[number].start()
     for store in stores:
         store.wait()
@@ -151,14 +171,21 @@
         lane_index(shape) == mirrored(row_index(shape)), sign_of(row_index(shape)), 0.0
     ).astype(B16)
 
-    def mirrored_map(matrix):
-        matrix = jnp.dot(matrix, mirror, preferred_element_type=F32).astype(B16)
-        return jnp.dot(mirror_back, matrix, preferred_element_type=F32)
+    order_of_four = [(target, source) for target in range(2) for source in range(2)]
 
     @pl.loop(0, levels)
     def _(level):
+        four = jnp.concatenate([mixing_ref[level, *place] for place in order_of_four], axis=0)
+        four = jnp.dot(four, mirror, preferred_element_type=F32).astype(B16)
+        four = jnp.concatenate(
+            [four[number * LANES : (number + 1) * LANES] for number in range(4)], axis=1
+        )
+        four = jnp.dot(mirror_back, four, preferred_element_type=F32)
         for source in range(2):
-            both = [mirrored_map(mixing_ref[level, target, source]) for target in range(2)]
+            both = [
+                four[:, (2 * target + source) * LANES : (2 * target + source + 1) * LANES]
+                for target in range(2)
+            ]
             for part in range(2):
                 to_first, to_second = (
                     matrix[part * HALF : (part + 1) * HALF] for matrix in both
@@ -179,8 +206,10 @@
     box_of_lane = lane_index((HALF, LANES)) // leaf
     slot = lane_index((2 * leaf, 2 * LANES))
     spread = (slot // LANES * leaf + slot % leaf == row_index((2 * leaf, 2 * LANES))).astype(B16)
-    eval_rows = jnp.dot(mirror_back, eval_ref[...], preferred_element_type=F32).astype(B16)
-    eval_rows = jnp.dot(eval_rows, spread, preferred_element_type=F32)
+    eval_rows = lax.dot_general(
+        eval_ref[...], spread, (((0,), (0,)), ((), ())), preferred_element_type=F32
+    ).astype(B16)
+    eval_rows = jnp.dot(mirror_back, eval_rows, preferred_element_type=F32)
     for pair in range(pairs):
         for number, box in enumerate(boxes_of_pair(pair, pairs)):
             for part in range(2):
@@ -206,14 +235,23 @@
     nodes = jnp.zeros(shape, F32)
     for piece in range(3):
         nodes = jnp.where(node_row // group == piece, nodes_ref[piece : piece + 1, :], nodes)
-    for part in range(2):
-        tiled = jnp.broadcast_to(
+    tiles = [
+        jnp.broadcast_to(
             leaf_rows[part * leaf : (part + 1) * leaf][None], (group, leaf, LANES)
         ).reshape(shape)
-        far = swapped(tiled)
-        here = slice(part * LANES, (part + 1) * LANES)
-        for pair in range(pairs):
-            left, right = boxes_of_pair(pair, pairs)
+        for part in range(2)
+    ]
+
+    @pl.loop(0, pairs)
+    def _(pair):
+        odd = odd_bits(pair) == 1
+        left = pair + jnp.where(odd, pairs, 0)
+        right = pair + jnp.where(odd, 0, pairs)
+        mine = node_row % group == jnp.where(in_left, left, right)
+        for part in range(2):
+            tiled = tiles[part]
+            far = swapped(tiled)
+            here = slice(part * LANES, (part + 1) * LANES)
             first, second = box_of_row == left, box_of_row == right
             leaf_maps[pair, here, :LANES] = jnp.where(
                 low, jnp.where(first, tiled, 0.0), jnp.where(second, far, 0.0)
@@ -221,18 +259,16 @@
             leaf_maps[pair, here, LANES:] = jnp.where(
                 low, jnp.where(first, far, 0.0), jnp.where(second, tiled, 0.0)
             ).astype(B16)
-            lanes = slice(pair % 2 * LANES, (pair % 2 + 1) * LANES)
-            mine = (node_row % group == jnp.where(in_left, left, right)) & (
-                lane_index(shape) // HALF == part
-            )
-            node_maps[pair // 2, here, lanes] = jnp.where(mine, nodes, 0.0).astype(B16)
+            node_maps[pair, here, :] = jnp.where(
+                mine & (lane_index(shape) // HALF == part), nodes, 0.0
+            ).astype(B16)
 
 
 def sine_cosine(turns):
     u = turns - jnp.round(turns)
     w = u * u
-    sin_terms = [(-1) ** i * math.pi ** (2 * i + 1) / math.factorial(2 * i + 1) for i in range(7)]
-    cos_terms = [(-1) ** i * math.pi ** (2 * i) / math.factorial(2 * i) for i in range(7)]
+    sin_terms = [(-1) ** i * math.pi ** (2 * i + 1) / math.factorial(2 * i + 1) for i in range(6)]
+    cos_terms = [(-1) ** i * math.pi ** (2 * i) / math.factorial(2 * i) for i in range(6)]
     half_sin = jnp.full_like(w, sin_terms[-1])
     for term in sin_terms[-2::-1]:
         half_sin = half_sin * w + term
@@ -250,15 +286,16 @@
 
 def butterfly_kernel(
     plan, leaf, pairs, packed_ref, leaf_ref, nodes_ref, weights_ref, out_ref,
-    leaf_maps, node_maps, weights, arrived, state_a, state_b, tables,
+    leaf_maps, node_maps, weights, arrived, states_ref, tables, speeds_ref,
 ):
-    rows = packed_ref.shape[0]
+    slabs = len(packed_ref.shape) == 3
+    rows = packed_ref.shape[0] * (TILE if slabs else 1)
     levels = len(plan)
-    states = (state_a, state_b)
+    states = pltpu.annotate(states_ref, no_hazard_no_deps=True)
     rotations = [sum(kind == "tiles" for kind, _ in plan[:level]) for level in range(levels)]
     row_tiles = rows // TILE
     row_bits, pair_bits = row_tiles.bit_length() - 1, pairs.bit_length() - 1
-    half_tiles = state_a.shape[0] // 2
+    half_tiles = states_ref.shape[1] // 2
     units = min(UNITS, half_tiles)
     blocks = half_tiles // units
     index_bits = row_bits + pair_bits
@@ -303,36 +340,52 @@
         count = count % index_bits
         return (place << count | place >> (index_bits - count)) & (2 * half_tiles - 1)
 
-    def turned(mixed, level, state, source, place):
+    def turned(mixed, level, source, place):
         real, imag = mixed[:, :LANES], mixed[:, LANES:]
         cosine, sine = tables[level, source, :, :LANES], tables[level, source, :, LANES:]
-        state[place, :, :LANES] = real * cosine - imag * sine
-        state[place, :, LANES:] = real * sine + imag * cosine
+        after = 1 - level % 2
+        states[after, place, :, :LANES] = real * cosine - imag * sine
+        states[after, place, :, LANES:] = real * sine + imag * cosine
 
     def run(*accumulators):
         few = min(TILE, row_tiles)
 
         rounds = row_tiles // few
 
-        def strip_of(item, i):
-            return pl.ds(pl.multiple_of((item % rounds * few + i) * TILE, TILE), TILE)
+        def charges_of(row_tile):
+            if slabs:
+                halves = [packed_ref[row_tile, half * TILE : (half + 1) * TILE] for half in range(2)]
+                return jnp.concatenate(halves, axis=1)
+            return packed_ref[pl.ds(pl.multiple_of(row_tile * TILE, TILE), TILE), : 2 * LANES]
+
+        def speeds_of(row_tile):
+            if slabs:
+                raw = packed_ref[row_tile, 2 * TILE :].astype(F32)
+                group = 2 * pairs
+                own = lanes // group == row_index(lanes.shape)
+                return [
+                    repeated(jnp.where(own, raw[half : half + 1], 0.0), group) for half in range(2)
+                ]
+            speeds = packed_ref[row_tile * TILE : (row_tile + 1) * TILE, 2 * LANES :].astype(F32)
+            return [speeds[: TILE // 2], speeds[TILE // 2 :]]
+
+        for i in range(0, row_tiles, 2):
+            both = [speeds_of(i), speeds_of(i + 1)]
+            speeds_ref[i // 2] = jnp.concatenate(
+                [jnp.concatenate([both[0][half], both[1][half]], axis=0) for half in range(2)],
+                axis=1,
+            ).astype(B16)
 
         def push_nodes(item):
             for order in range(2):
-                pltpu.matmul_push_rhs(node_maps[item // rounds], 0, order)
+                both = [node_maps[item // rounds * 2 + side] for side in range(2)]
+                pltpu.matmul_push_rhs(jnp.concatenate(both, axis=1), 0, order)
 
         def send_speeds(item, i):
-            speeds = [packed_ref[strip_of(item, i + side), 2 * LANES :] for side in range(2)]
-            speeds = [part.astype(F32) for part in speeds]
-            speeds = jnp.concatenate(
-                [
-                    jnp.concatenate([part[: TILE // 2] for part in speeds], axis=0),
-                    jnp.concatenate([part[TILE // 2 :] for part in speeds], axis=0),
-                ],
-                axis=1,
-            ).astype(B16)
             pltpu.matmul_acc_lhs(
-                accumulators[2 * few + i // 2], speeds, load_staged_rhs=0 if i < 4 else None
+                accumulators[2 * few + i // 2],
+                speeds_ref[(item % rounds * few + i) // 2],
+                load_staged_rhs=0 if i < 4 else None,
             )
 
         items = pairs // 2 * rounds
@@ -347,12 +400,12 @@
             coming = jnp.minimum(item + 1, items - 1)
             for order in range(2):
                 pltpu.matmul_push_rhs(leaf_maps[2 * duo + order], 1, order)
-            strips = [strip_of(item, i) for i in range(few)]
-            for i, strip in enumerate(strips):
+            for i in range(few):
+                charges = charges_of(start + i)
                 for order in range(2):
                     pltpu.matmul_acc_lhs(
                         accumulators[2 * i + order],
-                        packed_ref[strip, : 2 * LANES],
+                        charges,
                         load_staged_rhs=1 if i == 0 else None,
                     )
             push_nodes(coming)
@@ -363,7 +416,7 @@
                     sine, cosine = sine_cosine(turns[:, order * LANES : (order + 1) * LANES])
                     for side in range(2):
                         place = base + place_of(i + side, order)
-                        state_a[place] = pltpu.matmul_pop(
+                        states_ref[0, place] = pltpu.matmul_pop(
                             accumulators[2 * (i + side) + order]
                         ).astype(B16)
                         here = slice(side * TILE // 2, (side + 1) * TILE // 2)
@@ -386,9 +439,10 @@
             for order in range(2):
                 pltpu.matmul_push_rhs(weights[2 * level + order], 0, order)
 
-        def send(state, block, unit, fresh):
+        def send(level, block, unit, fresh):
             number = block * units + unit
-            first, second = state[number], state[number + half_tiles]
+            first = states[level % 2, number]
+            second = states[level % 2, number + half_tiles]
             for order in range(2):
                 pltpu.matmul_acc_lhs(
                     accumulators[2 * unit + order],
@@ -401,32 +455,40 @@
                 pltpu.matmul_pop(accumulators[2 * unit + order]).astype(B16) for order in range(2)
             ]
 
-        def finish(level, target, block, unit):
+        def finish(level, block, unit):
             one, other = received(unit)
             number = block * units + unit
-            turned(merged(one, other), level, target, number, 2 * number)
-            turned(merged(other, one), level, target, number + half_tiles, 2 * number + 1)
-
-        def across_tiles(level, source, target, next_level):
-            @pl.loop(0, blocks - 1)
-            def _(block):
+            turned(merged(one, other), level, number, 2 * number)
+            turned(merged(other, one), level, number + half_tiles, 2 * number + 1)
+
+        def across_tiles(first_level, count):
+            load_maps(first_level)
+            for unit in range(units):
+                send(first_level, 0, unit, True)
+
+            @pl.loop(first_level, first_level + count)
+            def _(level):
+                @pl.loop(0, blocks - 1)
+                def _(block):
+                    for unit in range(units):
+                        finish(level, block, unit)
+                        send(level, block + 1, unit, False)
+
+                next_level = jnp.minimum(level + 1, levels - 1)
+                load_maps(next_level)
                 for unit in range(units):
-                    finish(level, target, block, unit)
-                    send(source, block + 1, unit, False)
-
-            if next_level is not None:
-                load_maps(next_level)
+                    finish(level, blocks - 1, unit)
+                    send(next_level, 0, unit, True)
+
             for unit in range(units):
-                finish(level, target, blocks - 1, unit)
-                if next_level is not None:
-                    send(target, 0, unit, True)
-
-        def within_tiles(level, source, target, stride):
+                received(unit)
+
+        def within_tiles(level, stride):
             upper = row_index((TILE, 2 * LANES)) // stride % 2 == 1
             mask = (lane_index((TILE, 2 * LANES)) % LANES < HALF) != upper
 
             def one_tile(place, fresh):
-                own = source[place].astype(F32)
+                own = states_ref[level % 2, place].astype(F32)
                 other = jnp.where(
                     upper, pltpu.roll(own, stride, 0), pltpu.roll(own, TILE - stride, 0)
                 )
@@ -437,7 +499,7 @@
                         accumulators[order], lhs.astype(B16), load_staged_rhs=0 if fresh else None
                     )
                     pre.append(pltpu.matmul_pop(accumulators[order]))
-                turned(jnp.where(mask, *pre).astype(B16), level, target, place, place)
+                turned(jnp.where(mask, *pre).astype(B16), level, place, place)
 
             one_tile(0, True)
 
@@ -446,42 +508,36 @@
                 one_tile(place, False)
 
         fetches[0].wait()
-        if levels % 2 == 0 and blocks > 3 and all(kind == "tiles" for kind, _ in plan):
-            load_maps(0)
-            for unit in range(units):
-                send(state_a, 0, unit, True)
-
-            @pl.loop(0, levels // 2)
-            def _(two):
-                across_tiles(2 * two, state_a, state_b, 2 * two + 1)
-                across_tiles(2 * two + 1, state_b, state_a, jnp.minimum(2 * two + 2, levels - 1))
-
-            for unit in range(units):
-                received(unit)
-        else:
-            for level, (kind, stride) in enumerate(plan):
-                source, target = states[level % 2], states[1 - level % 2]
+        level = 0
+        while level < levels:
+            kind, stride = plan[level]
+            if kind == "rows":
                 load_maps(level)
-                if kind == "rows":
-                    within_tiles(level, source, target, stride)
-                    continue
-                for unit in range(units):
-                    send(source, 0, unit, True)
-                across_tiles(level, source, target, None)
+                within_tiles(level, stride)
+                level += 1
+                continue
+            count = 1
+            while blocks > 3 and level + count < levels and plan[level + count][0] == kind:
+                count += 1
+            across_tiles(level, count)
+            level += count
 
         fetches[1].wait()
-        final = states[levels % 2]
+        final = states_ref.at[levels % 2]
         share = row_tiles // 2
-        for pair in range(pairs):
+        @pl.loop(0, pairs)
+        def _(pair):
+            base = place_of(0, pair)
             for order in range(2):
-                pltpu.matmul_push_rhs(weights[2 * levels + pair], pair % 2, order)
+                pltpu.matmul_push_rhs(weights[2 * levels + pair], 0, order)
             for i in range(share):
                 for order in range(2):
                     pltpu.matmul_acc_lhs(
                         accumulators[2 * i + order],
-                        final[place_of(order * share + i, pair)],
-                        load_staged_rhs=pair % 2 if i == 0 else None,
+                        final[base + place_of(order * share + i, 0)],
+                        load_staged_rhs=0 if i == 0 else None,
                     )
+
         for i in range(share):
             for order in range(2):
                 top = (order * share + i) * TILE
@@ -532,16 +588,20 @@
 
     charge_rows = charges.reshape(2, rows, LANES).transpose(1, 0, 2).reshape(2 * rows, LANES)
     in_hbm = pl.BlockSpec(memory_space=pltpu.HBM)
+    if rows_per == TILE:
+        packed_shape = (devices, 2 * TILE + 8, LANES)
+    else:
+        packed_shape = (rows, 3 * LANES)
     packed = pl.pallas_call(
         functools.partial(pack_kernel, leaf),
         in_specs=[in_hbm] * 3,
         out_specs=in_hbm,
-        out_shape=jax.ShapeDtypeStruct((rows, 3 * LANES), B16),
+        out_shape=jax.ShapeDtypeStruct(packed_shape, B16),
         scratch_shapes=[
             pltpu.VMEM((2 * rows, LANES), F32),
             pltpu.VMEM((rows, LANES), jnp.int32),
             pltpu.VMEM((boxes // LANES, LANES), B16),
-            pltpu.VMEM((rows, 3 * LANES), B16),
+            pltpu.VMEM(packed_shape, B16),
             pltpu.SemaphoreType.DMA((STRIPS, 3)),
             pltpu.SemaphoreType.DMA((STRIPS,)),
         ],
@@ -550,8 +610,8 @@
     )(charge_rows, source_order.reshape(rows, LANES), velocity.reshape(boxes // LANES, LANES))
 
     packed = lax.all_to_all(
-        packed.reshape(devices, rows_per, 3 * LANES), AXES, 0, 0, tiled=True
-    ).reshape(rows, 3 * LANES)
+        packed.reshape(devices, -1, packed_shape[-1]), AXES, 0, 0, tiled=True
+    ).reshape(packed_shape)
 
     square = (2 * LANES, 2 * LANES)
     count = 2 * levels + pairs
@@ -563,10 +623,9 @@
         compiler_params=vmem(56),
         cost_estimate=pl.CostEstimate(flops=10**9, bytes_accessed=10**7, transcendentals=0),
         name="maps",
-    )(mixing, eval_weight)
+    )(mixing, eval_weight.T)
 
     tiles = rows // TILE * pairs
-    state = pltpu.VMEM((tiles, TILE, 2 * LANES), B16)
     values = pl.pallas_call(
         functools.partial(butterfly_kernel, level_plan(levels, local_levels, rows_per), leaf, pairs),
         out_shape=jax.ShapeDtypeStruct((rows, 2 * LANES), B16),
@@ -574,12 +633,12 @@
         + [in_hbm],
         scratch_shapes=[
             pltpu.VMEM((pairs, *square), B16),
-            pltpu.VMEM((pairs // 2, *square), B16),
+            pltpu.VMEM((pairs, 2 * LANES, LANES), B16),
             pltpu.VMEM((count, *square), B16),
             pltpu.SemaphoreType.DMA((2,)),
-            state,
-            state,
+            pltpu.VMEM((2, tiles, TILE, 2 * LANES), B16),
             pltpu.VMEM((levels, tiles, TILE, 2 * LANES), B16),
+            pltpu.VMEM((rows // TILE // 2, TILE, 2 * LANES), B16),
         ],
         compiler_params=vmem(40),
         name="butterfly",

time: 50.8 us -> 49.3 us (0.970)
  local copies, waits for them, and re-layouts: 1.41 us -> 0.01 us
    unnamed x7 -> x6, local copies, waits for them, and re-layouts: 1.41 us -> 0.01 us
    pallas_call x1, Pallas kernels: 3.03 us -> 2.5 us  [on_device(): pl.pallas_call(functools.partial(pack_kernel, leaf), in_specs=[in_hbm] *...]
  transfers between devices with their start and end apart: 1 -> 1, of which waited for: 1 -> 1; matrix products, arithmetic and copies ran while one was open for 3% -> 0% of each run, Pallas kernels for 13% -> 14%
where the time goes in v7:
time: 49.3 us; the launch traced here: 49 us
  Pallas kernels  23.7 us (48%)
  blocking collectives  12.8 us (26%)
  starting transfers between devices  7.3 us (15%)
  waiting for transfers between devices  5.11 us (10%)
    pallas_call x1, Pallas kernels, on_device(): pl.pallas_call(functools.partial(butterfly_kernel, level_plan(levels, loc...  13.4 us
    all_to_all x1, blocking collectives, on_device(): lax.all_to_all(values.reshape(devices, rows_per, 2 * LANES), AXES, 0, 0,...  12.8 us
    all_to_all x1, starting transfers between devices, on_device(): lax.all_to_all(packed.reshape(devices, -1, packed_shape[-1]), AXES, 0, 0,...  7.3 us
    pallas_call x1, Pallas kernels, on_device(): pl.pallas_call(functools.partial(maps_kernel, leaf), grid=(1,), out_specs...  6.87 us
    all_to_all x1, waiting for transfers between devices, on_device(): lax.all_to_all(packed.reshape(devices, -1, packed_shape[-1]), AXES, 0, 0,...  5.11 us
    pallas_call x1, Pallas kernels, on_device(): pl.pallas_call(functools.partial(pack_kernel, leaf), in_specs=[in_hbm] *...  2.5 us
  transfers between devices with their start and end apart: 1, of which 1 were waited for; matrix products, arithmetic and copies ran while one was open for 0% of the time, Pallas kernels for 14%

profile of v7, /device:TPU:0, one launch (start us, length us, event | category | flops | bytes accessed | tf_op | source)
XLA Modules:
  0.0 49.0 jit_solution(13330022641884644534)
XLA Ops:
  0.0 0.0 copy-start.2
  0.0 0.0 copy-start.1
  0.0 2.5 %pack.1 = bf16[32,40,128]{2,1,0:T(8,128)(2,1)} custom-call(f32[1024,128]{1,0:T(8,128)} %bitcast.19, s32[512,128]{1,0:T(8,128)} %bitcast.20, bf16[64,128]{1,0:T(8,128)(2,1)} %bitcast.21), custom_call_target="tpu_custom_call" | custom-call | tf_op jit(solution)/shard_map/pack/pallas_call | solution.py:595
  2.5 7.3 %all-to-all-start = ((bf16[32,40,128]{2,1,0:T(8,128)(2,1)}), bf16[32,40,128]{2,1,0:T(8,128)(2,1)S(1)}, u32[]{:S(2)}, u32[]{:S(2)}) async-start(bf16[32,40,128]{2,1,0:T(8,128)(2,1)} %pack.1), calls=%async_computation | async-start | bytes 655360 | tf_op jit(solution)/shard_map/all_to_all | solution.py:612
  9.8 0.0 copy-start
  9.8 6.9 %maps.1.weights_ref = bf16[200,256,256]{2,1,0:T(8,128)(2,1)} custom-call(bf16[8,2,2,128,128]{4,3,2,1,0:T(8,128)(2,1)} %mixing_ref.1, bf16[16,128]{1,0:T(8,128)(2,1)} %bitcast.22), custom_call_target="tpu_custom_call" | custom-call | flops 1000000000 | bytes 10000000 | tf_op jit(solution)/shard_map/maps/pallas_call | solution.py:618
  16.7 5.1 %all-to-all-done.packed_ref = bf16[32,40,128]{2,1,0:T(8,128)(2,1)S(1)} async-done(((bf16[32,40,128]{2,1,0:T(8,128)(2,1)}), bf16[32,40,128]{2,1,0:T(8,128)(2,1)S(1)}, u32[]{:S(2)}, u32[]{:S(2)}) %all-to-all-start) | async-done | bytes 327712 | tf_op jit(solution)/shard_map/all_to_all | solution.py:612
  21.8 0.0 copy-done.2
  21.8 0.0 copy-done.1
  21.8 13.4 %butterfly.1 = bf16[512,256]{1,0:T(8,128)(2,1)S(1)} custom-call(bf16[32,40,128]{2,1,0:T(8,128)(2,1)S(1)} %all-to-all-done.packed_ref, bf16[16,128]{1,0:T(8,128)(2,1)S(1)} %copy-done.1, f32[3,128]{1,0:T(4,128)S(1)} %copy-done.2, bf16[200,256,256]{2,1,0:T(8,128)(2,1)} %maps.1.weights_ref), custom_call_target="tpu_custom_call" | custom-call | tf_op jit(solution)/shard_map/butterfly/pallas_call | solution.py:629
  35.2 12.8 %all_to_all.10 = bf16[32,16,256]{2,1,0:T(8,128)(2,1)S(1)} all-to-all(bf16[32,16,256]{2,1,0:T(8,128)(2,1)S(1)} %bitcast.16), channel_id=1, replica_groups=mesh['wide'=8,'narrow'=4] {'wide','narrow'}, dimensions={0} | all-to-all | bytes 524288 | tf_op jit(solution)/shard_map/all_to_all | solution.py:647
  48.0 0.0 copy-done
  48.0 1.0 %unpack.1 = f32[1024,128]{1,0:T(8,128)} custom-call(bf16[512,256]{1,0:T(8,128)(2,1)S(1)} %bitcast.17, s32[512,128]{1,0:T(8,128)S(1)} %bitcast.18), custom_call_target="tpu_custom_call" | custom-call | tf_op jit(solution)/shard_map/unpack/pallas_call | solution.py:651
Async XLA Ops:
  0.0 21.8 %copy-start.2 = (f32[3,128]{1,0:T(4,128)S(1)}, f32[3,128]{1,0:T(4,128)}, u32[]{:S(2)}) copy-start(f32[3,128]{1,0:T(4,128)} %constant.2.clone.nodes_ref) | copy-start | bytes 4612
  0.0 21.8 %copy-start.1 = (bf16[16,128]{1,0:T(8,128)(2,1)S(1)}, bf16[16,128]{1,0:T(8,128)(2,1)}, u32[]{:S(2)}) copy-start(bf16[16,128]{1,0:T(8,128)(2,1)} %leaf_ref.1) | copy-start | bytes 12292
  2.5 19.3 %all-to-all-start = ((bf16[32,40,128]{2,1,0:T(8,128)(2,1)}), bf16[32,40,128]{2,1,0:T(8,128)(2,1)S(1)}, u32[]{:S(2)}, u32[]{:S(2)}) async-start(bf16[32,40,128]{2,1,0:T(8,128)(2,1)} %pack.1), calls=%async_computation | async-start | bytes 655360 | tf_op jit(solution)/shard_map/all_to_all | solution.py:612
  9.8 38.2 %copy-start = (s32[65536]{0:T(1024)S(1)}, s32[65536]{0:T(1024)}, u32[]{:S(2)}) copy-start(s32[65536]{0:T(1024)} %param.14) | copy-start | bytes 786436

commit v8 on v7

--- a/solution.py
+++ b/solution.py
@@ -348,7 +348,7 @@
         states[after, place, :, LANES:] = real * sine + imag * cosine
 
     def run(*accumulators):
-        few = min(TILE, row_tiles)
+        few = min(2 * TILE, row_tiles)
 
         rounds = row_tiles // few
 
@@ -546,7 +546,7 @@
                 ).astype(B16)
 
     pl.run_scoped(
-        run, *[pltpu.ACC(order)((TILE, 2 * LANES), F32) for _ in range(units) for order in range(2)]
+        run, *[pltpu.ACC(order)((TILE, 2 * LANES), F32) for _ in range(2 * units) for order in range(2)]
     )
 
 

time: 49.3 us -> 48.5 us (0.984)
  Pallas kernels: 23.7 us -> 22.9 us
    pallas_call x1, Pallas kernels: 13.4 us -> 12.6 us  [on_device(): pl.pallas_call(functools.partial(butterfly_kernel, level_plan(levels, loc...]
where the time goes in v8:
time: 48.5 us; the launch traced here: 48.2 us
  Pallas kernels  22.9 us (47%)
  blocking collectives  12.8 us (26%)
  starting transfers between devices  7.3 us (15%)
  waiting for transfers between devices  5.11 us (11%)
    all_to_all x1, blocking collectives, on_device(): lax.all_to_all(values.reshape(devices, rows_per, 2 * LANES), AXES, 0, 0,...  12.8 us
    pallas_call x1, Pallas kernels, on_device(): pl.pallas_call(functools.partial(butterfly_kernel, level_plan(levels, loc...  12.6 us
    all_to_all x1, starting transfers between devices, on_device(): lax.all_to_all(packed.reshape(devices, -1, packed_shape[-1]), AXES, 0, 0,...  7.3 us
    pallas_call x1, Pallas kernels, on_device(): pl.pallas_call(functools.partial(maps_kernel, leaf), grid=(1,), out_specs...  6.87 us
    all_to_all x1, waiting for transfers between devices, on_device(): lax.all_to_all(packed.reshape(devices, -1, packed_shape[-1]), AXES, 0, 0,...  5.11 us
    pallas_call x1, Pallas kernels, on_device(): pl.pallas_call(functools.partial(pack_kernel, leaf), in_specs=[in_hbm] *...  2.5 us
  transfers between devices with their start and end apart: 1, of which 1 were waited for; matrix products, arithmetic and copies ran while one was open for 0% of the time, Pallas kernels for 14%

profile of v8, /device:TPU:0, one launch (start us, length us, event | category | flops | bytes accessed | tf_op | source)
XLA Modules:
  0.0 48.2 jit_solution(329146733697724992)
XLA Ops:
  0.0 0.0 copy-start.2
  0.0 0.0 copy-start.1
  0.0 2.5 %pack.1 = bf16[32,40,128]{2,1,0:T(8,128)(2,1)} custom-call(f32[1024,128]{1,0:T(8,128)} %bitcast.19, s32[512,128]{1,0:T(8,128)} %bitcast.20, bf16[64,128]{1,0:T(8,128)(2,1)} %bitcast.21), custom_call_target="tpu_custom_call" | custom-call | tf_op jit(solution)/shard_map/pack/pallas_call | solution.py:595
  2.5 7.3 %all-to-all-start = ((bf16[32,40,128]{2,1,0:T(8,128)(2,1)}), bf16[32,40,128]{2,1,0:T(8,128)(2,1)S(1)}, u32[]{:S(2)}, u32[]{:S(2)}) async-start(bf16[32,40,128]{2,1,0:T(8,128)(2,1)} %pack.1), calls=%async_computation | async-start | bytes 655360 | tf_op jit(solution)/shard_map/all_to_all | solution.py:612
  9.8 0.0 copy-start
  9.8 6.9 %maps.1.weights_ref = bf16[200,256,256]{2,1,0:T(8,128)(2,1)} custom-call(bf16[8,2,2,128,128]{4,3,2,1,0:T(8,128)(2,1)} %mixing_ref.1, bf16[16,128]{1,0:T(8,128)(2,1)} %bitcast.22), custom_call_target="tpu_custom_call" | custom-call | flops 1000000000 | bytes 10000000 | tf_op jit(solution)/shard_map/maps/pallas_call | solution.py:618
  16.7 5.1 %all-to-all-done.packed_ref = bf16[32,40,128]{2,1,0:T(8,128)(2,1)S(1)} async-done(((bf16[32,40,128]{2,1,0:T(8,128)(2,1)}), bf16[32,40,128]{2,1,0:T(8,128)(2,1)S(1)}, u32[]{:S(2)}, u32[]{:S(2)}) %all-to-all-start) | async-done | bytes 327712 | tf_op jit(solution)/shard_map/all_to_all | solution.py:612
  21.8 0.0 copy-done.2
  21.8 0.0 copy-done.1
  21.8 12.6 %butterfly.1 = bf16[512,256]{1,0:T(8,128)(2,1)S(1)} custom-call(bf16[32,40,128]{2,1,0:T(8,128)(2,1)S(1)} %all-to-all-done.packed_ref, bf16[16,128]{1,0:T(8,128)(2,1)S(1)} %copy-done.1, f32[3,128]{1,0:T(4,128)S(1)} %copy-done.2, bf16[200,256,256]{2,1,0:T(8,128)(2,1)} %maps.1.weights_ref), custom_call_target="tpu_custom_call" | custom-call | tf_op jit(solution)/shard_map/butterfly/pallas_call | solution.py:629
  34.4 12.8 %all_to_all.10 = bf16[32,16,256]{2,1,0:T(8,128)(2,1)S(1)} all-to-all(bf16[32,16,256]{2,1,0:T(8,128)(2,1)S(1)} %bitcast.16), channel_id=1, replica_groups=mesh['wide'=8,'narrow'=4] {'wide','narrow'}, dimensions={0} | all-to-all | bytes 524288 | tf_op jit(solution)/shard_map/all_to_all | solution.py:647
  47.2 0.0 copy-done
  47.2 1.0 %unpack.1 = f32[1024,128]{1,0:T(8,128)} custom-call(bf16[512,256]{1,0:T(8,128)(2,1)S(1)} %bitcast.17, s32[512,128]{1,0:T(8,128)S(1)} %bitcast.18), custom_call_target="tpu_custom_call" | custom-call | tf_op jit(solution)/shard_map/unpack/pallas_call | solution.py:651
Async XLA Ops:
  0.0 21.8 %copy-start.2 = (f32[3,128]{1,0:T(4,128)S(1)}, f32[3,128]{1,0:T(4,128)}, u32[]{:S(2)}) copy-start(f32[3,128]{1,0:T(4,128)} %constant.2.clone.nodes_ref) | copy-start | bytes 4612
  0.0 21.8 %copy-start.1 = (bf16[16,128]{1,0:T(8,128)(2,1)S(1)}, bf16[16,128]{1,0:T(8,128)(2,1)}, u32[]{:S(2)}) copy-start(bf16[16,128]{1,0:T(8,128)(2,1)} %leaf_ref.1) | copy-start | bytes 12292
  2.5 19.3 %all-to-all-start = ((bf16[32,40,128]{2,1,0:T(8,128)(2,1)}), bf16[32,40,128]{2,1,0:T(8,128)(2,1)S(1)}, u32[]{:S(2)}, u32[]{:S(2)}) async-start(bf16[32,40,128]{2,1,0:T(8,128)(2,1)} %pack.1), calls=%async_computation | async-start | bytes 655360 | tf_op jit(solution)/shard_map/all_to_all | solution.py:612
  9.8 37.4 %copy-start = (s32[65536]{0:T(1024)S(1)}, s32[65536]{0:T(1024)}, u32[]{:S(2)}) copy-start(s32[65536]{0:T(1024)} %param.14) | copy-start | bytes 786436

commit v9 on v8

--- a/solution.py
+++ b/solution.py
@@ -21,7 +21,7 @@
     return pltpu.CompilerParams(vmem_limit_bytes=mebibytes * 2**20)
 
 
-STRIPS = 4
+STRIPS = 2
 
 
 def lane_index(shape):

time: 48.5 us -> 48.2 us (level)
  no operation moved by 1% of the time
where the time goes in v9:
time: 48.2 us; the launch traced here: 48 us
  Pallas kernels  22.7 us (47%)
  blocking collectives  12.8 us (27%)
  starting transfers between devices  7.3 us (15%)
  waiting for transfers between devices  5.11 us (11%)
    all_to_all x1, blocking collectives, on_device(): lax.all_to_all(values.reshape(devices, rows_per, 2 * LANES), AXES, 0, 0,...  12.8 us
    pallas_call x1, Pallas kernels, on_device(): pl.pallas_call(functools.partial(butterfly_kernel, level_plan(levels, loc...  12.6 us
    all_to_all x1, starting transfers between devices, on_device(): lax.all_to_all(packed.reshape(devices, -1, packed_shape[-1]), AXES, 0, 0,...  7.3 us
    pallas_call x1, Pallas kernels, on_device(): pl.pallas_call(functools.partial(maps_kernel, leaf), grid=(1,), out_specs...  6.87 us
    all_to_all x1, waiting for transfers between devices, on_device(): lax.all_to_all(packed.reshape(devices, -1, packed_shape[-1]), AXES, 0, 0,...  5.11 us
    pallas_call x1, Pallas kernels, on_device(): pl.pallas_call(functools.partial(pack_kernel, leaf), in_specs=[in_hbm] *...  2.25 us
    pallas_call x1, Pallas kernels, on_device(): pl.pallas_call(functools.partial(unpack_kernel, leaf), out_specs=in_hbm,...  0.98 us
  transfers between devices with their start and end apart: 1, of which 1 were waited for; matrix products, arithmetic and copies ran while one was open for 0% of the time, Pallas kernels for 14%

profile of v9, /device:TPU:0, one launch (start us, length us, event | category | flops | bytes accessed | tf_op | source)
XLA Modules:
  0.0 48.0 jit_solution(7213081513777236043)
XLA Ops:
  0.0 0.0 copy-start.2
  0.0 0.0 copy-start.1
  0.0 2.2 %pack.1 = bf16[32,40,128]{2,1,0:T(8,128)(2,1)} custom-call(f32[1024,128]{1,0:T(8,128)} %bitcast.19, s32[512,128]{1,0:T(8,128)} %bitcast.20, bf16[64,128]{1,0:T(8,128)(2,1)} %bitcast.21), custom_call_target="tpu_custom_call" | custom-call | tf_op jit(solution)/shard_map/pack/pallas_call | solution.py:595
  2.3 7.3 %all-to-all-start = ((bf16[32,40,128]{2,1,0:T(8,128)(2,1)}), bf16[32,40,128]{2,1,0:T(8,128)(2,1)S(1)}, u32[]{:S(2)}, u32[]{:S(2)}) async-start(bf16[32,40,128]{2,1,0:T(8,128)(2,1)} %pack.1), calls=%async_computation | async-start | bytes 655360 | tf_op jit(solution)/shard_map/all_to_all | solution.py:612
  9.6 0.0 copy-start
  9.6 6.9 %maps.1.weights_ref = bf16[200,256,256]{2,1,0:T(8,128)(2,1)} custom-call(bf16[8,2,2,128,128]{4,3,2,1,0:T(8,128)(2,1)} %mixing_ref.1, bf16[16,128]{1,0:T(8,128)(2,1)} %bitcast.22), custom_call_target="tpu_custom_call" | custom-call | flops 1000000000 | bytes 10000000 | tf_op jit(solution)/shard_map/maps/pallas_call | solution.py:618
  16.5 5.1 %all-to-all-done.packed_ref = bf16[32,40,128]{2,1,0:T(8,128)(2,1)S(1)} async-done(((bf16[32,40,128]{2,1,0:T(8,128)(2,1)}), bf16[32,40,128]{2,1,0:T(8,128)(2,1)S(1)}, u32[]{:S(2)}, u32[]{:S(2)}) %all-to-all-start) | async-done | bytes 327712 | tf_op jit(solution)/shard_map/all_to_all | solution.py:612
  21.6 0.0 copy-done.2
  21.6 0.0 copy-done.1
  21.6 12.6 %butterfly.1 = bf16[512,256]{1,0:T(8,128)(2,1)S(1)} custom-call(bf16[32,40,128]{2,1,0:T(8,128)(2,1)S(1)} %all-to-all-done.packed_ref, bf16[16,128]{1,0:T(8,128)(2,1)S(1)} %copy-done.1, f32[3,128]{1,0:T(4,128)S(1)} %copy-done.2, bf16[200,256,256]{2,1,0:T(8,128)(2,1)} %maps.1.weights_ref), custom_call_target="tpu_custom_call" | custom-call | tf_op jit(solution)/shard_map/butterfly/pallas_call | solution.py:629
  34.2 12.8 %all_to_all.10 = bf16[32,16,256]{2,1,0:T(8,128)(2,1)S(1)} all-to-all(bf16[32,16,256]{2,1,0:T(8,128)(2,1)S(1)} %bitcast.16), channel_id=1, replica_groups=mesh['wide'=8,'narrow'=4] {'wide','narrow'}, dimensions={0} | all-to-all | bytes 524288 | tf_op jit(solution)/shard_map/all_to_all | solution.py:647
  47.0 0.0 copy-done
  47.0 1.0 %unpack.1 = f32[1024,128]{1,0:T(8,128)} custom-call(bf16[512,256]{1,0:T(8,128)(2,1)S(1)} %bitcast.17, s32[512,128]{1,0:T(8,128)S(1)} %bitcast.18), custom_call_target="tpu_custom_call" | custom-call | tf_op jit(solution)/shard_map/unpack/pallas_call | solution.py:651
Async XLA Ops:
  0.0 21.6 %copy-start.2 = (f32[3,128]{1,0:T(4,128)S(1)}, f32[3,128]{1,0:T(4,128)}, u32[]{:S(2)}) copy-start(f32[3,128]{1,0:T(4,128)} %constant.2.clone.nodes_ref) | copy-start | bytes 4612
  0.0 21.6 %copy-start.1 = (bf16[16,128]{1,0:T(8,128)(2,1)S(1)}, bf16[16,128]{1,0:T(8,128)(2,1)}, u32[]{:S(2)}) copy-start(bf16[16,128]{1,0:T(8,128)(2,1)} %leaf_ref.1) | copy-start | bytes 12292
  2.3 19.3 %all-to-all-start = ((bf16[32,40,128]{2,1,0:T(8,128)(2,1)}), bf16[32,40,128]{2,1,0:T(8,128)(2,1)S(1)}, u32[]{:S(2)}, u32[]{:S(2)}) async-start(bf16[32,40,128]{2,1,0:T(8,128)(2,1)} %pack.1), calls=%async_computation | async-start | bytes 655360 | tf_op jit(solution)/shard_map/all_to_all | solution.py:612
  9.6 37.4 %copy-start = (s32[65536]{0:T(1024)S(1)}, s32[65536]{0:T(1024)}, u32[]{:S(2)}) copy-start(s32[65536]{0:T(1024)} %param.14) | copy-start | bytes 786436

commit v10 on v9

--- a/solution.py
+++ b/solution.py
@@ -264,11 +264,17 @@
             ).astype(B16)
 
 
+def fitted(function, degree):
+    domain = [0.0, 0.25]
+    series = np.polynomial.Chebyshev.interpolate(function, degree, domain=domain)
+    return [float(term) for term in series.convert(kind=np.polynomial.Polynomial).coef]
+
+
 def sine_cosine(turns):
     u = turns - jnp.round(turns)
     w = u * u
-    sin_terms = [(-1) ** i * math.pi ** (2 * i + 1) / math.factorial(2 * i + 1) for i in range(6)]
-    cos_terms = [(-1) ** i * math.pi ** (2 * i) / math.factorial(2 * i) for i in range(6)]
+    sin_terms = fitted(lambda x: math.pi * np.sinc(np.sqrt(x)), 4)
+    cos_terms = fitted(lambda x: np.cos(np.pi * np.sqrt(x)), 4)
     half_sin = jnp.full_like(w, sin_terms[-1])
     for term in sin_terms[-2::-1]:
         half_sin = half_sin * w + term

time: 48.2 us -> 48.1 us (level)
  no operation moved by 1% of the time
where the time goes in v10:
time: 48.1 us; the launch traced here: 47.8 us
  Pallas kernels  22.5 us (47%)
  blocking collectives  12.8 us (27%)
  starting transfers between devices  7.3 us (15%)
  waiting for transfers between devices  5.11 us (11%)
    all_to_all x1, blocking collectives, on_device(): lax.all_to_all(values.reshape(devices, rows_per, 2 * LANES), AXES, 0, 0,...  12.8 us
    pallas_call x1, Pallas kernels, on_device(): pl.pallas_call(functools.partial(butterfly_kernel, level_plan(levels, loc...  12.4 us
    all_to_all x1, starting transfers between devices, on_device(): lax.all_to_all(packed.reshape(devices, -1, packed_shape[-1]), AXES, 0, 0,...  7.3 us
    pallas_call x1, Pallas kernels, on_device(): pl.pallas_call(functools.partial(maps_kernel, leaf), grid=(1,), out_specs...  6.87 us
    all_to_all x1, waiting for transfers between devices, on_device(): lax.all_to_all(packed.reshape(devices, -1, packed_shape[-1]), AXES, 0, 0,...  5.11 us
    pallas_call x1, Pallas kernels, on_device(): pl.pallas_call(functools.partial(pack_kernel, leaf), in_specs=[in_hbm] *...  2.25 us
    pallas_call x1, Pallas kernels, on_device(): pl.pallas_call(functools.partial(unpack_kernel, leaf), out_specs=in_hbm,...  0.98 us
  transfers between devices with their start and end apart: 1, of which 1 were waited for; matrix products, arithmetic and copies ran while one was open for 0% of the time, Pallas kernels for 14%

profile of v10, /device:TPU:0, one launch (start us, length us, event | category | flops | bytes accessed | tf_op | source)
XLA Modules:
  0.0 47.8 jit_solution(14037335587768493809)
XLA Ops:
  0.0 0.0 copy-start.2
  0.0 0.0 copy-start.1
  0.0 2.2 %pack.1 = bf16[32,40,128]{2,1,0:T(8,128)(2,1)} custom-call(f32[1024,128]{1,0:T(8,128)} %bitcast.19, s32[512,128]{1,0:T(8,128)} %bitcast.20, bf16[64,128]{1,0:T(8,128)(2,1)} %bitcast.21), custom_call_target="tpu_custom_call" | custom-call | tf_op jit(solution)/shard_map/pack/pallas_call | solution.py:601
  2.3 7.3 %all-to-all-start = ((bf16[32,40,128]{2,1,0:T(8,128)(2,1)}), bf16[32,40,128]{2,1,0:T(8,128)(2,1)S(1)}, u32[]{:S(2)}, u32[]{:S(2)}) async-start(bf16[32,40,128]{2,1,0:T(8,128)(2,1)} %pack.1), calls=%async_computation | async-start | bytes 655360 | tf_op jit(solution)/shard_map/all_to_all | solution.py:618
  9.6 0.0 copy-start
  9.6 6.9 %maps.1.weights_ref = bf16[200,256,256]{2,1,0:T(8,128)(2,1)} custom-call(bf16[8,2,2,128,128]{4,3,2,1,0:T(8,128)(2,1)} %mixing_ref.1, bf16[16,128]{1,0:T(8,128)(2,1)} %bitcast.22), custom_call_target="tpu_custom_call" | custom-call | flops 1000000000 | bytes 10000000 | tf_op jit(solution)/shard_map/maps/pallas_call | solution.py:624
  16.5 5.1 %all-to-all-done.packed_ref = bf16[32,40,128]{2,1,0:T(8,128)(2,1)S(1)} async-done(((bf16[32,40,128]{2,1,0:T(8,128)(2,1)}), bf16[32,40,128]{2,1,0:T(8,128)(2,1)S(1)}, u32[]{:S(2)}, u32[]{:S(2)}) %all-to-all-start) | async-done | bytes 327712 | tf_op jit(solution)/shard_map/all_to_all | solution.py:618
  21.6 0.0 copy-done.2
  21.6 0.0 copy-done.1
  21.6 12.4 %butterfly.1 = bf16[512,256]{1,0:T(8,128)(2,1)S(1)} custom-call(bf16[32,40,128]{2,1,0:T(8,128)(2,1)S(1)} %all-to-all-done.packed_ref, bf16[16,128]{1,0:T(8,128)(2,1)S(1)} %copy-done.1, f32[3,128]{1,0:T(4,128)S(1)} %copy-done.2, bf16[200,256,256]{2,1,0:T(8,128)(2,1)} %maps.1.weights_ref), custom_call_target="tpu_custom_call" | custom-call | tf_op jit(solution)/shard_map/butterfly/pallas_call | solution.py:635
  34.0 12.8 %all_to_all.10 = bf16[32,16,256]{2,1,0:T(8,128)(2,1)S(1)} all-to-all(bf16[32,16,256]{2,1,0:T(8,128)(2,1)S(1)} %bitcast.16), channel_id=1, replica_groups=mesh['wide'=8,'narrow'=4] {'wide','narrow'}, dimensions={0} | all-to-all | bytes 524288 | tf_op jit(solution)/shard_map/all_to_all | solution.py:653
  46.8 0.0 copy-done
  46.8 1.0 %unpack.1 = f32[1024,128]{1,0:T(8,128)} custom-call(bf16[512,256]{1,0:T(8,128)(2,1)S(1)} %bitcast.17, s32[512,128]{1,0:T(8,128)S(1)} %bitcast.18), custom_call_target="tpu_custom_call" | custom-call | tf_op jit(solution)/shard_map/unpack/pallas_call | solution.py:657
Async XLA Ops:
  0.0 21.6 %copy-start.2 = (f32[3,128]{1,0:T(4,128)S(1)}, f32[3,128]{1,0:T(4,128)}, u32[]{:S(2)}) copy-start(f32[3,128]{1,0:T(4,128)} %constant.2.clone.nodes_ref) | copy-start | bytes 4612
  0.0 21.6 %copy-start.1 = (bf16[16,128]{1,0:T(8,128)(2,1)S(1)}, bf16[16,128]{1,0:T(8,128)(2,1)}, u32[]{:S(2)}) copy-start(bf16[16,128]{1,0:T(8,128)(2,1)} %leaf_ref.1) | copy-start | bytes 12292
  2.3 19.3 %all-to-all-start = ((bf16[32,40,128]{2,1,0:T(8,128)(2,1)}), bf16[32,40,128]{2,1,0:T(8,128)(2,1)S(1)}, u32[]{:S(2)}, u32[]{:S(2)}) async-start(bf16[32,40,128]{2,1,0:T(8,128)(2,1)} %pack.1), calls=%async_computation | async-start | bytes 655360 | tf_op jit(solution)/shard_map/all_to_all | solution.py:618
  9.6 37.3 %copy-start = (s32[65536]{0:T(1024)S(1)}, s32[65536]{0:T(1024)}, u32[]{:S(2)}) copy-start(s32[65536]{0:T(1024)} %param.14) | copy-start | bytes 786436
